TPU v7x, 32 devices: a whole 2x2x4 slice. The times are simulated.
32 devices in a mesh: dp: 4 (over z), index: 8 (over y, x, core).
Axes of the slice: x: 2, y: 2, z: 4, core: 2. Of those that a mesh axis runs over, the one named last changes fastest.
Arguments:
- decoder_input: bfloat16 [8, 1024, 1024], P('dp', 'index'), may hold values from -6 to 6
- encoder_memory: bfloat16 [8, 1920, 1024], P('dp', 'index'), may hold values from -6 to 6
- question_vectors: bfloat16 [8, 768], P('dp', 'index'), may hold values from -12 to 12
- passage_vectors: bfloat16 [32768, 768], P('index'), may hold values from -0.21875 to 0.21875
- passage_ids: int32 [8, 10], P('dp'), may hold values from 0 to 32767
- valid_count: int32 [8], P('dp'), may hold values from 2 to 10, as said below
- output_grad: bfloat16 [8, 1024, 1024], P('dp', 'index'), may hold values from -6 to 6
- attention_weight: float32 [8, 1024, 1024], P(None, ('dp', 'index'))
- expand_weight: float32 [1024, 4096], P(('dp', 'index')), may hold values from -0.1875 to 0.1875
- contract_weight: float32 [4096, 1024], P(('dp', 'index')), may hold values from -0.09375 to 0.09375
- vector_params: float32 [17, 1024], P(None, ('dp', 'index'))
- attention_mean: float32 [8, 1024, 1024], P(None, ('dp', 'index')), may hold values from -16 to 16
- attention_square: float32 [8, 1024, 1024], P(None, ('dp', 'index')), may hold values from 0.36864 to 5.89824
- expand_mean: float32 [1024, 4096], P(('dp', 'index')), may hold values from -32 to 32
- expand_square: float32 [1024, 4096], P(('dp', 'index')), may hold values from 1.024 to 16.384
- contract_mean: float32 [4096, 1024], P(('dp', 'index')), may hold values from -32 to 32
- contract_square: float32 [4096, 1024], P(('dp', 'index')), may hold values from 1.024 to 16.384
- vector_mean: float32 [17, 1024], P(None, ('dp', 'index')), may hold values from -64 to 64
- vector_square: float32 [17, 1024], P(None, ('dp', 'index')), may hold values from 4.096 to 65.536
Outputs:
- layer_output: bfloat16 [8, 1024, 1024], P('dp', 'index')
- input_gradient: float32 [8, 1024, 1024], P('dp', 'index')
- memory_gradient: float32 [8, 1920, 1024], P('dp', 'index')
- question_gradient: float32 [8, 768], P('dp', 'index')
- updated_attention: float32 [8, 1024, 1024], P(None, ('dp', 'index'))
- mean_attention: float32 [8, 1024, 1024], P(None, ('dp', 'index'))
- square_attention: float32 [8, 1024, 1024], P(None, ('dp', 'index'))
- updated_expand: float32 [1024, 4096], P(('dp', 'index'))
- mean_expand: float32 [1024, 4096], P(('dp', 'index'))
- square_expand: float32 [1024, 4096], P(('dp', 'index'))
- updated_contract: float32 [4096, 1024], P(('dp', 'index'))
- mean_contract: float32 [4096, 1024], P(('dp', 'index'))
- square_contract: float32 [4096, 1024], P(('dp', 'index'))
- updated_vector: float32 [17, 1024], P(None, ('dp', 'index'))
- mean_vector: float32 [17, 1024], P(None, ('dp', 'index'))
- square_vector: float32 [17, 1024], P(None, ('dp', 'index'))
Inputs may be any that keep to these rules, and one draw needn't show every extreme that they name: `valid_count`: some question has 10 usable candidates and some has 2.
All inputs are finite; a program needn't handle non-finite values.
Results may differ from a plain program's by a relative error of at most 0.023.
The roundings to bfloat16 on the way count: a program that leaves them out, or rounds other values in their place, can miss the bound.
Values may be sent and summed in bfloat16 or wider, within the bound.
No kernel may reach another device: no remote copies, remote signals or barrier semaphores. Data moves between devices by JAX's collectives and lax.ppermute only.
A program may use at most 384 MiB of HBM per device.

v0:
```python
from functools import partial

import jax
import jax.numpy as jnp
from jax import lax
from jax.sharding import PartitionSpec as P

HEADS = 16
MEM_P = 192
STEP = 10


negative_fill = -1e30
norm_eps = 1e-05
beta_first = 0.9
beta_second = 0.999
adam_eps = 1e-08
decay_matrix = 0.01
rate_attention = 0.1
rate_expand = 0.02
rate_contract = 0.01
rate_vector = 0.2


def layer_norm(hidden, norm_gain, norm_shift):
    center = hidden - jnp.mean(hidden, axis=-1, keepdims=True)
    spread = jnp.mean(center * center, axis=-1, keepdims=True)
    return center * lax.rsqrt(spread + norm_eps) * norm_gain + norm_shift


def split_heads(matrix):
    return matrix.reshape(matrix.shape[0], matrix.shape[1], HEADS, matrix.shape[2] // HEADS)


def merge_heads(matrix):
    return matrix.reshape(matrix.shape[0], matrix.shape[1], matrix.shape[2] * matrix.shape[3])


def project(left_side, weight):
    return jnp.einsum("srd,de->sre", left_side, weight, preferred_element_type=jnp.float32)


def project_back(gradient, weight):
    return jnp.einsum("sre,de->srd", gradient, weight, preferred_element_type=jnp.float32)


def weight_grad(left_side, gradient):
    return jnp.einsum("srd,sre->de", left_side, gradient, preferred_element_type=jnp.float32)


def row_total(values):
    return jnp.sum(values, axis=(0, 1))


def attend_forward(queries, key_rows, values, score_bias, allowed):
    scores = (
        jnp.einsum(
            "sqhd,skhd->shqk",
            split_heads(queries),
            split_heads(key_rows),
            preferred_element_type=jnp.float32,
        )
        * 0.125
        + score_bias
    )
    scores = jnp.where(allowed, scores, negative_fill)
    maximum = jnp.max(scores, axis=-1)
    exponent = jnp.exp(scores - maximum[..., None])
    partition = jnp.sum(exponent, axis=-1)
    attend_prob = exponent / partition[..., None]
    mixture = jnp.einsum(
        "shqk,skhd->sqhd",
        attend_prob.astype(jnp.bfloat16),
        split_heads(values),
        preferred_element_type=jnp.float32,
    )
    return (merge_heads(mixture).astype(jnp.bfloat16), attend_prob, maximum, partition)


def score_grads(grad_mixed, attend_prob, values):
    grad_prob = jnp.einsum(
        "sqhd,skhd->shqk",
        split_heads(grad_mixed),
        split_heads(values),
        preferred_element_type=jnp.float32,
    )
    row_inner = jnp.sum(attend_prob * grad_prob, axis=-1)
    return ((attend_prob * (grad_prob - row_inner[..., None])).astype(jnp.bfloat16), row_inner)


def to_queries(grad_score, key_rows):
    return (
        merge_heads(
            jnp.einsum(
                "shqk,skhd->sqhd",
                grad_score,
                split_heads(key_rows),
                preferred_element_type=jnp.float32,
            )
        )
        * 0.125
    )


def to_keys(grad_score, attend_prob, queries, grad_mixed):
    grad_key = (
        merge_heads(
            jnp.einsum(
                "shqk,sqhd->skhd",
                grad_score,
                split_heads(queries),
                preferred_element_type=jnp.float32,
            )
        )
        * 0.125
    )
    grad_value = merge_heads(
        jnp.einsum(
            "shqk,sqhd->skhd",
            attend_prob.astype(jnp.bfloat16),
            split_heads(grad_mixed),
            preferred_element_type=jnp.float32,
        )
    )
    return (grad_key, grad_value)


def adam_update(weight, moment_one, moment_two, gradient, step_rate, weight_decay):
    mean_new = beta_first * moment_one + (1.0 - beta_first) * gradient
    square_new = beta_second * moment_two + (1.0 - beta_second) * gradient * gradient
    mean_hat = mean_new / (1.0 - beta_first**STEP)
    square_hat = square_new / (1.0 - beta_second**STEP)
    updated = weight - step_rate * (
        mean_hat / (jnp.sqrt(square_hat) + adam_eps) + weight_decay * weight
    )
    return (updated, mean_new, square_new)


def body(
    decoder_input,
    encoder_memory,
    question_vectors,
    passage_vectors,
    passage_ids,
    valid_count,
    output_grad,
    attention_weight,
    expand_weight,
    contract_weight,
    vector_params,
    attention_mean,
    attention_square,
    expand_mean,
    expand_square,
    contract_mean,
    contract_square,
    vector_mean,
    vector_square,
):
    attention_low, expand_low, contract_low, vector_low = (
        lax.all_gather(attention_weight.astype(jnp.bfloat16), ("dp", "index"), axis=1, tiled=True),
        lax.all_gather(expand_weight.astype(jnp.bfloat16), ("dp", "index"), axis=0, tiled=True),
        lax.all_gather(contract_weight.astype(jnp.bfloat16), ("dp", "index"), axis=0, tiled=True),
        lax.all_gather(vector_params.astype(jnp.bfloat16), ("dp", "index"), axis=1, tiled=True),
    )
    vectors = vector_low.astype(jnp.float32)
    seqs_here, rows_here, model_width = decoder_input.shape
    shard_index = lax.axis_index("index")
    length = rows_here * lax.axis_size("index")
    ffn_width = expand_low.shape[1]
    self_query = (project(decoder_input, attention_low[0]) + vectors[0]).astype(jnp.bfloat16)
    self_key = project(decoder_input, attention_low[1]).astype(jnp.bfloat16)
    self_value = (project(decoder_input, attention_low[2]) + vectors[1]).astype(jnp.bfloat16)
    key_all, value_all = (
        lax.all_gather(self_key, "index", axis=1, tiled=True),
        lax.all_gather(self_value, "index", axis=1, tiled=True),
    )
    query_place = shard_index * rows_here + jnp.arange(rows_here)
    causal = (jnp.arange(length)[None, :] <= query_place[:, None])[None, None]
    self_mixed, self_prob, self_peak, self_total = attend_forward(
        self_query, key_all, value_all, 0.0, causal
    )
    first_in = (
        decoder_input.astype(jnp.float32) + project(self_mixed, attention_low[3]) + vectors[2]
    )
    first_out, first_back = jax.vjp(layer_norm, first_in, vectors[11], vectors[12])
    first_low = first_out.astype(jnp.bfloat16)
    cross_query = (project(first_low, attention_low[4]) + vectors[3]).astype(jnp.bfloat16)
    cross_key = project(encoder_memory, attention_low[5]).astype(jnp.bfloat16)
    cross_value = (project(encoder_memory, attention_low[6]) + vectors[4]).astype(jnp.bfloat16)
    memory_keys, memory_values = (
        lax.all_gather(cross_key, "index", axis=1, tiled=True),
        lax.all_gather(cross_value, "index", axis=1, tiled=True),
    )
    question_full = lax.all_gather(question_vectors, "index", axis=1, tiled=True)
    passages_here = passage_vectors.shape[0]
    local_ids = passage_ids - shard_index * passages_here
    owned_slot = (local_ids >= 0) & (local_ids < passages_here)
    picked = passage_vectors[jnp.clip(local_ids, 0, passages_here - 1)]
    local_scores = jnp.einsum(
        "sc,skc->sk", question_full, picked, preferred_element_type=jnp.float32
    )
    slots = passage_ids.shape[1]
    usable = jnp.arange(slots)[None, :] < valid_count[:, None]
    local_peak = jnp.max(jnp.where(owned_slot & usable, local_scores, negative_fill), axis=1)
    maximum = lax.pmax(local_peak, "index")
    local_exp = jnp.where(owned_slot & usable, jnp.exp(local_scores - maximum[:, None]), 0.0)
    exponent, scores = lax.psum((local_exp, jnp.where(owned_slot, local_scores, 0.0)), "index")
    masked = jnp.where(usable, scores, negative_fill)
    partition = jnp.sum(exponent, axis=1)
    passage_prob = exponent / partition[:, None]
    log_prior = masked - maximum[:, None] - jnp.log(partition)[:, None]
    memory_total = memory_keys.shape[1]
    bias_rows = jnp.repeat(log_prior, MEM_P, axis=1)
    key_bias = bias_rows[:, None, None, :]
    key_usable = ((jnp.arange(memory_total) // MEM_P)[None, :] < valid_count[:, None])[
        :, None, None, :
    ]
    cross_mixed, cross_prob, cross_peak, cross_total = attend_forward(
        cross_query, memory_keys, memory_values, key_bias, key_usable
    )
    second_in = first_out + project(cross_mixed, attention_low[7]) + vectors[5]
    second_out, second_back = jax.vjp(layer_norm, second_in, vectors[13], vectors[14])
    second_low = second_out.astype(jnp.bfloat16)
    inner_act = project(second_low, expand_low) + vectors[6:10].reshape(ffn_width)
    activated, gelu_back = jax.vjp(partial(jax.nn.gelu, approximate=False), inner_act)
    activ_low = activated.astype(jnp.bfloat16)
    third_in = second_out + project(activ_low, contract_low) + vectors[10]
    layer_output, third_back = jax.vjp(layer_norm, third_in, vectors[15], vectors[16])
    grad_third, gain_three, shift_three = third_back(output_grad.astype(jnp.float32))
    grad_ffn_low = grad_third.astype(jnp.bfloat16)
    grad_contract = weight_grad(activ_low, grad_ffn_low)
    (grad_inner,) = gelu_back(project_back(grad_ffn_low, contract_low))
    grad_inner_low = grad_inner.astype(jnp.bfloat16)
    grad_expand = weight_grad(second_low, grad_inner_low)
    grad_second = grad_third + project_back(grad_inner_low, expand_low)
    grad_second_in, gain_two, shift_two = second_back(grad_second)
    grad_cross_low = grad_second_in.astype(jnp.bfloat16)
    grad_cmix = project_back(grad_cross_low, attention_low[7]).astype(jnp.bfloat16)
    cross_score, cross_inner = score_grads(grad_cmix, cross_prob, memory_values)
    grad_cq = to_queries(cross_score, memory_keys)
    prior_part = (
        jnp.sum(cross_score, axis=(1, 2), dtype=jnp.float32)
        .reshape(seqs_here, slots, MEM_P)
        .sum(axis=-1)
    )
    prior_grad = jnp.where(usable, lax.psum(prior_part, "index"), 0.0)
    score_doc = jnp.where(
        usable, prior_grad - passage_prob * jnp.sum(prior_grad, axis=1, keepdims=True), 0.0
    )
    question_part = jnp.einsum(
        "sk,skc->sc",
        jnp.where(owned_slot, score_doc, 0.0),
        picked.astype(jnp.float32),
        precision=lax.Precision.HIGHEST,
    )
    question_gradient = lax.psum_scatter(question_part, "index", scatter_dimension=1, tiled=True)
    grad_cq_low = grad_cq.astype(jnp.bfloat16)
    grad_first = grad_second_in + project_back(grad_cq_low, attention_low[4])
    ck_part, cv_part = to_keys(cross_score, cross_prob, cross_query, grad_cmix)
    grad_ck, grad_cv = (
        lax.psum_scatter(
            ck_part.astype(jnp.bfloat16), "index", scatter_dimension=1, tiled=True
        ).astype(jnp.float32),
        lax.psum_scatter(
            cv_part.astype(jnp.bfloat16), "index", scatter_dimension=1, tiled=True
        ).astype(jnp.float32),
    )
    grad_ck_low = grad_ck.astype(jnp.bfloat16)
    grad_cv_low = grad_cv.astype(jnp.bfloat16)
    memory_gradient = project_back(grad_ck_low, attention_low[5]) + project_back(
        grad_cv_low, attention_low[6]
    )
    grad_first_in, gain_one, shift_one = first_back(grad_first)
    grad_self_low = grad_first_in.astype(jnp.bfloat16)
    grad_smix = project_back(grad_self_low, attention_low[3]).astype(jnp.bfloat16)
    self_score, row_inner = score_grads(grad_smix, self_prob, value_all)
    grad_sq = to_queries(self_score, key_all)
    key_part, value_part = to_keys(self_score, self_prob, self_query, grad_smix)
    grad_sk, grad_sv = (
        lax.psum_scatter(
            key_part.astype(jnp.bfloat16), "index", scatter_dimension=1, tiled=True
        ).astype(jnp.float32),
        lax.psum_scatter(
            value_part.astype(jnp.bfloat16), "index", scatter_dimension=1, tiled=True
        ).astype(jnp.float32),
    )
    grad_sq_low = grad_sq.astype(jnp.bfloat16)
    grad_sk_low = grad_sk.astype(jnp.bfloat16)
    grad_sv_low = grad_sv.astype(jnp.bfloat16)
    input_gradient = (
        grad_first_in
        + project_back(grad_sq_low, attention_low[0])
        + project_back(grad_sk_low, attention_low[1])
        + project_back(grad_sv_low, attention_low[2])
    )
    attention_grads = jnp.stack(
        [
            weight_grad(decoder_input, grad_sq_low),
            weight_grad(decoder_input, grad_sk_low),
            weight_grad(decoder_input, grad_sv_low),
            weight_grad(self_mixed, grad_self_low),
            weight_grad(first_low, grad_cq_low),
            weight_grad(encoder_memory, grad_ck_low),
            weight_grad(encoder_memory, grad_cv_low),
            weight_grad(cross_mixed, grad_cross_low),
        ]
    )
    vector_grads = jnp.concatenate(
        [
            jnp.stack(
                [
                    row_total(grad_sq),
                    row_total(grad_sv),
                    row_total(grad_first_in),
                    row_total(grad_cq),
                    row_total(grad_cv),
                    row_total(grad_second_in),
                ]
            ),
            row_total(grad_inner).reshape(ffn_width // model_width, model_width),
            jnp.stack(
                [
                    row_total(grad_third),
                    gain_one,
                    shift_one,
                    gain_two,
                    shift_two,
                    gain_three,
                    shift_three,
                ]
            ),
        ]
    )
    attention_sum, expand_sum, contract_sum, vector_sum = (
        lax.psum_scatter(attention_grads, ("dp", "index"), scatter_dimension=1, tiled=True),
        lax.psum_scatter(grad_expand, ("dp", "index"), scatter_dimension=0, tiled=True),
        lax.psum_scatter(grad_contract, ("dp", "index"), scatter_dimension=0, tiled=True),
        lax.psum_scatter(vector_grads, ("dp", "index"), scatter_dimension=1, tiled=True),
    )
    new_attention = adam_update(
        attention_weight,
        attention_mean,
        attention_square,
        attention_sum,
        rate_attention,
        decay_matrix,
    )
    new_expand = adam_update(
        expand_weight, expand_mean, expand_square, expand_sum, rate_expand, decay_matrix
    )
    new_contract = adam_update(
        contract_weight, contract_mean, contract_square, contract_sum, rate_contract, decay_matrix
    )
    new_vector = adam_update(
        vector_params, vector_mean, vector_square, vector_sum, rate_vector, 0.0
    )
    return (
        layer_output.astype(jnp.bfloat16),
        input_gradient,
        memory_gradient,
        question_gradient,
        new_attention[0],
        new_attention[1],
        new_attention[2],
        new_expand[0],
        new_expand[1],
        new_expand[2],
        new_contract[0],
        new_contract[1],
        new_contract[2],
        new_vector[0],
        new_vector[1],
        new_vector[2],
    )


def solution(mesh):
    return jax.shard_map(
        body,
        mesh=mesh,
        in_specs=(
            P("dp", "index", None),
            P("dp", "index", None),
            P("dp", "index"),
            P("index", None),
            P("dp", None),
            P("dp"),
            P("dp", "index", None),
            P(None, ("dp", "index"), None),
            P(("dp", "index"), None),
            P(("dp", "index"), None),
            P(None, ("dp", "index")),
            P(None, ("dp", "index"), None),
            P(None, ("dp", "index"), None),
            P(("dp", "index"), None),
            P(("dp", "index"), None),
            P(("dp", "index"), None),
            P(("dp", "index"), None),
            P(None, ("dp", "index")),
            P(None, ("dp", "index")),
        ),
        out_specs=(
            P("dp", "index", None),
            P("dp", "index", None),
            P("dp", "index", None),
            P("dp", "index"),
            P(None, ("dp", "index"), None),
            P(None, ("dp", "index"), None),
            P(None, ("dp", "index"), None),
            P(("dp", "index"), None),
            P(("dp", "index"), None),
            P(("dp", "index"), None),
            P(("dp", "index"), None),
            P(("dp", "index"), None),
            P(("dp", "index"), None),
            P(None, ("dp", "index")),
            P(None, ("dp", "index")),
            P(None, ("dp", "index")),
        ),
        check_vma=False,
    )
```

profile of v0, /device:TPU:0, one launch (start us, length us, event | category | flops | bytes accessed | tf_op | source)
XLA Modules:
  0.0 1768.9 jit_solution(9408273552886573980)
XLA Ops:
  10.3 44.4 %all-gather = bf16[32,32,17]{1,2,0:T(8,128)(2,1)S(1)} all-gather(bf16[1,32,17]{1,2,0:T(8,128)(2,1)S(1)} %convert_bitcast_fusion), channel_id=1, replica_groups=mesh['dp'=4,'index'=8] {'dp','index'}, dimensions={0}, use_global_device_ids=true | all-gather | bytes 35904 | tf_op jit(solution)/shard_map/all_gather | solution.py:164
  54.9 74.1 %all-gather.10.cloned.1.call-done = bf16[8,1024,1024]{2,1,0:T(8,128)(2,1)} async-done(((bf16[8,32,1024]{2,1,0:T(8,128)(2,1)}), bf16[8,1024,1024]{2,1,0:T(8,128)(2,1)}) %all-gather.10.cloned.1.call-update) | async-done | bytes 16777232 | tf_op jit(solution)/shard_map/all_gather | solution.py:161
  145.0 8.7 all-gather.1
  158.3 13.3 pmax.7
  171.8 12.2 all-reduce
  187.2 6.6 copy.139
  193.8 12.8 all-gather.14.cloned.1.call-done
  206.6 6.2 copy.141
  212.9 11.3 fusion.144
  224.2 10.1 fusion.84
  241.8 19.4 %all-gather.16.cloned.1.call-done = bf16[2,1920,1024]{2,1,0:T(8,128)(2,1)} async-done(((bf16[2,240,1024]{2,1,0:T(8,128)(2,1)}), bf16[2,1920,1024]{2,1,0:T(8,128)(2,1)}) %all-gather.16.cloned.1.call-update) | async-done | bytes 7864336 | tf_op jit(solution)/shard_map/all_gather | solution.py:193
  261.2 10.5 copy.143
  271.7 44.0 %all-gather.18.cloned.1.call-done = bf16[2,1920,1024]{2,1,0:T(8,128)(2,1)} async-done(((bf16[2,240,1024]{2,1,0:T(8,128)(2,1)}), bf16[2,1920,1024]{2,1,0:T(8,128)(2,1)}) %all-gather.18.cloned.1.call-update) | async-done | bytes 7864336 | tf_op jit(solution)/shard_map/all_gather | solution.py:192
  315.7 10.3 copy.145
  326.1 18.2 %fusion.146 = (f32[2,16,128]{2,1,0:T(8,128)S(1)}, f32[2,16,128,1920]{3,2,1,0:T(8,128)}) fusion(f32[2,1920]{1,0:T(2,128)S(1)} %add.302, pred[2,1920]{1,0:T(4,128)(4,1)S(1)} %broadcast_compare_fusion, bf16[2,128,16,64]{1,3,2,0:T(8,128)(2,1)S(1)} %bitcast.338, bf16[2,1920,16,64]{1,3,2,0:T(8,128)(2,1)} %bitcast.320), kind=kOutput, calls=%fused_computation.240 | convolution fusion | flops 1045956480 | bytes 39881472 | tf_op jit(solution)/shard_map/sub | solution.py:68
  344.3 16.4 fusion.93
  363.6 32.9 %all-gather.20.cloned.1.call-done = bf16[1024,4096]{1,0:T(8,128)(2,1)} async-done(((bf16[32,4096]{1,0:T(8,128)(2,1)}), bf16[1024,4096]{1,0:T(8,128)(2,1)}) %all-gather.20.cloned.1.call-update) | async-done | bytes 8388624 | tf_op jit(solution)/shard_map/all_gather | solution.py:162
  396.5 7.1 fusion.105
  405.6 10.8 multiply_convert_fusion.4
  416.4 59.6 %all-gather.22.cloned.1.call-done = bf16[4096,1024]{1,0:T(8,128)(2,1)} async-done(((bf16[128,1024]{1,0:T(8,128)(2,1)}), bf16[4096,1024]{1,0:T(8,128)(2,1)}) %all-gather.22.cloned.1.call-update) | async-done | bytes 8388624 | tf_op jit(solution)/shard_map/all_gather | solution.py:163
  476.0 6.6 fusion.148
  485.2 9.4 fusion.149
  494.6 7.3 multiply_reduce_fusion.2
  506.0 26.9 %multiply_reduce_fusion = (f32[2,16,128]{2,1,0:T(8,128)S(1)}, f32[2,16,128,1920]{3,2,1,0:T(8,128)}) fusion(f32[2,16,128,1920]{3,2,1,0:T(8,128)} %get-tuple-element.142, f32[2,16,128]{2,1,0:T(8,128)S(1)} %get-tuple-element.141, bf16[2,128,16,64]{1,3,2,0:T(8,128)(2,1)S(1)} %bitcast.352, bf16[2,1920,16,64]{1,3,2,0:T(8,128)(2,1)} %bitcast.331), kind=kOutput, calls=%fused_computation.5 | convolution fusion | flops 1030221824 | bytes 71335936 | tf_op jit(solution)/shard_map/sqhd,skhd->shqk/dot_general | solution.py:81
  532.9 26.0 %convert_reduce_fusion = (f32[2,1920]{1,0:T(2,128)S(1)}, bf16[2,16,128,1920]{3,2,1,0:T(8,128)(2,1)}) fusion(f32[2,16,128,1920]{3,2,1,0:T(8,128)} %get-tuple-element.150, f32[2,16,128]{2,1,0:T(8,128)S(1)} %get-tuple-element.149, f32[2,16,128,1920]{3,2,1,0:T(8,128)} %get-tuple-element.142, f32[2,16,128]{2,1,0:T(8,128)S(1)} %get-tuple-element.141), kind=kLoop, calls=%fused_computation.3 | loop fusion | flops 47182080 | bytes 78691328 | tf_op jit(solution)/shard_map/reduce_sum | solution.py:243
  558.9 12.2 fusion.141
  577.1 8.7 fusion.41
  585.8 11.4 copy.193
  597.1 5.6 copy.201
  603.8 16.6 fusion.23
  620.4 10.7 copy.155
  631.1 13.5 multiply_reduce_fusion.1
  644.6 11.8 multiply_convert_fusion.1
  660.9 11.6 copy.191
  672.5 5.7 copy.200
  679.3 12.3 multiply_convert_fusion.2
  691.6 10.7 copy.154
  702.5 13.4 psum.23
  717.7 8.8 fusion.142
  737.1 10.1 convolution_bitcast_fusion
  748.5 9.8 convolution_bitcast_fusion.1
  762.2 18.4 %reduce-scatter.28.cloned.1.call-done = bf16[128,2048]{1,0:T(8,128)(2,1)} async-done(((bf16[1024,2048]{1,0:T(8,128)(2,1)}), bf16[128,2048]{1,0:T(8,128)(2,1)}) %reduce-scatter.28.cloned.1.call-update) | async-done | bytes 524304
  795.6 58.3 %reduce-scatter.18.cloned.1.call-done = bf16[2,240,1024]{2,1,0:T(8,128)(2,1)} async-done(((bf16[2,1920,1024]{2,1,0:T(8,128)(2,1)}), bf16[2,240,1024]{2,1,0:T(8,128)(2,1)}) %reduce-scatter.18.cloned.1.call-update) | async-done | bytes 983056 | tf_op jit(solution)/shard_map/reduce_scatter | solution.py:262
  864.5 33.3 %copy.162 = f32[8,1024,1024]{2,0,1:T(8,128)} copy(f32[8,1024,1024]{1,2,0:T(8,128)} %bitcast_dynamic-update-slice_fusion.5) | data formatting | bytes 67108864 | tf_op jit(solution)/shard_map/stack | solution.py:297
  915.9 111.1 %reduce-scatter.34.cloned.1.call-done = f32[32,17]{1,0:T(8,128)} async-done(((f32[1024,17]{1,0:T(8,128)}), f32[32,17]{1,0:T(8,128)}) %reduce-scatter.34.cloned.1.call-update) | async-done | bytes 2192
  1028.4 180.2 %reduce-scatter.26.cloned.1.call-done = f32[128,1024]{1,0:T(8,128)} async-done(((f32[4096,1024]{1,0:T(8,128)}), f32[128,1024]{1,0:T(8,128)}) %reduce-scatter.26.cloned.1.call-update) | async-done | bytes 524304 | tf_op jit(solution)/shard_map/reduce_scatter | solution.py:338
  1211.5 183.3 %reduce-scatter.24.cloned.1.call-done = f32[32,4096]{1,0:T(8,128)} async-done(((f32[1024,4096]{1,0:T(8,128)}), f32[32,4096]{1,0:T(8,128)}) %reduce-scatter.24.cloned.1.call-update) | async-done | bytes 524304 | tf_op jit(solution)/shard_map/reduce_scatter | solution.py:337
  1397.5 355.5 %reduce-scatter.22.cloned.1.call-done = f32[8,32,1024]{2,0,1:T(8,128)} async-done(((f32[8,1024,1024]{2,0,1:T(8,128)}), f32[8,32,1024]{2,0,1:T(8,128)}) %reduce-scatter.22.cloned.1.call-update) | async-done | bytes 1048592 | tf_op jit(solution)/shard_map/reduce_scatter | solution.py:336
  (308 shorter events, 135.2 us)
Async XLA Ops:
  7.2 128.3 %copy-start = (bf16[2,240,1024]{2,1,0:T(8,128)(2,1)S(1)}, bf16[2,240,1024]{2,1,0:T(8,128)(2,1)}, u32[]{:S(2)}) copy-start(bf16[2,240,1024]{2,1,0:T(8,128)(2,1)} %param.20) | copy-start | bytes 2949124
  7.2 125.1 %copy-start.11 = (bf16[2,128,1024]{2,1,0:T(8,128)(2,1)S(1)}, bf16[2,128,1024]{2,1,0:T(8,128)(2,1)}, u32[]{:S(2)}) copy-start(bf16[2,128,1024]{2,1,0:T(8,128)(2,1)} %param.19) | copy-start | bytes 1572868
  7.2 121.7 %all-gather.10.cloned.1.call-start = ((), (), s32[]{:S(2)}) async-start(), calls=%async_computation.9 | async-start | bytes 17301504 | tf_op jit(solution)/shard_map/all_gather | solution.py:161
  9.5 177.7 %all-gather.12.cloned.1.call-start = ((), (), s32[]{:S(2)}) async-start(), calls=%async_computation.10 | async-start | bytes 4718592 | tf_op jit(solution)/shard_map/all_gather | solution.py:176
  54.8 305.8 %copy-start.60 = (f32[1,1024]{1,0:T(1,128)}, f32[1,1024]{1,0:T(1,128)S(1)}, u32[]{:S(2)}) copy-start(f32[1,1024]{1,0:T(1,128)S(1)} %get-tuple-element.130) | copy-start | bytes 12292
  54.8 421.2 %copy-start.42 = (f32[1,1024]{1,0:T(1,128)}, f32[1,1024]{1,0:T(1,128)S(1)}, u32[]{:S(2)}) copy-start(f32[1,1024]{1,0:T(1,128)S(1)} %get-tuple-element.125) | copy-start | bytes 12292
  54.9 447.1 %copy-start.40 = (f32[1,1024]{1,0:T(1,128)}, f32[1,1024]{1,0:T(1,128)S(1)}, u32[]{:S(2)}) copy-start(f32[1,1024]{1,0:T(1,128)S(1)} %get-tuple-element.126) | copy-start | bytes 12292
  54.9 519.1 %copy-start.49 = (f32[1,1024]{1,0:T(1,128)}, f32[1,1024]{1,0:T(1,128)S(1)}, u32[]{:S(2)}) copy-start(f32[1,1024]{1,0:T(1,128)S(1)} %get-tuple-element.131) | copy-start | bytes 12292
  132.2 74.4 %all-gather.14.cloned.1.call-start = ((), (), s32[]{:S(2)}) async-start(), calls=%async_computation.11 | async-start | bytes 4718592 | tf_op jit(solution)/shard_map/all_gather | solution.py:175
  135.4 125.8 %all-gather.16.cloned.1.call-start = ((), (), s32[]{:S(2)}) async-start(), calls=%async_computation.12 | async-start | bytes 8847360 | tf_op jit(solution)/shard_map/all_gather | solution.py:193
  139.3 18.8 %copy-start.53 = (s32[2]{0:T(128)S(1)}, s32[2]{0:T(128)}, u32[]{:S(2)}) copy-start(s32[2]{0:T(128)} %param.24) | copy-start | bytes 28
  139.3 176.4 %all-gather.18.cloned.1.call-start = ((), (), s32[]{:S(2)}) async-start(), calls=%async_computation.13 | async-start | bytes 8847360 | tf_op jit(solution)/shard_map/all_gather | solution.py:192
  143.2 253.3 %all-gather.20.cloned.1.call-start = ((), (), s32[]{:S(2)}) async-start(), calls=%async_computation.14 | async-start | bytes 8650752 | tf_op jit(solution)/shard_map/all_gather | solution.py:162
  144.0 332.0 %all-gather.22.cloned.1.call-start = ((), (), s32[]{:S(2)}) async-start(), calls=%async_computation.15 | async-start | bytes 8650752 | tf_op jit(solution)/shard_map/all_gather | solution.py:163
  144.8 583.8 %reduce-scatter.30.cloned.1.call-start = ((), (), s32[]{:S(2)}) async-start(), calls=%async_computation.22 | async-start | bytes 4718592
  158.0 26.6 %copy-start.44 = (bf16[2,10,768]{2,1,0:T(8,128)(2,1)}, bf16[2,10,768]{2,1,0:T(8,128)(2,1)S(1)}, u32[]{:S(2)}) copy-start(bf16[2,10,768]{2,1,0:T(8,128)(2,1)S(1)} %reshape.295) | copy-start | bytes 92164
  158.3 35.5 %copy-start.72 = (pred[2,10]{1,0:T(4,128)(4,1)}, pred[2,10]{1,0:T(4,128)(4,1)S(1)}, u32[]{:S(2)}) copy-start(pred[2,10]{1,0:T(4,128)(4,1)S(1)} %get-tuple-element.116) | copy-start | bytes 64
  187.2 25.7 %copy-start.31 = (bf16[2,128,1024]{1,2,0:T(8,128)(2,1)}, bf16[2,128,1024]{1,2,0:T(8,128)(2,1)S(1)}, u32[]{:S(2)}) copy-start(bf16[2,128,1024]{1,2,0:T(8,128)(2,1)S(1)} %copy.140) | copy-start | bytes 1572868
  236.9 337.0 %copy-start.2 = (f32[2,128,1024]{2,1,0:T(8,128)}, f32[2,128,1024]{2,1,0:T(8,128)S(1)}, u32[]{:S(2)}) copy-start(f32[2,128,1024]{2,1,0:T(8,128)S(1)} %get-tuple-element.140) | copy-start | bytes 3145732
  237.0 337.0 %copy-start.62 = (f32[2,128]{1,0:T(2,128)}, f32[2,128]{1,0:T(2,128)S(1)}, u32[]{:S(2)}) copy-start(f32[2,128]{1,0:T(2,128)S(1)} %broadcast_multiply_fusion.2) | copy-start | bytes 3076
  237.2 34.5 %copy-start.68 = (f32[2,128]{1,0:T(2,128)}, f32[2,128]{1,0:T(2,128)S(1)}, u32[]{:S(2)}) copy-start(f32[2,128]{1,0:T(2,128)S(1)} %multiply_reduce_fusion.8) | copy-start | bytes 3076
  237.2 336.7 %copy-start.70 = (f32[2,128]{1,0:T(2,128)}, f32[2,128]{1,0:T(2,128)S(1)}, u32[]{:S(2)}) copy-start(f32[2,128]{1,0:T(2,128)S(1)} %fusion.124) | copy-start | bytes 3076
  241.8 84.3 %copy-start.25 = (bf16[2,128,1024]{1,2,0:T(8,128)(2,1)}, bf16[2,128,1024]{1,2,0:T(8,128)(2,1)S(1)}, u32[]{:S(2)}) copy-start(bf16[2,128,1024]{1,2,0:T(8,128)(2,1)S(1)} %copy.144) | copy-start | bytes 1572868
  363.3 138.7 %copy-start.4 = (f32[2,128,1024]{2,1,0:T(8,128)}, f32[2,128,1024]{2,1,0:T(8,128)S(1)}, u32[]{:S(2)}) copy-start(f32[2,128,1024]{2,1,0:T(8,128)S(1)} %get-tuple-element.144) | copy-start | bytes 3145732
  363.3 138.6 %copy-start.47 = (f32[2,128]{1,0:T(2,128)}, f32[2,128]{1,0:T(2,128)S(1)}, u32[]{:S(2)}) copy-start(f32[2,128]{1,0:T(2,128)S(1)} %broadcast_multiply_fusion.1) | copy-start | bytes 3076
  363.6 138.4 %copy-start.51 = (f32[2,128]{1,0:T(2,128)}, f32[2,128]{1,0:T(2,128)S(1)}, u32[]{:S(2)}) copy-start(f32[2,128]{1,0:T(2,128)S(1)} %fusion.126) | copy-start | bytes 3076
  506.0 26.9 %copy-start.38 = (bf16[2,128,1024]{1,2,0:T(8,128)(2,1)}, bf16[2,128,1024]{1,2,0:T(8,128)(2,1)S(1)}, u32[]{:S(2)}) copy-start(bf16[2,128,1024]{1,2,0:T(8,128)(2,1)S(1)} %copy.148) | copy-start | bytes 1572868
  602.7 131.6 %reduce-scatter.20.cloned.1.call-start = ((), (), s32[]{:S(2)}) async-start(), calls=%async_computation.17 | async-start | bytes 8847360 | tf_op jit(solution)/shard_map/reduce_scatter | solution.py:265
  631.1 149.6 %reduce-scatter.28.cloned.1.call-start = ((), (), s32[]{:S(2)}) async-start(), calls=%async_computation.21 | async-start | bytes 4718592
  678.3 175.7 %reduce-scatter.18.cloned.1.call-start = ((), (), s32[]{:S(2)}) async-start(), calls=%async_computation.16 | async-start | bytes 8847360 | tf_op jit(solution)/shard_map/reduce_scatter | solution.py:262
  702.2 13.7 copy-start.59
  702.2 13.7 copy-start.13
  702.2 14.0 copy-start.54
  702.2 14.2 copy-start.73
  702.2 14.2 copy-start.75
  702.2 14.2 copy-start.80
  702.3 14.3 copy-start.45
  702.3 199.1 %reduce-scatter.32.cloned.1.call-start = ((), (), s32[]{:S(2)}) async-start(), calls=%async_computation.23 | async-start | bytes 442368
  728.5 298.5 %reduce-scatter.34.cloned.1.call-start = ((), (), s32[]{:S(2)}) async-start(), calls=%async_computation.24 | async-start | bytes 540672
  737.1 471.6 %reduce-scatter.26.cloned.1.call-start = ((), (), s32[]{:S(2)}) async-start(), calls=%async_computation.20 | async-start | bytes 17301504 | tf_op jit(solution)/shard_map/reduce_scatter | solution.py:338
  747.3 647.5 %reduce-scatter.24.cloned.1.call-start = ((), (), s32[]{:S(2)}) async-start(), calls=%async_computation.19 | async-start | bytes 17301504 | tf_op jit(solution)/shard_map/reduce_scatter | solution.py:337
  758.3 994.7 %reduce-scatter.22.cloned.1.call-start = ((), (), s32[]{:S(2)}) async-start(), calls=%async_computation.18 | async-start | bytes 34603008 | tf_op jit(solution)/shard_map/reduce_scatter | solution.py:336
  911.7 116.1 %copy-start.46 = (f32[17,32]{1,0:T(8,128)S(1)}, f32[17,32]{1,0:T(8,128)}, u32[]{:S(2)}) copy-start(f32[17,32]{1,0:T(8,128)} %param.29) | copy-start | bytes 6532
  911.7 116.1 %copy-start.64 = (f32[17,32]{1,0:T(8,128)S(1)}, f32[17,32]{1,0:T(8,128)}, u32[]{:S(2)}) copy-start(f32[17,32]{1,0:T(8,128)} %param.36) | copy-start | bytes 6532
  911.7 116.1 %copy-start.65 = (f32[17,32]{1,0:T(8,128)S(1)}, f32[17,32]{1,0:T(8,128)}, u32[]{:S(2)}) copy-start(f32[17,32]{1,0:T(8,128)} %param.37) | copy-start | bytes 6532
  911.7 297.0 %copy-start.28 = (f32[128,1024]{1,0:T(8,128)S(1)}, f32[128,1024]{1,0:T(8,128)}, u32[]{:S(2)}) copy-start(f32[128,1024]{1,0:T(8,128)} %param.28) | copy-start | bytes 1572868
  911.7 483.0 %copy-start.30 = (f32[32,4096]{1,0:T(8,128)S(1)}, f32[32,4096]{1,0:T(8,128)}, u32[]{:S(2)}) copy-start(f32[32,4096]{1,0:T(8,128)} %param.27) | copy-start | bytes 1572868
  915.9 837.0 %copy-start.18 = (f32[8,32,1024]{2,1,0:T(8,128)S(1)}, f32[8,32,1024]{2,1,0:T(8,128)}, u32[]{:S(2)}) copy-start(f32[8,32,1024]{2,1,0:T(8,128)} %param.26) | copy-start | bytes 3145732
  (50 other events, 253.7 us)
Sparse Core Ops, SparseCore 0:
  11.5 117.3 all-gather.9
  132.4 34.9 all-gather.11
  169.8 36.7 all-gather.13
  209.0 52.1 all-gather.15
  263.5 52.1 all-gather.17
  319.0 77.4 all-gather.19
  399.9 76.0 all-gather.21
  602.9 49.9 reduce-scatter.29
  656.7 69.4 reduce-scatter.19
  729.4 51.2 reduce-scatter.27
  784.5 69.3 reduce-scatter.17
  856.8 33.8 reduce-scatter.31
  893.0 133.9 reduce-scatter.33
  1029.3 179.3 reduce-scatter.25
  1210.9 183.7 reduce-scatter.23
  1397.0 355.9 reduce-scatter.21
where the time goes:
time: 1780 us; the launch traced here: 1770 us
  waiting for transfers between devices  1150 us (65%)
  matrix products  284 us (16%)
  local copies, waits for them, and re-layouts  154 us (9%)
  blocking collectives  92 us (5%)
  other arithmetic  73 us (4%)
    reduce_scatter x1, waiting for transfers between devices, body(): lax.psum_scatter(attention_grads, ('dp', 'index'), scatter_dimension=1, t...  356 us
    reduce_scatter x1, waiting for transfers between devices, body(): lax.psum_scatter(grad_expand, ('dp', 'index'), scatter_dimension=0, tiled...  183 us
    reduce_scatter x1, waiting for transfers between devices, body(): lax.psum_scatter(grad_contract, ('dp', 'index'), scatter_dimension=0, til...  180 us
    unnamed x20, waiting for transfers between devices  130 us
    all_gather x1, waiting for transfers between devices, body(): lax.all_gather(attention_weight.astype(jnp.bfloat16), ('dp', 'index'), ax...  74.1 us
    all_gather x1, waiting for transfers between devices, body(): lax.all_gather(contract_weight.astype(jnp.bfloat16), ('dp', 'index'), axi...  59.6 us
    unnamed x182, local copies, waits for them, and re-layouts  58.7 us
    reduce_scatter x1, waiting for transfers between devices, body(): lax.psum_scatter(ck_part.astype(jnp.bfloat16), 'index', scatter_dimension...  58.3 us
  transfers between devices with their start and end apart: 16, of which 12 were waited for; matrix products, arithmetic and copies ran while one was open for 21% of the time, Pallas kernels for 0%

commit v1 on v0

--- a/solution.py
+++ b/solution.py
@@ -3,6 +3,8 @@
 import jax
 import jax.numpy as jnp
 from jax import lax
+from jax.experimental import pallas as pl
+from jax.experimental.pallas import tpu as pltpu
 from jax.sharding import PartitionSpec as P
 
 HEADS = 16
@@ -136,7 +138,7 @@
     return (updated, mean_new, square_new)
 
 
-def body(
+def general_body(
     decoder_input,
     encoder_memory,
     question_vectors,
@@ -375,9 +377,1331 @@
     )
 
 
+NT = (((1,), (1,)), ((), ()))
+NN = (((1,), (0,)), ((), ()))
+TN = (((0,), (0,)), ((), ()))
+CHIPS = 4
+DP_ORDER = (0, 2, 1, 3)
+VMEM_LIMIT = 56 << 20
+
+
+def dot(left_side, right_side, dims):
+    return lax.dot_general(left_side, right_side, dims, preferred_element_type=jnp.float32)
+
+
+def norm_parts(hidden):
+    center = hidden - jnp.mean(hidden, axis=-1, keepdims=True)
+    inverse = lax.rsqrt(jnp.mean(center * center, axis=-1, keepdims=True) + norm_eps)
+    return center * inverse, inverse
+
+
+def norm_back(gradient, unit, inverse, gain):
+    scaled = gradient * gain
+    return inverse * (
+        scaled
+        - jnp.mean(scaled, axis=-1, keepdims=True)
+        - unit * jnp.mean(scaled * unit, axis=-1, keepdims=True)
+    )
+
+
+def column_sum(values):
+    return jnp.sum(values, axis=0, keepdims=True)
+
+
+def join(parts, place=None):
+    picked = [parts[j] if place is None else parts[j, place] for j in range(parts.shape[0])]
+    return jnp.concatenate(
+        [block.reshape(block.shape[0] * block.shape[1], block.shape[2]) for block in picked],
+        axis=1,
+    )
+
+
+def spread(out_ref, value):
+    count, seqs, rows, width = out_ref.shape
+    for j in range(count):
+        out_ref[j] = value[:, j * width : (j + 1) * width].reshape(seqs, rows, width)
+
+
+def times(activation, weight):
+    count, groups, rows, width = weight.shape
+    depth = count * rows
+    total = None
+    for d in range(groups):
+        part = dot(
+            activation[:, d * depth : (d + 1) * depth], weight[:, d].reshape(depth, width), NN
+        )
+        total = part if total is None else total + part
+    return total
+
+
+def times_back(gradient, weight):
+    count, groups, rows, width = weight.shape
+    depth = count * rows
+    return jnp.concatenate(
+        [dot(gradient, weight[:, d].reshape(depth, width), NT) for d in range(groups)], axis=1
+    )
+
+
+def outer(out_ref, left_side, gradient):
+    count, groups, rows, width = out_ref.shape
+    depth = count * rows
+    for d in range(groups):
+        out_ref[:, d] = (
+            dot(left_side[:, d * depth : (d + 1) * depth], gradient, TN)
+            .astype(jnp.bfloat16)
+            .reshape(count, rows, width)
+        )
+
+
+def whole(array):
+    return pl.BlockSpec(array.shape, lambda *_, rank=len(array.shape): (0,) * rank)
+
+
+def shape(dims, dtype):
+    return jax.ShapeDtypeStruct(tuple(dims), dtype)
+
+
+def params():
+    return pltpu.CompilerParams(vmem_limit_bytes=VMEM_LIMIT)
+
+
+def cost(flops, moved):
+    return pl.CostEstimate(flops=int(flops) // 16, bytes_accessed=int(moved) // 16, transcendentals=0)
+
+
+def in_head(dims, head_width, head):
+    return lax.broadcasted_iota(jnp.int32, dims, 1) // head_width == head
+
+
+def attend_forward_kernel(causal, head_width, q_ref, k_ref, v_ref, bias_ref, out_ref, stat_ref):
+    count, _, tile, width = q_ref.shape
+    keys = k_ref.shape[0] * k_ref.shape[2]
+    key_rows, values = k_ref[...].reshape(keys, width), v_ref[...].reshape(keys, width)
+    step = 2
+    rows = step * tile
+    for b in range(count // step):
+        queries = q_ref[b * step : (b + 1) * step].reshape(rows, width)
+        seen = (b + 1) * rows if causal else keys
+        mixed = None
+        for h in range(width // head_width):
+            mask = in_head((rows, width), head_width, h)
+            scores = dot(
+                jnp.where(mask, queries * 0.125, 0).astype(jnp.bfloat16), key_rows[:seen], NT
+            )
+            if causal:
+                corner = scores[:, seen - rows :]
+                corner = jnp.where(
+                    lax.broadcasted_iota(jnp.int32, corner.shape, 1)
+                    <= lax.broadcasted_iota(jnp.int32, corner.shape, 0),
+                    corner,
+                    negative_fill,
+                )
+                if b == 0:
+                    scores = corner
+                else:
+                    scores = jnp.concatenate([scores[:, : seen - rows], corner], axis=1)
+            else:
+                scores = scores + bias_ref[0]
+            peak = jnp.max(scores, axis=1, keepdims=True)
+            exponent = jnp.exp(scores - peak)
+            total = jnp.sum(exponent, axis=1, keepdims=True)
+            prob = (exponent * (1.0 / total)).astype(jnp.bfloat16)
+            part = dot(prob, values[:seen], NN)
+            mixed = part if mixed is None else jnp.where(mask, part, mixed)
+            log_total = jnp.broadcast_to(peak + jnp.log(total), (rows, 128))
+            stat_ref[0, h : h + 1, b * rows : (b + 1) * rows] = log_total.T[0:1]
+        out_ref[b * step : (b + 1) * step] = mixed.astype(jnp.bfloat16).reshape(
+            step, 1, tile, width
+        )
+
+
+def attend_backward_kernel(
+    causal,
+    head_width,
+    q_ref,
+    k_ref,
+    v_ref,
+    grad_ref,
+    stat_ref,
+    bias_ref,
+    _,
+    dq_ref,
+    dkv_ref,
+    prior_ref,
+    dk_sum,
+    dv_sum,
+    prior_sum,
+):
+    count, _, tile, width = q_ref.shape
+    keys = k_ref.shape[0] * k_ref.shape[2]
+    key_rows, values = k_ref[...].reshape(keys, width), v_ref[...].reshape(keys, width)
+    step = 2
+    rows = step * tile
+    dk_sum[...] = jnp.zeros_like(dk_sum)
+    dv_sum[...] = jnp.zeros_like(dv_sum)
+    if not causal:
+        prior_sum[...] = jnp.zeros_like(prior_sum)
+    for b in range(count // step):
+        queries = q_ref[b * step : (b + 1) * step].reshape(rows, width)
+        gradient = grad_ref[b * step : (b + 1) * step].reshape(rows, width)
+        seen = (b + 1) * rows if causal else keys
+        query_grad = None
+        for h in range(width // head_width):
+            mask = in_head((rows, width), head_width, h)
+            one_query = jnp.where(mask, queries * 0.125, 0).astype(jnp.bfloat16)
+            one_grad = jnp.where(mask, gradient, 0).astype(jnp.bfloat16)
+            scores = dot(key_rows[:seen], one_query, NT)
+            if causal:
+                corner = scores[seen - rows :]
+                corner = jnp.where(
+                    lax.broadcasted_iota(jnp.int32, corner.shape, 0)
+                    <= lax.broadcasted_iota(jnp.int32, corner.shape, 1),
+                    corner,
+                    negative_fill,
+                )
+                if b == 0:
+                    scores = corner
+                else:
+                    scores = jnp.concatenate([scores[: seen - rows], corner], axis=0)
+            else:
+                scores = scores + bias_ref[0]
+            prob = jnp.exp(scores - stat_ref[0, h : h + 1, b * rows : (b + 1) * rows])
+            grad_prob = dot(values[:seen], one_grad, NT)
+            inner = jnp.sum(prob * grad_prob, axis=0, keepdims=True)
+            grad_score = prob * (grad_prob - inner)
+            score_low = grad_score.astype(jnp.bfloat16)
+            dv_sum[:seen] += dot(prob.astype(jnp.bfloat16), one_grad, NN)
+            dk_sum[:seen] += dot(score_low, one_query, NN)
+            if not causal:
+                partial_sum = grad_score[:, :128]
+                for piece in range(128, rows, 128):
+                    partial_sum = partial_sum + grad_score[:, piece : piece + 128]
+                prior_sum[...] += partial_sum
+            part = dot(score_low, key_rows[:seen], TN)
+            query_grad = part if query_grad is None else jnp.where(mask, part, query_grad)
+        dq_ref[b * step : (b + 1) * step] = (
+            (query_grad * 0.125).astype(jnp.bfloat16).reshape(step, 1, tile, width)
+        )
+    dkv_ref[:, 0] = dk_sum[...].astype(jnp.bfloat16).reshape(k_ref.shape)
+    dkv_ref[:, 1] = dv_sum[...].astype(jnp.bfloat16).reshape(k_ref.shape)
+    if causal:
+        prior_ref[...] = jnp.zeros_like(prior_ref)
+    else:
+        prior_ref[0] = jnp.sum(prior_sum[...], axis=1, keepdims=True)
+
+
+def pick(array, place):
+    count, _, _, rows, width = array.shape
+    return pl.BlockSpec((count, None, 1, rows, width), lambda s: (0, place, s, 0, 0))
+
+
+def attend(causal, queries, query_at, keys, key_at, value_at, bias):
+    count, _, seqs, tile, width = queries.shape
+    key_rows = keys.shape[0] * keys.shape[3]
+    head_width = width * count // HEADS
+    length = count * tile
+    heads = width // head_width
+    return pl.pallas_call(
+        partial(attend_forward_kernel, causal, head_width),
+        grid=(seqs,),
+        in_specs=[
+            pick(queries, query_at),
+            pick(keys, key_at),
+            pick(keys, value_at),
+            pl.BlockSpec(memory_space=pl.ANY)
+            if causal
+            else pl.BlockSpec((1, 1, key_rows), lambda s: (s, 0, 0)),
+        ],
+        out_specs=[
+            pl.BlockSpec((count, 1, tile, width), lambda s: (0, s, 0, 0)),
+            pl.BlockSpec((1, heads, length), lambda s: (s, 0, 0)),
+        ],
+        out_shape=[
+            shape((count, seqs, tile, width), jnp.bfloat16),
+            shape((seqs, heads, length), jnp.float32),
+        ],
+        compiler_params=params(),
+        cost_estimate=cost(
+            16 * seqs * length * key_rows * width, 4 * seqs * (length + key_rows) * width
+        ),
+        name="attend_self" if causal else "attend_memory",
+    )(queries, keys, keys, bias)
+
+
+def attend_back(
+    causal, queries, query_at, keys, key_at, value_at, gradient, stat, bias, after
+):
+    count, _, seqs, tile, width = queries.shape
+    key_tile = keys.shape[3]
+    key_rows = count * key_tile
+    head_width = width * count // HEADS
+    length = count * tile
+    heads = width // head_width
+    return pl.pallas_call(
+        partial(attend_backward_kernel, causal, head_width),
+        grid=(seqs,),
+        in_specs=[
+            pick(queries, query_at),
+            pick(keys, key_at),
+            pick(keys, value_at),
+            pl.BlockSpec((count, 1, tile, width), lambda s: (0, s, 0, 0)),
+            pl.BlockSpec((1, heads, length), lambda s: (s, 0, 0)),
+            pl.BlockSpec(memory_space=pl.ANY)
+            if causal
+            else pl.BlockSpec((1, key_rows, 1), lambda s: (s, 0, 0)),
+            pl.BlockSpec(memory_space=pl.ANY),
+        ],
+        out_specs=[
+            pl.BlockSpec((count, 1, tile, width), lambda s: (0, s, 0, 0)),
+            pl.BlockSpec((count, 2, 1, key_tile, width), lambda s: (0, 0, s, 0, 0)),
+            pl.BlockSpec((1, key_rows, 1), lambda s: (s, 0, 0)),
+        ],
+        out_shape=[
+            shape((count, seqs, tile, width), jnp.bfloat16),
+            shape((count, 2, seqs, key_tile, width), jnp.bfloat16),
+            shape((seqs, key_rows, 1), jnp.float32),
+        ],
+        scratch_shapes=[
+            pltpu.VMEM((key_rows, width), jnp.float32),
+            pltpu.VMEM((key_rows, width), jnp.float32),
+            pltpu.VMEM((key_rows, 128), jnp.float32),
+        ],
+        compiler_params=params(),
+        cost_estimate=cost(
+            40 * seqs * length * key_rows * width, 8 * seqs * (length + key_rows) * width
+        ),
+        name="attend_self_back" if causal else "attend_memory_back",
+    )(queries, keys, keys, gradient, stat, bias, after)
+
+
+def take_columns(scratch, slices, first):
+    width = slices.shape[3]
+    depth = scratch.shape[0]
+    rows = depth // (slices.shape[0] * slices.shape[1])
+    for m in range(scratch.shape[1] // width):
+        start = (first + m) * rows
+        scratch[:, m * width : (m + 1) * width] = slices[:, :, start : start + rows].reshape(
+            depth, width
+        )
+
+
+def columns_kernel(first, row_ref, slice_ref, bias_ref, out_ref, weight):
+    @pl.when(pl.program_id(0) == 0)
+    def _():
+        take_columns(weight, slice_ref, first)
+
+    _, many, seqs, rows, width = out_ref.shape
+    taken = row_ref[0, :, :rows].reshape(seqs * rows, weight.shape[0])
+    result = dot(taken, weight[...], NN) + bias_ref[...]
+    for m in range(many):
+        out_ref[0, m] = (
+            result[:, m * width : (m + 1) * width]
+            .astype(jnp.bfloat16)
+            .reshape(seqs, rows, width)
+        )
+
+
+def project_columns(name, gathered_rows, block_rows, row_block, rows, slices, first, many, bias):
+    count, seqs, _, depth = gathered_rows.shape
+    width = slices.shape[3]
+    return pl.pallas_call(
+        partial(columns_kernel, first),
+        grid=(count,),
+        in_specs=[
+            pl.BlockSpec((1, seqs, block_rows, depth), lambda i: (i, 0, row_block, 0)),
+            whole(slices),
+            whole(bias),
+        ],
+        out_specs=pl.BlockSpec((1, many, seqs, rows, width), lambda i: (i, 0, 0, 0, 0)),
+        out_shape=shape((count, many, seqs, rows, width), jnp.bfloat16),
+        scratch_shapes=[pltpu.VMEM((depth, many * width), jnp.bfloat16)],
+        compiler_params=params(),
+        cost_estimate=cost(
+            2 * many * count * seqs * rows * depth * width, 2 * count * seqs * rows * depth
+        ),
+        name=name,
+    )(gathered_rows, slices, bias)
+
+
+def columns_back_kernel(
+    first, _, row_ref, *refs
+):
+    grad_refs, (slice_ref, mine_out, other_out, dw_ref, bias_ref, weight, total) = (
+        refs[:-7],
+        refs[-7:],
+    )
+    turn, step = pl.program_id(0), pl.program_id(1)
+
+    @pl.when((turn == 0) & (step == 0))
+    def _():
+        take_columns(weight, slice_ref, first)
+        total[...] = jnp.zeros_like(total)
+        bias_ref[...] = jnp.zeros_like(bias_ref)
+
+    depth = weight.shape[0]
+    pieces = []
+    for grad_ref in grad_refs:
+        seqs, rows, width = grad_ref.shape[-3:]
+        for m in range(grad_ref.shape[1] if len(grad_ref.shape) == 5 else 1):
+            piece = grad_ref[0, m] if len(grad_ref.shape) == 5 else grad_ref[0]
+            pieces.append(piece.reshape(seqs * rows, width))
+    gradient = jnp.concatenate(pieces, axis=1)
+    taken = row_ref[0, :, :rows].reshape(seqs * rows, depth)
+    bias_ref[...] += column_sum(gradient.astype(jnp.float32))
+    total[...] += dot(taken, gradient, TN)
+    row_grad = dot(gradient, weight[...], NT).astype(jnp.bfloat16)
+
+    @pl.when(turn == 0)
+    def _():
+        mine_out[0, 0] = row_grad
+
+    @pl.when(turn == 1)
+    def _():
+        other_out[0, 0] = row_grad
+
+    @pl.when((turn == 1) & (step == pl.num_programs(1) - 1))
+    def _():
+        groups, count, all_rows, _ = dw_ref.shape
+        part = depth // (groups * count)
+        for m in range(all_rows // part):
+            dw_ref[:, :, m * part : (m + 1) * part] = (
+                total[:, m * width : (m + 1) * width]
+                .astype(jnp.bfloat16)
+                .reshape(groups, count, part, width)
+            )
+
+
+def project_columns_back(
+    name, order, gathered_rows, block_rows, row_block, rows, gradients, slices, first, many
+):
+    count, seqs, _, depth = gathered_rows.shape
+    half = count // 2
+    groups, _, _, width = slices.shape
+    part = depth // (groups * count)
+
+    def one_device(array):
+        rest = (0,) * (len(array.shape) - 1)
+        return pl.BlockSpec(
+            (1,) + array.shape[1:], lambda p, k, order: (order[p * half + k],) + rest
+        )
+
+    dw_shape = shape((groups, count, many * part, width), jnp.bfloat16)
+    return pl.pallas_call(
+        partial(columns_back_kernel, first),
+        grid_spec=pltpu.PrefetchScalarGridSpec(
+            num_scalar_prefetch=1,
+            grid=(2, half),
+            in_specs=[
+                pl.BlockSpec(
+                    (1, seqs, block_rows, depth),
+                    lambda p, k, order: (order[p * half + k], 0, row_block, 0),
+                ),
+                *[one_device(array) for array in gradients],
+                whole(slices),
+            ],
+            out_specs=[
+                pl.BlockSpec(
+                    (1, 1, seqs * rows, depth),
+                    lambda p, k, _: (jnp.where(p == 0, k, half - 1), 0, 0, 0),
+                ),
+                pl.BlockSpec(
+                    (1, 1, seqs * rows, depth), lambda p, k, _: (jnp.where(p == 0, 0, k), 0, 0, 0)
+                ),
+                whole(dw_shape),
+                pl.BlockSpec((1, many * width), lambda *_: (0, 0)),
+            ],
+            scratch_shapes=[
+                pltpu.VMEM((depth, many * width), jnp.bfloat16),
+                pltpu.VMEM((depth, many * width), jnp.float32),
+            ],
+        ),
+        out_shape=[
+            shape((half, 1, seqs * rows, depth), jnp.bfloat16),
+            shape((half, 1, seqs * rows, depth), jnp.bfloat16),
+            dw_shape,
+            shape((1, many * width), jnp.float32),
+        ],
+        compiler_params=params(),
+        cost_estimate=cost(
+            4 * many * count * seqs * rows * depth * width, 4 * count * seqs * rows * depth
+        ),
+        name=name,
+    )(order, gathered_rows, *gradients, slices)
+
+
+def gathered(weights, width, place):
+    count, groups, rows, _ = weights.shape
+    return pl.BlockSpec((count, groups, rows, width), lambda *_: (0, 0, 0, place))
+
+
+def first_kernel(
+    mixed_ref, x_ref, out_w, query_w, vector_ref, _, mixed_out, in_out, low_out, query_out
+):
+    mixed = join(mixed_ref)
+    mixed_out[...] = mixed
+    first_in = x_ref[...].astype(jnp.float32) + times(mixed, out_w) + vector_ref[2:3]
+    in_out[...] = first_in
+    unit, _ = norm_parts(first_in)
+    low = (unit * vector_ref[11:12] + vector_ref[12:13]).astype(jnp.bfloat16)
+    low_out[...] = low
+    spread(query_out, (times(low, query_w) + vector_ref[3:4]).astype(jnp.bfloat16))
+
+
+def first_forward(mixed, x_rows, weights, vectors, after):
+    rows, depth = x_rows.shape
+    return pl.pallas_call(
+        first_kernel,
+        grid=(1,),
+        in_specs=[
+            whole(mixed),
+            whole(x_rows),
+            gathered(weights, depth, 0),
+            gathered(weights, depth, 1),
+            whole(vectors),
+            pl.BlockSpec(memory_space=pl.ANY),
+        ],
+        out_specs=[whole(x_rows), whole(x_rows), whole(x_rows), whole(mixed)],
+        out_shape=[
+            shape((rows, depth), jnp.bfloat16),
+            shape((rows, depth), jnp.float32),
+            shape((rows, depth), jnp.bfloat16),
+            shape(mixed.shape, jnp.bfloat16),
+        ],
+        compiler_params=params(),
+        cost_estimate=cost(4 * rows * depth * depth, 4 * depth * depth),
+        name="first_forward",
+    )(mixed, x_rows, weights, weights, vectors, after)
+
+
+def ffn_kernel(
+    order,
+    places,
+    mixed_ref,
+    first_ref,
+    out_w,
+    vector_ref,
+    bias_ref,
+    grad_ref,
+    wide_ref,
+    mine_ref,
+    other_ref,
+    mixed_out,
+    layer_out,
+    wide_grad,
+    mine_grad,
+    other_grad,
+    dbias_ref,
+    second_grad,
+    cross_low,
+    mixed_grad,
+    stat_out,
+    columns,
+    contracts,
+    active,
+    slope,
+    low,
+    third_low,
+    second_in,
+    total,
+    wide_sem,
+    contract_sem,
+):
+    blocks, count, groups, rows, block = columns.shape
+    part = block // CHIPS
+    depth = vector_ref.shape[1]
+
+    def wide_copies(t, array, outward):
+        result = []
+        for k in range(CHIPS):
+            column = pl.multiple_of(order[t % 2 * CHIPS + k] * part, part)
+            row = pl.multiple_of(places[t // 2] * rows, rows)
+            there = array.at[:, :, pl.ds(row, rows), pl.ds(column, part)]
+            here = columns.at[t, :, :, :, pl.ds(k * part, part)]
+            ends = (here, there) if outward else (there, here)
+            result.append(pltpu.make_async_copy(*ends, wide_sem.at[t, k]))
+        return result
+
+    def contract_copy(t, mine, other, outward):
+        there = (mine, other)[t % 2].at[t // 2]
+        here = contracts.at[t]
+        ends = (here, there) if outward else (there, here)
+        return pltpu.make_async_copy(*ends, contract_sem.at[t])
+
+    for t in range(blocks):
+        for copy in wide_copies(t, wide_ref, False):
+            copy.start()
+        contract_copy(t, mine_ref, other_ref, False).start()
+
+    mixed = join(mixed_ref)
+    mixed_out[...] = mixed
+    unit, _ = norm_parts(first_ref[...])
+    second_in[...] = (
+        unit * vector_ref[11:12] + vector_ref[12:13] + times(mixed, out_w) + vector_ref[5:6]
+    )
+    unit, _ = norm_parts(second_in[...])
+    second = unit * vector_ref[13:14] + vector_ref[14:15]
+    low[...] = second.astype(jnp.bfloat16)
+    total[...] = second + vector_ref[10:11]
+
+    def shard(t, k):
+        return places[t // 2] * count + order[t % 2 * CHIPS + k]
+
+    for t in range(blocks):
+        for copy in wide_copies(t, wide_ref, False):
+            copy.wait()
+        bias = jnp.concatenate([bias_ref[pl.ds(shard(t, k), 1)] for k in range(CHIPS)], axis=1)
+        inner = times(low[...], columns.at[t]) + bias
+        phi = 0.5 + 0.5 * lax.erf(inner * (0.5**0.5))
+        out = (inner * phi).astype(jnp.bfloat16)
+        active[t] = out
+        slope[t] = phi + inner * jnp.exp(-0.5 * inner * inner) * 0.3989422804014327
+        contract_copy(t, mine_ref, other_ref, False).wait()
+        total[...] += dot(out, contracts[t].reshape(block, depth), NN)
+
+    unit, inverse = norm_parts(total[...])
+    gain = vector_ref[15:16]
+    layer_out[...] = (unit * gain + vector_ref[16:17]).astype(jnp.bfloat16)
+    gradient = grad_ref[...].astype(jnp.float32)
+    grad_third = norm_back(gradient, unit, inverse, gain)
+    stat_out[...] = jnp.zeros_like(stat_out)
+    stat_out[0:1] = column_sum(grad_third)
+    stat_out[1:2] = column_sum(gradient * unit)
+    stat_out[2:3] = column_sum(gradient)
+    total[...] = grad_third
+    third_low[...] = grad_third.astype(jnp.bfloat16)
+    turned = low[...].T
+
+    for t in range(blocks):
+        grad_inner = dot(third_low[...], contracts[t].reshape(block, depth), NT) * slope[t]
+        inner_low = grad_inner.astype(jnp.bfloat16)
+        sums = column_sum(grad_inner)
+        for k in range(CHIPS):
+            dbias_ref[pl.ds(shard(t, k), 1)] = sums[:, k * part : (k + 1) * part]
+        contracts[t] = (
+            dot(active[t], third_low[...], TN).astype(jnp.bfloat16).reshape(CHIPS, part, depth)
+        )
+        contract_copy(t, mine_grad, other_grad, True).start()
+        total[...] += times_back(inner_low, columns.at[t])
+        result = dot(turned, inner_low, NN).astype(jnp.bfloat16)
+        for d in range(groups):
+            columns[t, :, d] = result[d * count * rows : (d + 1) * count * rows].reshape(
+                count, rows, block
+            )
+        for copy in wide_copies(t, wide_grad, True):
+            copy.start()
+
+    unit, inverse = norm_parts(second_in[...])
+    grad_second = total[...]
+    grad_in = norm_back(grad_second, unit, inverse, vector_ref[13:14])
+    second_grad[...] = grad_in
+    grad_low = grad_in.astype(jnp.bfloat16)
+    cross_low[...] = grad_low
+    spread(mixed_grad, times_back(grad_low, out_w).astype(jnp.bfloat16))
+    stat_out[8:9] = column_sum(grad_in)
+    stat_out[9:10] = column_sum(grad_second * unit)
+    stat_out[10:11] = column_sum(grad_second)
+    for t in range(blocks):
+        contract_copy(t, mine_grad, other_grad, True).wait()
+        for copy in wide_copies(t, wide_grad, True):
+            copy.wait()
+
+
+def ffn(orders, mixed, first_in, wide, contract, vectors, bias, output_grad):
+    rows, depth = first_in.shape
+    hidden = bias.size
+    block = depth // 2
+    count, groups, all_rows, _ = wide.shape
+    part = depth // (count * groups)
+    blocks = hidden // block
+    full = whole(first_in)
+    anywhere = pl.BlockSpec(memory_space=pl.ANY)
+    heads_out = shape(mixed.shape, jnp.bfloat16)
+    stats = shape((16, depth), jnp.float32)
+    return pl.pallas_call(
+        ffn_kernel,
+        grid_spec=pltpu.PrefetchScalarGridSpec(
+            num_scalar_prefetch=2,
+            grid=(1,),
+            in_specs=[
+                whole(mixed),
+                full,
+                pl.BlockSpec((count, groups, part, depth), lambda *_: (0, 0, groups, 0)),
+                whole(vectors),
+                whole(bias),
+                full,
+                anywhere,
+                anywhere,
+                anywhere,
+            ],
+            out_specs=[
+                full,
+                full,
+                anywhere,
+                anywhere,
+                anywhere,
+                whole(bias),
+                full,
+                full,
+                whole(heads_out),
+                whole(stats),
+            ],
+            scratch_shapes=[
+                pltpu.VMEM((blocks, count, groups, part, block), jnp.bfloat16),
+                pltpu.VMEM((blocks,) + contract[0].shape[1:], jnp.bfloat16),
+                pltpu.VMEM((blocks, rows, block), jnp.bfloat16),
+                pltpu.VMEM((blocks, rows, block), jnp.float32),
+                pltpu.VMEM((rows, depth), jnp.bfloat16),
+                pltpu.VMEM((rows, depth), jnp.bfloat16),
+                pltpu.VMEM((rows, depth), jnp.float32),
+                pltpu.VMEM((rows, depth), jnp.float32),
+                pltpu.SemaphoreType.DMA((blocks, CHIPS)),
+                pltpu.SemaphoreType.DMA((blocks,)),
+            ],
+        ),
+        out_shape=[
+            shape((rows, depth), jnp.bfloat16),
+            shape((rows, depth), jnp.bfloat16),
+            shape((count, groups, all_rows - part, depth), jnp.bfloat16),
+            shape(contract[0].shape, jnp.bfloat16),
+            shape(contract[0].shape, jnp.bfloat16),
+            shape(bias.shape, jnp.float32),
+            shape((rows, depth), jnp.float32),
+            shape((rows, depth), jnp.bfloat16),
+            heads_out,
+            stats,
+        ],
+        compiler_params=params(),
+        cost_estimate=cost(12 * rows * depth * hidden, 16 * depth * hidden),
+        name="ffn",
+    )(*orders, mixed, first_in, wide, vectors, bias, output_grad, wide, *contract)
+
+
+def first_back_kernel(
+    dq_ref,
+    second_grad,
+    first_ref,
+    out_w,
+    query_w,
+    vector_ref,
+    _,
+    query_low,
+    grad_in_out,
+    self_low,
+    mixed_grad,
+    stat_out,
+):
+    query_grad = join(dq_ref)
+    query_low[...] = query_grad
+    grad_first = second_grad[...] + times_back(query_grad, query_w)
+    unit, inverse = norm_parts(first_ref[...])
+    grad_in = norm_back(grad_first, unit, inverse, vector_ref[11:12])
+    grad_in_out[...] = grad_in
+    grad_low = grad_in.astype(jnp.bfloat16)
+    self_low[...] = grad_low
+    spread(mixed_grad, times_back(grad_low, out_w).astype(jnp.bfloat16))
+    stat_out[...] = jnp.zeros_like(stat_out)
+    stat_out[0:1] = column_sum(query_grad.astype(jnp.float32))
+    stat_out[1:2] = column_sum(grad_in)
+    stat_out[2:3] = column_sum(grad_first * unit)
+    stat_out[3:4] = column_sum(grad_first)
+
+
+def first_back(dq, second_grad, first_in, weights, vectors, after):
+    rows, depth = first_in.shape
+    full = whole(first_in)
+    return pl.pallas_call(
+        first_back_kernel,
+        grid=(1,),
+        in_specs=[
+            whole(dq),
+            full,
+            full,
+            gathered(weights, depth, 0),
+            gathered(weights, depth, 1),
+            whole(vectors),
+            pl.BlockSpec(memory_space=pl.ANY),
+        ],
+        out_specs=[full, full, full, whole(dq), pl.BlockSpec((8, depth), lambda *_: (0, 0))],
+        out_shape=[
+            shape((rows, depth), jnp.bfloat16),
+            shape((rows, depth), jnp.float32),
+            shape((rows, depth), jnp.bfloat16),
+            shape(dq.shape, jnp.bfloat16),
+            shape((8, depth), jnp.float32),
+        ],
+        compiler_params=params(),
+        cost_estimate=cost(4 * rows * depth * depth, 4 * depth * depth),
+        name="first_back",
+    )(dq, second_grad, first_in, weights, weights, vectors, after)
+
+
+def weight_grads_kernel(
+    order,
+    mixed,
+    self_low,
+    first_low,
+    query_low,
+    cross,
+    cross_low,
+    mine_out,
+    other_out,
+    result,
+):
+    step = pl.program_id(0)
+    pairs = ((mixed, self_low), (first_low, query_low), (cross, cross_low))
+    half, groups, part, _ = mine_out.shape
+    for m, (left_side, gradient) in enumerate(pairs):
+
+        @pl.when(step == m)
+        def _(left_side=left_side, gradient=gradient):
+            result[...] = dot(left_side[...], gradient[...], TN).astype(jnp.bfloat16)
+
+    for d in range(groups):
+        for k in range(half):
+            for p, out_ref in enumerate((mine_out, other_out)):
+                row = pl.multiple_of((2 * half * d + order[p * half + k]) * part, part)
+                out_ref[k, d] = result[pl.ds(row, part)]
+
+
+def weight_grads(dims, order, mixed, self_low, first_low, query_low, cross, cross_low):
+    count, groups, part, depth = dims
+    half = pl.BlockSpec((count // 2, groups, part, depth), lambda m, _: (0, 0, m, 0))
+    return pl.pallas_call(
+        weight_grads_kernel,
+        grid_spec=pltpu.PrefetchScalarGridSpec(
+            num_scalar_prefetch=1,
+            grid=(3,),
+            in_specs=[whole(mixed)] * 6,
+            out_specs=[half, half],
+            scratch_shapes=[pltpu.VMEM((depth, depth), jnp.bfloat16)],
+        ),
+        out_shape=[shape((count // 2, groups, 3 * part, depth), jnp.bfloat16)] * 2,
+        compiler_params=params(),
+        cost_estimate=cost(6 * mixed.shape[0] * depth * depth, 6 * depth * depth),
+        name="weight_grads",
+    )(order, mixed, self_low, first_low, query_low, cross, cross_low)
+
+
+def send_dp(piece):
+    size = lax.axis_size("dp")
+    return [
+        lax.ppermute(piece, "dp", [(i, (i + shift) % size) for i in range(size)])
+        for shift in range(1, size)
+    ]
+
+
+def place_dp(piece, arrived):
+    size, me = lax.axis_size("dp"), lax.axis_index("dp")
+    result = jnp.zeros((size,) + piece.shape, piece.dtype)
+    result = lax.dynamic_update_index_in_dim(result, piece, me, 0)
+    for shift, got in enumerate(arrived, 1):
+        result = lax.dynamic_update_index_in_dim(result, got, lax.rem(me - shift + size, size), 0)
+    return result
+
+
+class HalvingDp:
+    def __init__(self, pieces):
+        me = lax.axis_index("dp")
+        self.parts = [
+            lax.dynamic_index_in_dim(pieces, me ^ flip, 0, keepdims=False) for flip in DP_ORDER
+        ]
+
+    def first(self):
+        return jnp.stack(self.parts[2:]).astype(jnp.bfloat16)
+
+    def second(self, sent):
+        self.got = exchange_dp(sent, 1)
+        return low_sum(self.parts[1], self.got[1])
+
+    def finish(self, sent):
+        last = exchange_dp(sent, 2)
+        return sum(
+            one.astype(jnp.float32) for one in (self.parts[0], self.got[0], last)
+        )
+
+
+def sum_dp(pieces):
+    halves = HalvingDp(pieces)
+    return halves.finish(halves.second(halves.first()))
+
+
+def relative_order():
+    size, me = lax.axis_size("index"), lax.axis_index("index")
+    steps = jnp.arange(size // 2, dtype=jnp.int32) * 2
+    return jnp.concatenate([me ^ steps, me ^ 1 ^ steps])
+
+
+def exchange(piece, flip):
+    size = lax.axis_size("index")
+    return lax.ppermute(piece, "index", [(i, i ^ flip) for i in range(size)])
+
+
+def exchange_dp(piece, flip):
+    size = lax.axis_size("dp")
+    return lax.ppermute(piece, "dp", [(i, i ^ flip) for i in range(size)])
+
+
+def low_sum(*parts):
+    return sum(part.astype(jnp.float32) for part in parts).astype(jnp.bfloat16)
+
+
+class Halving:
+    def __init__(self, mine, other):
+        self.pair = (mine, exchange(other, 1))
+        middle = mine.shape[2] // 2
+        self.top, self.low = slice(0, middle), slice(middle, None)
+
+    def total(self, k, rows, *more):
+        result = sum(one[k, :, rows].astype(jnp.float32) for one in self.pair)
+        return sum((one.astype(jnp.float32) for one in more), result)
+
+    def first(self):
+        return [
+            jnp.stack([self.total(k, rows) for k in blocks]).astype(jnp.bfloat16)
+            for blocks, rows in (((1, 3), self.top), ((2, 3), self.low))
+        ]
+
+    def send(self, sent):
+        return [exchange(sent[0], 2), exchange(sent[1], 4)]
+
+    def second(self, got):
+        self.got = got
+        return [
+            self.total(2, self.top, self.got[0][1]).astype(jnp.bfloat16),
+            self.total(1, self.low, self.got[1][1]).astype(jnp.bfloat16),
+        ]
+
+    def finish(self, sent):
+        last = exchange(sent[0], 4), exchange(sent[1], 2)
+        return jnp.concatenate(
+            [
+                self.total(0, self.top, self.got[0][0], last[0]),
+                self.total(0, self.low, self.got[1][0], last[1]),
+            ],
+            axis=1,
+        )
+
+
+def small_sum(values):
+    size = lax.axis_size("index")
+    flat = jnp.pad(values.reshape(-1), (0, 1024 - values.size)).reshape(1, 8, 128)
+    arrived = swap(jnp.broadcast_to(flat, (size, 8, 128)))
+    return jnp.sum(arrived, axis=0).reshape(-1)[: values.size].reshape(values.shape)
+
+
+def hold_kernel(*_):
+    pass
+
+
+def hold(values, *others):
+    anywhere = pl.BlockSpec(memory_space=pl.ANY)
+    return pl.pallas_call(
+        hold_kernel,
+        in_specs=[anywhere] * (len(values) + len(others)),
+        out_specs=[anywhere] * len(values),
+        out_shape=[shape(value.shape, value.dtype) for value in values],
+        input_output_aliases={i: i for i in range(len(values))},
+        name="hold",
+    )(*values, *others)
+
+
+def swap(pieces):
+    return lax.all_to_all(pieces, "index", 0, 0, tiled=True)
+
+
+def head_body(
+    decoder_input,
+    encoder_memory,
+    question_vectors,
+    passage_vectors,
+    passage_ids,
+    valid_count,
+    output_grad,
+    attention_weight,
+    expand_weight,
+    contract_weight,
+    vector_params,
+    attention_mean,
+    attention_square,
+    expand_mean,
+    expand_square,
+    contract_mean,
+    contract_square,
+    vector_mean,
+    vector_square,
+):
+    low = jnp.bfloat16
+    count, groups = lax.axis_size("index"), lax.axis_size("dp")
+    place = lax.axis_index("index")
+    seqs, rows_here, depth = decoder_input.shape
+    memory_here = encoder_memory.shape[1]
+    width = depth // count
+    part = attention_weight.shape[1]
+    hidden = expand_weight.shape[1]
+    vector_rows, vector_width = vector_params.shape
+    question_width = question_vectors.shape[1]
+    rows = seqs * rows_here
+
+    attention_low = attention_weight.astype(low)
+    extras = jnp.concatenate(
+        [vector_params.astype(low).reshape(-1), question_vectors.reshape(-1)]
+    )
+    extra_rows = -(-extras.shape[0] // (16 * width)) * 16
+    extras = jnp.pad(extras, (0, extra_rows * width - extras.shape[0])).reshape(
+        1, extra_rows, width
+    )
+    split = jnp.concatenate([attention_low[:3], attention_low[5:7]], axis=0)
+    columns = split.reshape(5, part, count, width).transpose(2, 0, 1, 3)
+    package = jnp.concatenate(
+        [
+            columns.reshape(count, 5 * part, width),
+            jnp.broadcast_to(extras, (count, extra_rows, width)),
+        ],
+        axis=1,
+    )
+    order = relative_order()
+    memory_block = -(-memory_here // rows_here) * rows_here
+    rows_all = lax.all_gather(
+        jnp.concatenate(
+            [
+                jnp.pad(encoder_memory, ((0, 0), (0, memory_block - memory_here), (0, 0))),
+                decoder_input,
+            ],
+            axis=1,
+        ),
+        "index",
+        axis=0,
+        tiled=False,
+    )
+    input_rows = (rows_all, rows_here, memory_block // rows_here, rows_here)
+    memory_rows = (rows_all, memory_block, 0, memory_here)
+    square = attention_low[3:5].transpose(1, 0, 2).reshape(part, 2 * depth)
+    received = swap(package)
+    arrived = hold(send_dp(square), received)
+    (received,) = hold([received], *arrived)
+    square = lax.all_gather(place_dp(square, arrived), "index", axis=0, tiled=False)
+    received_sent = send_dp(received)
+    (contract,) = hold([contract_weight.astype(low)], received)
+    contract = jnp.stack([contract] + [exchange(contract, 2 * k) for k in range(1, CHIPS)])
+    slices = place_dp(received, hold(received_sent, contract))
+    vectors = (
+        slices[:, :, 5 * part :]
+        .reshape(groups, count, extra_rows * width)[:, :, : vector_rows * vector_width]
+        .reshape(groups, count, vector_rows, vector_width)
+        .transpose(2, 0, 1, 3)
+        .reshape(vector_rows, depth)
+        .astype(jnp.float32)
+    )
+    question_full = (
+        received[:, 5 * part :]
+        .reshape(count, extra_rows * width)[:, vector_rows * vector_width :][
+            :, : seqs * question_width
+        ]
+        .reshape(count, seqs, question_width)
+        .transpose(1, 0, 2)
+        .reshape(seqs, count * question_width)
+    )
+    expand_part = hidden // depth * part
+    late = jnp.concatenate(
+        [
+            expand_weight.astype(low)
+            .reshape(part, hidden // depth, depth)
+            .transpose(1, 0, 2)
+            .reshape(expand_part, depth),
+            attention_low[7],
+        ],
+        axis=0,
+    )
+    (late,) = hold([late], slices)
+    across = exchange_dp(jnp.concatenate([late, contract.reshape(-1, depth)], axis=0), 2)
+    late_arrived = send_dp(late)
+    late_arrived[1] = across
+
+    passages_here = passage_vectors.shape[0]
+    local_ids = passage_ids - place * passages_here
+    owned_slot = (local_ids >= 0) & (local_ids < passages_here)
+    picked = passage_vectors[jnp.clip(local_ids, 0, passages_here - 1)]
+    local_scores = jnp.einsum(
+        "sc,skc->sk", question_full, picked, preferred_element_type=jnp.float32
+    )
+    slots = passage_ids.shape[1]
+    usable = jnp.arange(slots)[None, :] < valid_count[:, None]
+    scores = small_sum(jnp.where(owned_slot, local_scores, 0.0))
+    masked = jnp.where(usable, scores, negative_fill)
+    maximum = jnp.max(masked, axis=1)
+    exponent = jnp.where(usable, jnp.exp(masked - maximum[:, None]), 0.0)
+    partition = jnp.sum(exponent, axis=1)
+    passage_prob = exponent / partition[:, None]
+    log_prior = jnp.where(
+        usable, masked - maximum[:, None] - jnp.log(partition)[:, None], negative_fill
+    )
+    key_bias = jnp.repeat(log_prior, MEM_P, axis=1)
+
+    vector_here = lax.dynamic_slice_in_dim(vectors[:5], place * width, width, axis=1)
+    no_bias = jnp.zeros((1, width), jnp.float32)
+    qkv_bias = jnp.concatenate([vector_here[0:1], no_bias, vector_here[1:2]], axis=1)
+    kv_bias = jnp.concatenate([no_bias, vector_here[4:5]], axis=1)
+    x_rows = decoder_input.reshape(rows, depth)
+    qkv = project_columns("self_qkv", *input_rows, slices, 0, 3, qkv_bias)
+    self_out, self_stat = attend(True, qkv, 0, qkv, 1, 2, key_bias[:, None, :])
+    self_got = swap(self_out)
+    memory_kv = project_columns("memory_kv", *memory_rows, slices, 3, 2, kv_bias)
+    late_arrived = list(hold(late_arrived, self_got))
+    across = late_arrived[1][late.shape[0] :]
+    late_arrived[1] = late_arrived[1][: late.shape[0]]
+    contract = jnp.stack([contract, across.reshape(contract.shape)])
+    late = place_dp(late, late_arrived)
+    late = lax.all_gather(late, "index", axis=0, tiled=False)
+    (self_got,) = hold([self_got], contract)
+    contract_far = exchange_dp(contract, 1)
+    self_mixed, first_in, first_low, cross_query = first_forward(
+        self_got, x_rows, square, vectors, memory_kv
+    )
+    cross_query = swap(cross_query)[:, None]
+    cross_out, cross_stat = attend(
+        False, cross_query, 0, memory_kv, 0, 1, key_bias[:, None, :]
+    )
+    contract = jnp.concatenate([contract, *hold([contract_far], cross_out)], axis=0)
+    places = lax.axis_index("dp") ^ jnp.array(DP_ORDER, jnp.int32)
+    (
+        cross_mixed,
+        layer_output,
+        wide_grad,
+        contract_mine,
+        contract_other,
+        inner_total,
+        second_grad,
+        cross_low,
+        cross_mix_grad,
+        stats,
+    ) = ffn(
+        (order, places),
+        swap(cross_out),
+        first_in,
+        late,
+        (contract, exchange(contract, 1)),
+        vectors,
+        vectors[6:10].reshape(groups * count, -1),
+        output_grad.reshape(rows, depth),
+    )
+    third_stat, second_stat = stats[:8], stats[8:]
+
+    expand_part_sum = lax.psum_scatter(wide_grad, "index", scatter_dimension=0, tiled=False)
+    contract_pair = (contract_mine, exchange(contract_other, 1))
+    contract_sent = low_sum(*(one[2:] for one in contract_pair))
+    cross_mix_got, contract_sent = hold([swap(cross_mix_grad), contract_sent])
+    contract_got = exchange_dp(contract_sent, 1)
+    contract_next = low_sum(*(one[1] for one in contract_pair), contract_got[1])
+    cross_dq, cross_dkv, prior_rows = attend_back(
+        False,
+        cross_query,
+        0,
+        memory_kv,
+        0,
+        1,
+        cross_mix_got,
+        cross_stat,
+        key_bias[:, :, None],
+        contract_sent,
+    )
+    memory_mine, memory_other, kv_grads, kv_total = project_columns_back(
+        "memory_kv_back", order, *memory_rows, [cross_dkv], slices, 3, 2
+    )
+    cross_dq_got, contract_next = hold([swap(cross_dq), contract_next], memory_mine)
+    contract_last = exchange_dp(contract_next, 2)
+    query_low, first_grad, self_low, self_mix_grad, first_stat = first_back(
+        cross_dq_got, second_grad, first_in, square, vectors, memory_mine
+    )
+    memory_sum = Halving(memory_mine, memory_other)
+    memory_sent = memory_sum.first()
+    square_mine, square_other = weight_grads(
+        (count, groups, part, depth),
+        order,
+        self_mixed,
+        self_low,
+        first_low,
+        query_low,
+        cross_mixed,
+        cross_low,
+    )
+    square_sum = Halving(square_mine, square_other)
+    (self_mix_got,) = hold([swap(self_mix_grad)], *memory_sent)
+    self_dq, self_dkv, _ = attend_back(
+        True, qkv, 0, qkv, 1, 2, self_mix_got, self_stat, self_stat, square_mine
+    )
+    square_sent = square_sum.first()
+    self_dq, expand_part_sum = hold([self_dq, expand_part_sum], *square_sent)
+    dx_mine, dx_other, qkv_slice_grads, qkv_total = project_columns_back(
+        "self_qkv_back", order, *input_rows, [self_dq, self_dkv], slices, 0, 3
+    )
+    own = jnp.concatenate(
+        [qkv_total[:, :width], qkv_total[:, 2 * width :], kv_total[:, width:]], axis=0
+    )
+    own = lax.dynamic_update_slice(
+        jnp.zeros((3, depth), jnp.float32), own, (jnp.int32(0), place * width)
+    )
+    vector_grads = jnp.concatenate(
+        [
+            own[:2],
+            first_stat[1:2],
+            first_stat[0:1],
+            own[2:],
+            second_stat[0:1],
+            inner_total.reshape(hidden // depth, depth),
+            third_stat[0:1],
+            first_stat[2:4],
+            second_stat[1:3],
+            third_stat[1:3],
+        ],
+        axis=0,
+    )
+    vector_size = vector_rows * vector_width
+    question_size = seqs * question_width
+    vector_send = (
+        vector_grads.reshape(vector_rows, groups, count, vector_width)
+        .transpose(1, 2, 0, 3)
+        .reshape(groups, count, vector_size)
+    )
+    vector_send = jnp.pad(
+        vector_send, ((0, 0), (0, 0), (0, extra_rows * width - vector_size))
+    ).reshape(groups, count, extra_rows, width)
+    slice_sum = HalvingDp(
+        jnp.concatenate([qkv_slice_grads, kv_grads, vector_send.astype(low)], axis=2)
+    )
+    (
+        dx_mine,
+        dx_other,
+        slice_sent,
+        expand_part_sum,
+        contract_last,
+        memory_top,
+        memory_low,
+        square_top,
+        square_low,
+    ) = hold(
+        [
+            dx_mine,
+            dx_other,
+            slice_sum.first(),
+            expand_part_sum,
+            contract_last,
+            *memory_sum.send(memory_sent),
+            *square_sum.send(square_sent),
+        ]
+    )
+    square_last = square_sum.second([square_top, square_low])
+    memory_last = memory_sum.second([memory_top, memory_low])
+    expand_sum = HalvingDp(expand_part_sum)
+    expand_sent = expand_sum.first()
+    dx_sum = Halving(dx_mine, dx_other)
+    dx_sent = dx_sum.first()
+    dx_last = dx_sum.second(dx_sum.send(dx_sent))
+    memory_last = hold(memory_last, *dx_sent)
+    memory_gradient = memory_sum.finish(memory_last).reshape(encoder_memory.shape)
+    contract_four = low_sum(*(one[0] for one in contract_pair), contract_got[0], contract_last)
+    (contract_four,) = hold([contract_four], *dx_sent)
+    contract_sum = sum(
+        (exchange(contract_four[k], 2 * k).astype(jnp.float32) for k in range(1, CHIPS)),
+        contract_four[0].astype(jnp.float32),
+    )
+    square_part = square_sum.finish(square_last).astype(low)
+    input_gradient = first_grad + dx_sum.finish(dx_last).reshape(rows, depth)
+
+    prior_part = prior_rows.reshape(seqs, slots, MEM_P).sum(axis=-1)
+    prior_grad = jnp.where(usable, small_sum(prior_part), 0.0)
+    score_doc = jnp.where(
+        usable, prior_grad - passage_prob * jnp.sum(prior_grad, axis=1, keepdims=True), 0.0
+    )
+    question_part = jnp.einsum(
+        "sk,skc->sc",
+        jnp.where(owned_slot, score_doc, 0.0),
+        picked.astype(jnp.float32),
+        precision=lax.Precision.HIGHEST,
+    )
+
+    square_far = HalvingDp(square_part)
+    (square_sent,) = hold([square_far.first()], *dx_sent)
+    square_next = square_far.second(square_sent)
+    (slice_next,) = hold([slice_sum.second(slice_sent)], *dx_last)
+    slice_sum = slice_sum.finish(slice_next)
+    question_send = (
+        question_part.reshape(seqs, count, question_width)
+        .transpose(1, 0, 2)
+        .reshape(count, question_size)
+    )
+    question_send = jnp.pad(
+        question_send,
+        ((0, 0), (vector_size, extra_rows * width - vector_size - question_size)),
+    ).reshape(count, extra_rows, width)
+    slice_sum = jnp.concatenate(
+        [slice_sum[:, : 5 * part], slice_sum[:, 5 * part :] + question_send], axis=1
+    )
+    (slice_send,) = hold(
+        [slice_sum.astype(low)], contract_sum, memory_gradient, input_gradient
+    )
+    arrived = swap(slice_send).astype(jnp.float32)
+    split_grads = (
+        arrived[:, : 5 * part]
+        .reshape(count, 5, part, width)
+        .transpose(1, 2, 0, 3)
+        .reshape(5, part, depth)
+    )
+    extra_sum = jnp.sum(arrived[:, 5 * part :].reshape(count, extra_rows * width), axis=0)
+    vector_sum = extra_sum[:vector_size].reshape(vector_rows, vector_width)
+    question_gradient = extra_sum[vector_size : vector_size + question_size].reshape(
+        seqs, question_width
+    )
+
+    expand_sum = (
+        expand_sum.finish(expand_sum.second(expand_sent))
+        .reshape(hidden // depth, part, depth)
+        .transpose(1, 0, 2)
+        .reshape(part, hidden)
+    )
+    square_total = square_far.finish(square_next).reshape(3, part, depth)
+    attention_sum = jnp.concatenate(
+        [split_grads[:3], square_total[:2], split_grads[3:], square_total[2:]], axis=0
+    )
+
+    new_attention = adam_update(
+        attention_weight,
+        attention_mean,
+        attention_square,
+        attention_sum,
+        rate_attention,
+        decay_matrix,
+    )
+    new_expand = adam_update(
+        expand_weight, expand_mean, expand_square, expand_sum, rate_expand, decay_matrix
+    )
+    new_contract = adam_update(
+        contract_weight, contract_mean, contract_square, contract_sum, rate_contract, decay_matrix
+    )
+    new_vector = adam_update(
+        vector_params, vector_mean, vector_square, vector_sum, rate_vector, 0.0
+    )
+    return (
+        layer_output.reshape(decoder_input.shape),
+        input_gradient.reshape(decoder_input.shape),
+        memory_gradient,
+        question_gradient,
+        *new_attention,
+        *new_expand,
+        *new_contract,
+        *new_vector,
+    )
+
+
+def body(sizes, *arrays):
+    depth = arrays[0].shape[2]
+    if sizes == (4, 8) and depth // 8 % 128 == 0:
+        return head_body(*arrays)
+    return general_body(*arrays)
+
+
 def solution(mesh):
     return jax.shard_map(
-        body,
+        partial(body, (mesh.shape["dp"], mesh.shape["index"])),
         mesh=mesh,
         in_specs=(
             P("dp", "index", None),

time: 1780 us -> 558 us (0.31)
  waiting for transfers between devices: 1150 us -> 136 us
  matrix products: 284 us -> 0.27 us
  Pallas kernels: 0 us -> 159 us
  local copies, waits for them, and re-layouts: 154 us -> 53.6 us
  starting transfers between devices: 0.67 us -> 91.1 us
  blocking collectives: 92 us -> 14.5 us
    reduce_scatter x5 -> x1, waiting for transfers between devices: 777 us -> 0.01 us  [head_body(): lax.psum_scatter(wide_grad, 'index', scatter_dimension=0, tiled=False)]
    dot_general x42 -> x2, matrix products: 254 us -> 0.27 us  [the longest x1 0.14 us: head_body(): jnp.einsum('sk,skc->sc', jnp.where(owned_slot, score_doc, 0.0), picked.as...]
    all_gather x7 -> x3, waiting for transfers between devices: 243 us -> 2.3 us  [the longest x1 2.3 us: head_body(): lax.all_gather(jnp.concatenate([jnp.pad(encoder_memory, ((0, 0), (0, memo...]
    pallas_call x0 -> x30, Pallas kernels: none -> 159 us  [the longest x2 41.9 us: attend_back(): pl.pallas_call(partial(attend_backward_kernel, causal, head_width), grid=...]
    unnamed x20 -> x4, waiting for transfers between devices: 130 us -> 0.07 us
    ppermute x0 -> x41, waiting for transfers between devices: none -> 100 us  [the longest x8 54.8 us: send_dp(): lax.ppermute(piece, 'dp', [(i, (i + shift) % size) for i in range(size)])]
    ppermute x0 -> x41, starting transfers between devices: none -> 57 us  [the longest x23 20.5 us: exchange(): return lax.ppermute(piece, 'index', [(i, i ^ flip) for i in range(size)])]
    all_gather x2 -> x0, blocking collectives: 53 us -> none  [the longest x1 44.4 us: body(): lax.all_gather(vector_params.astype(jnp.bfloat16), ('dp', 'index'), axis=...]
  transfers between devices with their start and end apart: 16 -> 54, of which waited for: 12 -> 22; matrix products, arithmetic and copies ran while one was open for 21% -> 19% of each run, Pallas kernels for 0% -> 24%
where the time goes in v1:
time: 558 us; the launch traced here: 548 us
  Pallas kernels  159 us (28%)
  waiting for transfers between devices  136 us (24%)
  starting transfers between devices  91.1 us (16%)
  other arithmetic  77.4 us (14%)
  local copies, waits for them, and re-layouts  53.6 us (10%)
  between operations  15.5 us (3%)
  blocking collectives  14.5 us (3%)
    ppermute x8, waiting for transfers between devices, send_dp(): lax.ppermute(piece, 'dp', [(i, (i + shift) % size) for i in range(size)])  54.8 us
    pallas_call x2, Pallas kernels, attend_back(): pl.pallas_call(partial(attend_backward_kernel, causal, head_width), grid=...  41.9 us
    all_to_all x9, starting transfers between devices, swap(): return lax.all_to_all(pieces, 'index', 0, 0, tiled=True)  33.8 us
    all_to_all x9, waiting for transfers between devices, swap(): return lax.all_to_all(pieces, 'index', 0, 0, tiled=True)  33.8 us
    pallas_call x2, Pallas kernels, attend(): pl.pallas_call(partial(attend_forward_kernel, causal, head_width), grid=(...  29.7 us
    ppermute x10, waiting for transfers between devices, exchange_dp(): return lax.ppermute(piece, 'dp', [(i, i ^ flip) for i in range(size)])  26.6 us
    pallas_call x1, Pallas kernels, ffn(): pl.pallas_call(ffn_kernel, grid_spec=pltpu.PrefetchScalarGridSpec(num_sca...  26.3 us
    pallas_call x2, Pallas kernels, project_columns_back(): pl.pallas_call(partial(columns_back_kernel, first), grid_spec=pltpu.Prefe...  25.8 us
  transfers between devices with their start and end apart: 54, of which 22 were waited for; matrix products, arithmetic and copies ran while one was open for 19% of the time, Pallas kernels for 24%

profile of v1, /device:TPU:0, one launch (start us, length us, event | category | flops | bytes accessed | tf_op | source)
XLA Modules:
  0.0 547.9 jit_solution(10875829495750639899)
XLA Ops:
  11.8 5.3 all-to-all-start
  25.4 5.2 collective-permute-done.1.__1_
  36.6 4.2 gather_fusion
  45.7 3.3 collective-permute-start.3
  52.6 3.8 all-to-all-start.1
  56.7 9.3 %all-to-all-done.1 = f32[8,8,128]{2,1,0:T(8,128)S(1)} async-done(((f32[8,8,128]{2,1,0:T(8,128)}), f32[8,8,128]{2,1,0:T(8,128)S(1)}, u32[]{:S(2)}, u32[]{:S(2)}) %all-to-all-start.1) | async-done | bytes 32800 | tf_op jit(solution)/shard_map/all_to_all | solution.py:1309
  66.3 4.9 collective-permute-start.5
  75.5 5.4 collective-permute-done.5.__2_
  94.0 8.2 %self_qkv.1.q_ref.k_ref.v_ref = bf16[8,3,2,128,128]{4,3,2,1,0:T(8,128)(2,1)} custom-call(bf16[8,2,384,1024]{3,2,1,0:T(8,128)(2,1)} %bitcast.194, bf16[4,8,176,128]{3,2,1,0:T(8,128)(2,1)} %copy-done, f32[1,384]{1,0:T(1,128)} %fusion.31.bias_ref), custom_call_target="tpu_custom_call" | custom-call | flops 100663296 | bytes 262144 | tf_op jit(solution)/shard_map/self_qkv/pallas_call | solution.py:707
  102.1 10.2 %attend_self.1 = (bf16[8,2,128,128]{3,2,1,0:T(8,128)(2,1)}, f32[2,2,1024]{2,1,0:T(2,128)}) custom-call(bf16[8,3,2,128,128]{4,3,2,1,0:T(8,128)(2,1)} %self_qkv.1.q_ref.k_ref.v_ref, bf16[8,3,2,128,128]{4,3,2,1,0:T(8,128)(2,1)} %self_qkv.1.q_ref.k_ref.v_ref, bf16[8,3,2,128,128]{4,3,2,1,0:T(8,128)(2,1)} %self_qkv.1.q_ref.k_ref.v_ref, ...), custom_call_target="tpu_custom_call" | custom-call | flops 268435456 | bytes 131072 | tf_op jit(solution)/shard_map/attend_self/pallas_call | solution.py:604
  112.3 3.5 all-to-all-start.2
  115.9 3.8 collective-permute-start.11
  122.1 41.8 %collective-permute-done.11.__2_ = bf16[160,1024]{1,0:T(8,128)(2,1)S(1)} collective-permute-done((bf16[160,1024]{1,0:T(8,128)(2,1)S(1)}, bf16[160,1024]{1,0:T(8,128)(2,1)S(1)}, u32[]{:S(2)}, u32[]{:S(2)}) %collective-permute-start.11) | collective-permute-done | bytes 327712 | tf_op jit(solution)/shard_map/ppermute | solution.py:1188
  175.6 9.3 %memory_kv.1._.k_ref.v_ref = bf16[8,2,2,240,128]{4,3,2,1,0:T(8,128)(2,1)} custom-call(bf16[8,2,384,1024]{3,2,1,0:T(8,128)(2,1)} %bitcast.195, bf16[4,8,176,128]{3,2,1,0:T(8,128)(2,1)} %copy-done, f32[1,256]{1,0:T(1,128)} %concatenate.123.bias_ref), custom_call_target="tpu_custom_call" | custom-call | flops 125829120 | bytes 491520 | tf_op jit(solution)/shard_map/memory_kv/pallas_call | solution.py:707
  184.9 5.0 first_forward.1
  189.9 14.5 %all_to_all.50 = bf16[8,2,128,128]{3,2,1,0:T(8,128)(2,1)} all-to-all(bf16[8,2,128,128]{3,2,1,0:T(8,128)(2,1)} %get-tuple-element.88), channel_id=1, replica_groups=mesh['dp'=4,'index'=8] {'index'}, dimensions={0} | all-to-all | bytes 1048576 | tf_op jit(solution)/shard_map/all_to_all | solution.py:1309
  204.4 19.6 %attend_memory.1 = (bf16[8,2,128,128]{3,2,1,0:T(8,128)(2,1)}, f32[2,2,1024]{2,1,0:T(2,128)}) custom-call(bf16[8,1,2,128,128]{4,3,2,1,0:T(8,128)(2,1)} %bitcast.204, bf16[8,2,2,240,128]{4,3,2,1,0:T(8,128)(2,1)} %memory_kv.1._.k_ref.v_ref, bf16[8,2,2,240,128]{4,3,2,1,0:T(8,128)(2,1)} %memory_kv.1._.k_ref.v_ref, f32[2,1,1920]{2,1,0:T(1,128)} %broadcast_in_dim_reshape.10.bias_ref), custom_call_target="tpu_custom_call" | custom-call | flops 503316480 | bytes 188416 | tf_op jit(solution)/shard_map/attend_memory/pallas_call | solution.py:604
  224.0 3.4 pad_maximum_fusion.mine_ref
  227.5 3.5 all-to-all-start.4
  233.0 7.6 %all-to-all-done.4.mixed_ref = bf16[8,2,128,128]{3,2,1,0:T(8,128)(2,1)S(1)} async-done(((bf16[8,2,128,128]{3,2,1,0:T(8,128)(2,1)}), bf16[8,2,128,128]{3,2,1,0:T(8,128)(2,1)S(1)}, u32[]{:S(2)}, u32[]{:S(2)}) %all-to-all-start.4) | async-done | bytes 524320 | tf_op jit(solution)/shard_map/all_to_all | solution.py:1309
  241.4 26.3 %ffn.1 = (bf16[256,1024]{1,0:T(8,128)(2,1)}, bf16[256,1024]{1,0:T(8,128)(2,1)}, bf16[8,4,128,1024]{3,2,1,0:T(8,128)(2,1)}, bf16[4,4,128,1024]{3,2,1,0:T(8,128)(2...) custom-call(s32[8]{0:T(128)} %pad_add_fusion.order._, ...), custom_call_target="tpu_custom_call" | custom-call | flops 805306368 | bytes 4194304 | tf_op jit(solution)/shard_map/ffn/pallas_call | solution.py:1020
  267.8 3.5 all-to-all-start.5
  271.3 4.0 collective-permute-done.14
  275.3 4.9 add_convert_fusion.__1_
  285.8 29.5 %attend_memory_back.1 = (bf16[8,2,128,128]{3,2,1,0:T(8,128)(2,1)}, bf16[8,2,2,240,128]{4,3,2,1,0:T(8,128)(2,1)}, f32[2,1920,1]{2,1,0:T(8,128)}) custom-call(bf16[8,1,2,128,128]{4,3,2,1,0:T(8,128)(2,1)} %bitcast.205, bf16[8,2,2,240,128]{4,3,2,1,0:T(8,128)(2,1)} %memory_kv.1._.k_ref.v_ref, bf16[8,2,2,240,128]{4,3,2,1,0:T(8,128)(2,1)} %memory_kv.1._.k_ref.v_ref, ...), custom_call_target="tpu_custom_call" | custom-call | flops 1258291200 | bytes 376832 | tf_op jit(solution)/shard_map/attend_memory_back/pallas_call | solution.py:640
  315.3 13.8 %memory_kv_back.1 = (bf16[4,1,480,1024]{3,2,1,0:T(8,128)(2,1)}, bf16[4,1,480,1024]{3,2,1,0:T(8,128)(2,1)}, bf16[4,8,64,128]{3,2,1,0:T(8,128)(2,1)}, f32[1,256]{1,0:T(1,128)}) custom-call(s32[8]{0:T(128)} %pad_add_fusion.order._, bf16[8,2,384,1024]{3,2,1,0:T(8,128)(2,1)} %bitcast.196, bf16[8,2,2,240,128]{4,3,2,1,0:T(8,128)(2,1)} %get-tuple-element.101.refs_0_, ...), custom_call_target="tpu_custom_call" | custom-call | flops 251658240 | bytes 983040 | tf_op jit(solution)/shard_map/memory_kv_back/pallas_call | solution.py:789
  329.2 3.5 all-to-all-start.6
  332.8 3.9 fusion.4.__1_
  336.7 5.7 %all-to-all-done.6.__0_ = bf16[8,2,128,128]{3,2,1,0:T(8,128)(2,1)S(1)} async-done(((bf16[8,2,128,128]{3,2,1,0:T(8,128)(2,1)}), bf16[8,2,128,128]{3,2,1,0:T(8,128)(2,1)S(1)}, u32[]{:S(2)}, u32[]{:S(2)}) %all-to-all-start.6) | async-done | bytes 524320 | tf_op jit(solution)/shard_map/all_to_all | solution.py:1309
  343.2 5.7 %first_back.1 = (bf16[256,1024]{1,0:T(8,128)(2,1)}, f32[256,1024]{1,0:T(8,128)}, bf16[256,1024]{1,0:T(8,128)(2,1)}, bf16[8,2,128,128]{3,2,1,0:T(8,128)(2,1)}, f32[8,1024]{1,0:T(8,128)}) custom-call(bf16[8,2,128,128]{3,2,1,0:T(8,128)(2,1)} %get-tuple-element.103.dq_ref, f32[256,1024]{1,0:T(8,128)} %get-tuple-element.104.second_grad, ...), custom_call_target="tpu_custom_call" | custom-call | flops 67108864 | bytes 262144 | tf_op jit(solution)/shard_map/first_back/pallas_call | solution.py:1112
  348.9 7.2 %weight_grads.1 = (bf16[4,4,96,1024]{3,2,1,0:T(8,128)(2,1)}, bf16[4,4,96,1024]{3,2,1,0:T(8,128)(2,1)}) custom-call(s32[8]{0:T(128)} %pad_add_fusion.order._, bf16[256,1024]{1,0:T(8,128)(2,1)} %get-tuple-element.109.mixed, bf16[256,1024]{1,0:T(8,128)(2,1)} %get-tuple-element.110.self_low, bf16[256,1024]{1,0:T(8,128)(2,1)} %get-tuple-element.111.first_low, ...), custom_call_target="tpu_custom_call" | custom-call | flops 100663296 | bytes 393216 | tf_op jit(solution)/shard_map/weight_grads/pallas_call | solution.py:1169
  357.8 3.3 all-to-all-start.8
  361.7 4.2 all-to-all-done.8
  367.4 3.7 all-to-all-start.7
  382.7 12.4 %attend_self_back.1 = (bf16[8,2,128,128]{3,2,1,0:T(8,128)(2,1)}, bf16[8,2,2,128,128]{4,3,2,1,0:T(8,128)(2,1)}, f32[2,1024,1]{2,1,0:T(8,128)}) custom-call(bf16[8,3,2,128,128]{4,3,2,1,0:T(8,128)(2,1)} %self_qkv.1.q_ref.k_ref.v_ref, bf16[8,3,2,128,128]{4,3,2,1,0:T(8,128)(2,1)} %self_qkv.1.q_ref.k_ref.v_ref, ...), custom_call_target="tpu_custom_call" | custom-call | flops 671088640 | bytes 262144 | tf_op jit(solution)/shard_map/attend_self_back/pallas_call | solution.py:640
  399.6 12.0 %self_qkv_back.1 = (bf16[4,1,256,1024]{3,2,1,0:T(8,128)(2,1)}, bf16[4,1,256,1024]{3,2,1,0:T(8,128)(2,1)}, bf16[4,8,96,128]{3,2,1,0:T(8,128)(2,1)}, f32[1,384]{1,0:T(1,128)}) custom-call(s32[8]{0:T(128)} %pad_add_fusion.order._, bf16[8,2,384,1024]{3,2,1,0:T(8,128)(2,1)} %bitcast.197, bf16[8,2,128,128]{3,2,1,0:T(8,128)(2,1)} %get-tuple-element.119.refs_0_, ...), custom_call_target="tpu_custom_call" | custom-call | flops 201326592 | bytes 524288 | tf_op jit(solution)/shard_map/self_qkv_back/pallas_call | solution.py:789
  417.2 3.4 collective-permute-done.18.__4_
  429.1 3.7 fusion.1.__0_
  432.8 3.3 fusion.13
  443.2 13.4 %collective-permute-done.30 = bf16[2,8,176,128]{3,2,1,0:T(8,128)(2,1)S(1)} collective-permute-done((bf16[2,8,176,128]{3,2,1,0:T(8,128)(2,1)S(1)}, bf16[2,8,176,128]{3,2,1,0:T(8,128)(2,1)S(1)}, u32[]{:S(2)}, u32[]{:S(2)}) %collective-permute-start.30) | collective-permute-done | bytes 720928 | tf_op jit(solution)/shard_map/ppermute | solution.py:1241
  475.2 5.3 collective-permute-done.33
  487.2 3.7 collective-permute-start.38
  495.9 6.2 %collective-permute-done.28 = bf16[1,240,1024]{2,1,0:T(8,128)(2,1)S(1)} collective-permute-done((bf16[1,240,1024]{2,1,0:T(8,128)(2,1)}, bf16[1,240,1024]{2,1,0:T(8,128)(2,1)S(1)}, u32[]{:S(2)}, u32[]{:S(2)}) %collective-permute-start.28) | collective-permute-done | bytes 491552 | tf_op jit(solution)/shard_map/ppermute | solution.py:1236
  506.1 3.6 collective-permute-start.31
  512.5 9.8 %collective-permute-done.31 = bf16[8,176,128]{2,1,0:T(8,128)(2,1)S(1)} collective-permute-done((bf16[8,176,128]{2,1,0:T(8,128)(2,1)}, bf16[8,176,128]{2,1,0:T(8,128)(2,1)S(1)}, u32[]{:S(2)}, u32[]{:S(2)}) %collective-permute-start.31) | collective-permute-done | bytes 360480 | tf_op jit(solution)/shard_map/ppermute | solution.py:1241
  524.4 3.6 all-to-all-start.9
  529.8 6.1 %all-to-all-done.9 = bf16[8,176,128]{2,1,0:T(8,128)(2,1)S(1)} async-done(((bf16[8,176,128]{2,1,0:T(8,128)(2,1)}), bf16[8,176,128]{2,1,0:T(8,128)(2,1)S(1)}, u32[]{:S(2)}, u32[]{:S(2)}) %all-to-all-start.9) | async-done | bytes 360480 | tf_op jit(solution)/shard_map/all_to_all | solution.py:1309
  537.5 3.5 multiply_subtract_fusion
  (434 shorter events, 151.5 us)
Async XLA Ops:
  7.2 86.8 %all-gather.9.cloned.1.call-start = ((), (), s32[]{:S(2)}) async-start(), calls=%async_computation.14 | async-start | bytes 14155776 | tf_op jit(solution)/shard_map/all_gather | solution.py:1364
  11.8 18.8 %all-to-all-start = ((bf16[8,176,128]{2,1,0:T(8,128)(2,1)}), bf16[8,176,128]{2,1,0:T(8,128)(2,1)S(1)}, u32[]{:S(2)}, u32[]{:S(2)}) async-start(bf16[8,176,128]{2,1,0:T(8,128)(2,1)} %pad_maximum_fusion.15), calls=%async_computation | async-start | bytes 720896 | tf_op jit(solution)/shard_map/all_to_all | solution.py:1309
  17.1 167.8 %all-gather.5.cloned.1.call-start = ((), (), s32[]{:S(2)}) async-start(), calls=%async_computation.11 | async-start | bytes 4718592 | tf_op jit(solution)/shard_map/all_gather | solution.py:1382
  18.8 11.8 %collective-permute-start.1 = (bf16[32,2048]{1,0:T(8,128)(2,1)S(1)}, bf16[32,2048]{1,0:T(8,128)(2,1)S(1)}, u32[]{:S(2)}, u32[]{:S(2)}) collective-permute-start(bf16[32,2048]{1,0:T(8,128)(2,1)S(1)} %bitcast.228), channel_id=1, source_target_pairs={{0,16},{8,24},{16,0},{24,8},{1,17},{9,25},{17,1},{25,9},{2,18},{10... | collective-permute-start | bytes 393224 | tf_op jit(solution)/shard_map/ppermute | solution.py:1188
  42.2 24.1 %collective-permute-start.6 = (bf16[128,1024]{1,0:T(8,128)(2,1)}, bf16[128,1024]{1,0:T(8,128)(2,1)S(1)}, u32[]{:S(2)}, u32[]{:S(2)}) collective-permute-start(bf16[128,1024]{1,0:T(8,128)(2,1)} %hold.20), channel_id=1, source_target_pairs={{0,2},{1,3},{2,0},{3,1},{4,6},{5,7},{6,4},{7,5},{8,10},{9,11},{10,... | collective-permute-start | bytes 786440 | tf_op jit(solution)/shard_map/ppermute | solution.py:1236
  43.9 28.5 %collective-permute-start.7 = (bf16[128,1024]{1,0:T(8,128)(2,1)}, bf16[128,1024]{1,0:T(8,128)(2,1)S(1)}, u32[]{:S(2)}, u32[]{:S(2)}) collective-permute-start(bf16[128,1024]{1,0:T(8,128)(2,1)} %hold.20), channel_id=1, source_target_pairs={{0,4},{1,5},{2,6},{3,7},{4,0},{5,1},{6,2},{7,3},{8,12},{9,13},{10,... | collective-permute-start | bytes 786440 | tf_op jit(solution)/shard_map/ppermute | solution.py:1236
  45.4 27.1 %collective-permute-start.8 = (bf16[128,1024]{1,0:T(8,128)(2,1)}, bf16[128,1024]{1,0:T(8,128)(2,1)S(1)}, u32[]{:S(2)}, u32[]{:S(2)}) collective-permute-start(bf16[128,1024]{1,0:T(8,128)(2,1)} %hold.20), channel_id=1, source_target_pairs={{0,6},{1,7},{2,4},{3,5},{4,2},{5,3},{6,0},{7,1},{8,14},{9,15},{10,... | collective-permute-start | bytes 786440 | tf_op jit(solution)/shard_map/ppermute | solution.py:1236
  45.7 29.8 %collective-permute-start.3 = (bf16[8,176,128]{2,1,0:T(8,128)(2,1)}, bf16[8,176,128]{2,1,0:T(8,128)(2,1)S(1)}, u32[]{:S(2)}, u32[]{:S(2)}) collective-permute-start(bf16[8,176,128]{2,1,0:T(8,128)(2,1)} %hold.19.__1_), channel_id=1, source_target_pairs={{0,8},{8,16},{16,24},{24,0},{1,9},{9,17},{17,25},{25,1},{2,10},{10... | collective-permute-start | bytes 1081352 | tf_op jit(solution)/shard_map/ppermute | solution.py:1188
  49.0 26.5 %collective-permute-start.4 = (bf16[8,176,128]{2,1,0:T(8,128)(2,1)}, bf16[8,176,128]{2,1,0:T(8,128)(2,1)}, u32[]{:S(2)}, u32[]{:S(2)}) collective-permute-start(bf16[8,176,128]{2,1,0:T(8,128)(2,1)} %hold.19.__1_), channel_id=1, source_target_pairs={{0,16},{8,24},{16,0},{24,8},{1,17},{9,25},{17,1},{25,9},{2,18},{10... | collective-permute-start | bytes 1081352 | tf_op jit(solution)/shard_map/ppermute | solution.py:1188
  52.6 13.4 %all-to-all-start.1 = ((f32[8,8,128]{2,1,0:T(8,128)}), f32[8,8,128]{2,1,0:T(8,128)S(1)}, u32[]{:S(2)}, u32[]{:S(2)}) async-start(f32[8,8,128]{2,1,0:T(8,128)} %broadcast_in_dim.94), calls=%async_computation.1 | async-start | bytes 65536 | tf_op jit(solution)/shard_map/all_to_all | solution.py:1309
  66.3 14.6 %collective-permute-start.5 = (bf16[8,176,128]{2,1,0:T(8,128)(2,1)S(1)}, bf16[8,176,128]{2,1,0:T(8,128)(2,1)S(1)}, u32[]{:S(2)}, u32[]{:S(2)}) collective-permute-start(bf16[8,176,128]{2,1,0:T(8,128)(2,1)S(1)} %copy-done.5), channel_id=1, source_target_pairs={{0,24},{8,0},{16,8},{24,16},{1,25},{9,1},{17,9},{25,17},{2,26},{10... | collective-permute-start | bytes 1081352 | tf_op jit(solution)/shard_map/ppermute | solution.py:1188
  88.3 75.6 %collective-permute-start.10 = (bf16[672,1024]{1,0:T(8,128)(2,1)}, bf16[672,1024]{1,0:T(8,128)(2,1)}, u32[]{:S(2)}, u32[]{:S(2)}) collective-permute-start(bf16[672,1024]{1,0:T(8,128)(2,1)} %pad_maximum_fusion.3), channel_id=1, source_target_pairs={{0,16},{8,24},{16,0},{24,8},{1,17},{9,25},{17,1},{25,9},{2,18},{10... | collective-permute-start | bytes 4128776 | tf_op jit(solution)/shard_map/ppermute | solution.py:1241
  112.3 51.6 %all-to-all-start.2 = ((bf16[8,2,128,128]{3,2,1,0:T(8,128)(2,1)}), bf16[8,2,128,128]{3,2,1,0:T(8,128)(2,1)S(1)}, u32[]{:S(2)}, u32[]{:S(2)}) async-start(bf16[8,2,128,128]{3,2,1,0:T(8,128)(2,1)} %get-tuple-element.86), calls=%async_computation.2 | async-start | bytes 1048576 | tf_op jit(solution)/shard_map/all_to_all | solution.py:1309
  115.8 124.8 %all-gather.7.cloned.1.call-start = ((), (), s32[]{:S(2)}) async-start(), calls=%async_computation.12 | async-start | bytes 11796480 | tf_op jit(solution)/shard_map/all_gather | solution.py:1454
  115.9 48.1 %collective-permute-start.11 = (bf16[160,1024]{1,0:T(8,128)(2,1)S(1)}, bf16[160,1024]{1,0:T(8,128)(2,1)S(1)}, u32[]{:S(2)}, u32[]{:S(2)}) collective-permute-start(bf16[160,1024]{1,0:T(8,128)(2,1)S(1)} %copy-done.13), channel_id=1, source_target_pairs={{0,24},{8,0},{16,8},{24,16},{1,25},{9,1},{17,9},{25,17},{2,26},{10... | collective-permute-start | bytes 983048 | tf_op jit(solution)/shard_map/ppermute | solution.py:1188
  119.7 44.3 %collective-permute-start.9 = (bf16[160,1024]{1,0:T(8,128)(2,1)S(1)}, bf16[160,1024]{1,0:T(8,128)(2,1)S(1)}, u32[]{:S(2)}, u32[]{:S(2)}) collective-permute-start(bf16[160,1024]{1,0:T(8,128)(2,1)S(1)} %copy-done.13), channel_id=1, source_target_pairs={{0,8},{8,16},{16,24},{24,0},{1,9},{9,17},{17,25},{25,1},{2,10},{10... | collective-permute-start | bytes 983048 | tf_op jit(solution)/shard_map/ppermute | solution.py:1188
  173.6 50.4 %collective-permute-start.12 = (bf16[2,4,128,1024]{3,2,1,0:T(8,128)(2,1)}, bf16[2,4,128,1024]{3,2,1,0:T(8,128)(2,1)}, u32[]{:S(2)}, u32[]{:S(2)}) collective-permute-start(bf16[2,4,128,1024]{3,2,1,0:T(8,128)(2,1)} %pad_maximum_fusion.1.__1_), channel_id=1, source_target_pairs={{0,8},{8,0},{16,24},{24,16},{1,9},{9,1},{17,25},{25,17},{2,10},{10... | collective-permute-start | bytes 6291464 | tf_op jit(solution)/shard_map/ppermute | solution.py:1241
  227.5 13.2 %collective-permute-start.13 = (bf16[4,4,128,1024]{3,2,1,0:T(8,128)(2,1)}, bf16[4,4,128,1024]{3,2,1,0:T(8,128)(2,1)}, u32[]{:S(2)}, u32[]{:S(2)}) collective-permute-start(bf16[4,4,128,1024]{3,2,1,0:T(8,128)(2,1)} %pad_maximum_fusion.mine_ref), channel_id=1, source_target_pairs={{0,1},{1,0},{2,3},{3,2},{4,5},{5,4},{6,7},{7,6},{8,9},{9,8},{10,11... | collective-permute-start | bytes 12582920 | tf_op jit(solution)/shard_map/ppermute | solution.py:1236
  227.5 13.2 %all-to-all-start.4 = ((bf16[8,2,128,128]{3,2,1,0:T(8,128)(2,1)}), bf16[8,2,128,128]{3,2,1,0:T(8,128)(2,1)S(1)}, u32[]{:S(2)}, u32[]{:S(2)}) async-start(bf16[8,2,128,128]{3,2,1,0:T(8,128)(2,1)} %get-tuple-element.89.__1_), calls=%async_computation.4 | async-start | bytes 1048576 | tf_op jit(solution)/shard_map/all_to_all | solution.py:1309
  231.0 168.6 %reduce-scatter.2.cloned.1.call-start = ((), (), s32[]{:S(2)}) async-start(), calls=%async_computation.13 | async-start | bytes 9437184 | tf_op jit(solution)/shard_map/reduce_scatter | solution.py:1489
  267.8 13.2 %all-to-all-start.5 = ((bf16[8,2,128,128]{3,2,1,0:T(8,128)(2,1)}), bf16[8,2,128,128]{3,2,1,0:T(8,128)(2,1)S(1)}, u32[]{:S(2)}, u32[]{:S(2)}) async-start(bf16[8,2,128,128]{3,2,1,0:T(8,128)(2,1)} %get-tuple-element.94), calls=%async_computation.5 | async-start | bytes 1048576 | tf_op jit(solution)/shard_map/all_to_all | solution.py:1309
  281.8 50.9 %collective-permute-start.15 = (bf16[2,4,128,1024]{3,2,1,0:T(8,128)(2,1)}, bf16[2,4,128,1024]{3,2,1,0:T(8,128)(2,1)S(1)}, u32[]{:S(2)}, u32[]{:S(2)}) collective-permute-start(bf16[2,4,128,1024]{3,2,1,0:T(8,128)(2,1)} %get-tuple-element.99._), channel_id=1, source_target_pairs={{0,8},{8,0},{16,24},{24,16},{1,9},{9,1},{17,25},{25,17},{2,10},{10... | collective-permute-start | bytes 6291464 | tf_op jit(solution)/shard_map/ppermute | solution.py:1241
  329.1 44.3 %collective-permute-start.16 = (bf16[4,1,480,1024]{3,2,1,0:T(8,128)(2,1)}, bf16[4,1,480,1024]{3,2,1,0:T(8,128)(2,1)}, u32[]{:S(2)}, u32[]{:S(2)}) collective-permute-start(bf16[4,1,480,1024]{3,2,1,0:T(8,128)(2,1)} %get-tuple-element.107), channel_id=1, source_target_pairs={{0,1},{1,0},{2,3},{3,2},{4,5},{5,4},{6,7},{7,6},{8,9},{9,8},{10,11... | collective-permute-start | bytes 11796488 | tf_op jit(solution)/shard_map/ppermute | solution.py:1236
  329.2 13.2 %all-to-all-start.6 = ((bf16[8,2,128,128]{3,2,1,0:T(8,128)(2,1)}), bf16[8,2,128,128]{3,2,1,0:T(8,128)(2,1)S(1)}, u32[]{:S(2)}, u32[]{:S(2)}) async-start(bf16[8,2,128,128]{3,2,1,0:T(8,128)(2,1)} %get-tuple-element.100), calls=%async_computation.6 | async-start | bytes 1048576 | tf_op jit(solution)/shard_map/all_to_all | solution.py:1309
  356.2 38.9 %collective-permute-start.17 = (bf16[4,4,96,1024]{3,2,1,0:T(8,128)(2,1)}, bf16[4,4,96,1024]{3,2,1,0:T(8,128)(2,1)}, u32[]{:S(2)}, u32[]{:S(2)}) collective-permute-start(bf16[4,4,96,1024]{3,2,1,0:T(8,128)(2,1)} %get-tuple-element.118), channel_id=1, source_target_pairs={{0,1},{1,0},{2,3},{3,2},{4,5},{5,4},{6,7},{7,6},{8,9},{9,8},{10,11... | collective-permute-start | bytes 9437192 | tf_op jit(solution)/shard_map/ppermute | solution.py:1236
  367.4 14.5 %all-to-all-start.7 = ((bf16[8,2,128,128]{3,2,1,0:T(8,128)(2,1)}), bf16[8,2,128,128]{3,2,1,0:T(8,128)(2,1)S(1)}, u32[]{:S(2)}, u32[]{:S(2)}) async-start(bf16[8,2,128,128]{3,2,1,0:T(8,128)(2,1)} %get-tuple-element.106), calls=%async_computation.7 | async-start | bytes 1048576 | tf_op jit(solution)/shard_map/all_to_all | solution.py:1309
  371.4 49.2 %collective-permute-start.18 = (bf16[4,128,1024]{2,1,0:T(8,128)(2,1)}, bf16[4,128,1024]{2,1,0:T(8,128)(2,1)}, u32[]{:S(2)}, u32[]{:S(2)}) collective-permute-start(bf16[4,128,1024]{2,1,0:T(8,128)(2,1)} %get-tuple-element.131), channel_id=1, source_target_pairs={{0,16},{8,24},{16,0},{24,8},{1,17},{9,25},{17,1},{25,9},{2,18},{10... | collective-permute-start | bytes 3145736 | tf_op jit(solution)/shard_map/ppermute | solution.py:1241
  377.4 43.2 %collective-permute-start.20 = (bf16[2,1,240,1024]{3,2,1,0:T(8,128)(2,1)}, bf16[2,1,240,1024]{3,2,1,0:T(8,128)(2,1)}, u32[]{:S(2)}, u32[]{:S(2)}) collective-permute-start(bf16[2,1,240,1024]{3,2,1,0:T(8,128)(2,1)} %pad_maximum_fusion.7.__2_), channel_id=1, source_target_pairs={{0,4},{1,5},{2,6},{3,7},{4,0},{5,1},{6,2},{7,3},{8,12},{9,13},{10,... | collective-permute-start | bytes 2949128 | tf_op jit(solution)/shard_map/ppermute | solution.py:1236
  380.4 40.2 %collective-permute-start.19 = (bf16[2,1,240,1024]{3,2,1,0:T(8,128)(2,1)}, bf16[2,1,240,1024]{3,2,1,0:T(8,128)(2,1)}, u32[]{:S(2)}, u32[]{:S(2)}) collective-permute-start(bf16[2,1,240,1024]{3,2,1,0:T(8,128)(2,1)} %pad_maximum_fusion.6.__1_), channel_id=1, source_target_pairs={{0,2},{1,3},{2,0},{3,1},{4,6},{5,7},{6,4},{7,5},{8,10},{9,11},{10,... | collective-permute-start | bytes 2949128 | tf_op jit(solution)/shard_map/ppermute | solution.py:1236
  398.1 22.5 %collective-permute-start.22 = (bf16[2,4,48,1024]{3,2,1,0:T(8,128)(2,1)}, bf16[2,4,48,1024]{3,2,1,0:T(8,128)(2,1)}, u32[]{:S(2)}, u32[]{:S(2)}) collective-permute-start(bf16[2,4,48,1024]{3,2,1,0:T(8,128)(2,1)} %pad_maximum_fusion.9.__3_), channel_id=1, source_target_pairs={{0,4},{1,5},{2,6},{3,7},{4,0},{5,1},{6,2},{7,3},{8,12},{9,13},{10,... | collective-permute-start | bytes 2359304 | tf_op jit(solution)/shard_map/ppermute | solution.py:1236
  399.5 21.3 %collective-permute-start.21 = (bf16[2,4,48,1024]{3,2,1,0:T(8,128)(2,1)}, bf16[2,4,48,1024]{3,2,1,0:T(8,128)(2,1)}, u32[]{:S(2)}, u32[]{:S(2)}) collective-permute-start(bf16[2,4,48,1024]{3,2,1,0:T(8,128)(2,1)} %pad_maximum_fusion.8.__2_), channel_id=1, source_target_pairs={{0,2},{1,3},{2,0},{3,1},{4,6},{5,7},{6,4},{7,5},{8,10},{9,11},{10,... | collective-permute-start | bytes 2359304 | tf_op jit(solution)/shard_map/ppermute | solution.py:1236
  422.1 17.1 %collective-permute-start.39 = (bf16[2,128,1024]{2,1,0:T(8,128)(2,1)S(1)}, bf16[2,128,1024]{2,1,0:T(8,128)(2,1)S(1)}, u32[]{:S(2)}, u32[]{:S(2)}) collective-permute-start(bf16[2,128,1024]{2,1,0:T(8,128)(2,1)S(1)} %pad_maximum_fusion.13), channel_id=1, source_target_pairs={{0,8},{8,0},{16,24},{24,16},{1,9},{9,1},{17,25},{25,17},{2,10},{10... | collective-permute-start | bytes 1572872 | tf_op jit(solution)/shard_map/ppermute | solution.py:1241
  423.7 35.9 %collective-permute-start.23 = (bf16[4,1,256,1024]{3,2,1,0:T(8,128)(2,1)S(1)}, bf16[4,1,256,1024]{3,2,1,0:T(8,128)(2,1)S(1)}, u32[]{:S(2)}, u32[]{:S(2)}) collective-permute-start(bf16[4,1,256,1024]{3,2,1,0:T(8,128)(2,1)S(1)} %copy-done.23), channel_id=1, source_target_pairs={{0,1},{1,0},{2,3},{3,2},{4,5},{5,4},{6,7},{7,6},{8,9},{9,8},{10,11... | collective-permute-start | bytes 6291464 | tf_op jit(solution)/shard_map/ppermute | solution.py:1236
  425.4 11.6 %collective-permute-start.35 = (bf16[4,48,1024]{2,1,0:T(8,128)(2,1)S(1)}, bf16[4,48,1024]{2,1,0:T(8,128)(2,1)S(1)}, u32[]{:S(2)}, u32[]{:S(2)}) collective-permute-start(bf16[4,48,1024]{2,1,0:T(8,128)(2,1)S(1)} %get-tuple-element.174), channel_id=1, source_target_pairs={{0,4},{1,5},{2,6},{3,7},{4,0},{5,1},{6,2},{7,3},{8,12},{9,13},{10,... | collective-permute-start | bytes 1179656 | tf_op jit(solution)/shard_map/ppermute | solution.py:1236
  427.7 28.9 %collective-permute-start.30 = (bf16[2,8,176,128]{3,2,1,0:T(8,128)(2,1)S(1)}, bf16[2,8,176,128]{3,2,1,0:T(8,128)(2,1)S(1)}, u32[]{:S(2)}, u32[]{:S(2)}) collective-permute-start(bf16[2,8,176,128]{3,2,1,0:T(8,128)(2,1)S(1)} %copy-done.20), channel_id=1, source_target_pairs={{0,8},{8,0},{16,24},{24,16},{1,9},{9,1},{17,25},{25,17},{2,10},{10... | collective-permute-start | bytes 2162696 | tf_op jit(solution)/shard_map/ppermute | solution.py:1241
  439.3 19.3 %collective-permute-start.40 = (bf16[128,1024]{1,0:T(8,128)(2,1)S(1)}, bf16[128,1024]{1,0:T(8,128)(2,1)S(1)}, u32[]{:S(2)}, u32[]{:S(2)}) collective-permute-start(bf16[128,1024]{1,0:T(8,128)(2,1)S(1)} %fusion.19), channel_id=1, source_target_pairs={{0,16},{8,24},{16,0},{24,8},{1,17},{9,25},{17,1},{25,9},{2,18},{10... | collective-permute-start | bytes 786440 | tf_op jit(solution)/shard_map/ppermute | solution.py:1241
  461.9 23.6 %collective-permute-start.37 = (bf16[2,96,1024]{2,1,0:T(8,128)(2,1)}, bf16[2,96,1024]{2,1,0:T(8,128)(2,1)}, u32[]{:S(2)}, u32[]{:S(2)}) collective-permute-start(bf16[2,96,1024]{2,1,0:T(8,128)(2,1)} %hold.35), channel_id=1, source_target_pairs={{0,8},{8,0},{16,24},{24,16},{1,9},{9,1},{17,25},{25,17},{2,10},{10... | collective-permute-start | bytes 1179656 | tf_op jit(solution)/shard_map/ppermute | solution.py:1241
  465.6 14.8 %collective-permute-start.33 = (bf16[128,1024]{1,0:T(8,128)(2,1)}, bf16[128,1024]{1,0:T(8,128)(2,1)}, u32[]{:S(2)}, u32[]{:S(2)}) collective-permute-start(bf16[128,1024]{1,0:T(8,128)(2,1)} %get-tuple-element.193), channel_id=1, source_target_pairs={{0,4},{1,5},{2,6},{3,7},{4,0},{5,1},{6,2},{7,3},{8,12},{9,13},{10,... | collective-permute-start | bytes 786440 | tf_op jit(solution)/shard_map/ppermute | solution.py:1236
  467.1 15.2 %collective-permute-start.34 = (bf16[128,1024]{1,0:T(8,128)(2,1)}, bf16[128,1024]{1,0:T(8,128)(2,1)}, u32[]{:S(2)}, u32[]{:S(2)}) collective-permute-start(bf16[128,1024]{1,0:T(8,128)(2,1)} %get-tuple-element.192), channel_id=1, source_target_pairs={{0,6},{1,7},{2,4},{3,5},{4,2},{5,3},{6,0},{7,1},{8,14},{9,15},{10,... | collective-permute-start | bytes 786440 | tf_op jit(solution)/shard_map/ppermute | solution.py:1236
  470.4 21.3 %collective-permute-start.26 = (bf16[2,1,128,1024]{3,2,1,0:T(8,128)(2,1)S(1)}, bf16[2,1,128,1024]{3,2,1,0:T(8,128)(2,1)}, u32[]{:S(2)}, u32[]{:S(2)}) collective-permute-start(bf16[2,1,128,1024]{3,2,1,0:T(8,128)(2,1)S(1)} %copy-done.8), channel_id=1, source_target_pairs={{0,4},{1,5},{2,6},{3,7},{4,0},{5,1},{6,2},{7,3},{8,12},{9,13},{10,... | collective-permute-start | bytes 1572872 | tf_op jit(solution)/shard_map/ppermute | solution.py:1236
  473.5 18.2 %collective-permute-start.24 = (bf16[2,1,128,1024]{3,2,1,0:T(8,128)(2,1)S(1)}, bf16[2,1,128,1024]{3,2,1,0:T(8,128)(2,1)S(1)}, u32[]{:S(2)}, u32[]{:S(2)}) collective-permute-start(bf16[2,1,128,1024]{3,2,1,0:T(8,128)(2,1)S(1)} %copy-done.9), channel_id=1, source_target_pairs={{0,2},{1,3},{2,0},{3,1},{4,6},{5,7},{6,4},{7,5},{8,10},{9,11},{10,... | collective-permute-start | bytes 1572872 | tf_op jit(solution)/shard_map/ppermute | solution.py:1236
  480.4 21.7 %collective-permute-start.28 = (bf16[1,240,1024]{2,1,0:T(8,128)(2,1)}, bf16[1,240,1024]{2,1,0:T(8,128)(2,1)S(1)}, u32[]{:S(2)}, u32[]{:S(2)}) collective-permute-start(bf16[1,240,1024]{2,1,0:T(8,128)(2,1)} %get-tuple-element.136), channel_id=1, source_target_pairs={{0,4},{1,5},{2,6},{3,7},{4,0},{5,1},{6,2},{7,3},{8,12},{9,13},{10,... | collective-permute-start | bytes 1474568 | tf_op jit(solution)/shard_map/ppermute | solution.py:1236
  482.3 19.8 %collective-permute-start.29 = (bf16[1,240,1024]{2,1,0:T(8,128)(2,1)}, bf16[1,240,1024]{2,1,0:T(8,128)(2,1)S(1)}, u32[]{:S(2)}, u32[]{:S(2)}) collective-permute-start(bf16[1,240,1024]{2,1,0:T(8,128)(2,1)} %get-tuple-element.137), channel_id=1, source_target_pairs={{0,2},{1,3},{2,0},{3,1},{4,6},{5,7},{6,4},{7,5},{8,10},{9,11},{10,... | collective-permute-start | bytes 1474568 | tf_op jit(solution)/shard_map/ppermute | solution.py:1236
  487.2 40.7 %collective-permute-start.38 = (bf16[96,1024]{1,0:T(8,128)(2,1)}, bf16[96,1024]{1,0:T(8,128)(2,1)}, u32[]{:S(2)}, u32[]{:S(2)}) collective-permute-start(bf16[96,1024]{1,0:T(8,128)(2,1)} %fusion.20), channel_id=1, source_target_pairs={{0,16},{8,24},{16,0},{24,8},{1,17},{9,25},{17,1},{25,9},{2,18},{10... | collective-permute-start | bytes 589832 | tf_op jit(solution)/shard_map/ppermute | solution.py:1241
  494.1 15.6 %collective-permute-start.25 = (bf16[1,128,1024]{2,1,0:T(8,128)(2,1)}, bf16[1,128,1024]{2,1,0:T(8,128)(2,1)}, u32[]{:S(2)}, u32[]{:S(2)}) collective-permute-start(bf16[1,128,1024]{2,1,0:T(8,128)(2,1)} %get-tuple-element.181.__1_), channel_id=1, source_target_pairs={{0,4},{1,5},{2,6},{3,7},{4,0},{5,1},{6,2},{7,3},{8,12},{9,13},{10,... | collective-permute-start | bytes 786440 | tf_op jit(solution)/shard_map/ppermute | solution.py:1236
  495.9 13.8 %collective-permute-start.27 = (bf16[1,128,1024]{2,1,0:T(8,128)(2,1)}, bf16[1,128,1024]{2,1,0:T(8,128)(2,1)}, u32[]{:S(2)}, u32[]{:S(2)}) collective-permute-start(bf16[1,128,1024]{2,1,0:T(8,128)(2,1)} %get-tuple-element.182.__2_), channel_id=1, source_target_pairs={{0,2},{1,3},{2,0},{3,1},{4,6},{5,7},{6,4},{7,5},{8,10},{9,11},{10,... | collective-permute-start | bytes 786440 | tf_op jit(solution)/shard_map/ppermute | solution.py:1236
  506.1 16.3 %collective-permute-start.31 = (bf16[8,176,128]{2,1,0:T(8,128)(2,1)}, bf16[8,176,128]{2,1,0:T(8,128)(2,1)S(1)}, u32[]{:S(2)}, u32[]{:S(2)}) collective-permute-start(bf16[8,176,128]{2,1,0:T(8,128)(2,1)} %hold.32), channel_id=1, source_target_pairs={{0,16},{8,24},{16,0},{24,8},{1,17},{9,25},{17,1},{25,9},{2,18},{10... | collective-permute-start | bytes 1081352 | tf_op jit(solution)/shard_map/ppermute | solution.py:1241
  524.4 11.5 %all-to-all-start.9 = ((bf16[8,176,128]{2,1,0:T(8,128)(2,1)}), bf16[8,176,128]{2,1,0:T(8,128)(2,1)S(1)}, u32[]{:S(2)}, u32[]{:S(2)}) async-start(bf16[8,176,128]{2,1,0:T(8,128)(2,1)} %hold.34), calls=%async_computation.10 | async-start | bytes 720896 | tf_op jit(solution)/shard_map/all_to_all | solution.py:1309
  (80 other events, 546.2 us)
Sparse Core Ops, SparseCore 0:
  10.5 83.4 all-gather.8
  96.4 41.0 all-gather.4
  170.9 64.8 all-gather.6
  267.9 69.0 reduce-scatter.1

commit v2 on v1

--- a/solution.py
+++ b/solution.py
@@ -537,6 +537,8 @@
     key_rows, values = k_ref[...].reshape(keys, width), v_ref[...].reshape(keys, width)
     step = 2
     rows = step * tile
+    if not causal:
+        bias = jnp.broadcast_to(bias_ref[0], (128, keys)).T[:, :1]
     dk_sum[...] = jnp.zeros_like(dk_sum)
     dv_sum[...] = jnp.zeros_like(dv_sum)
     if not causal:
@@ -564,7 +566,7 @@
                 else:
                     scores = jnp.concatenate([scores[: seen - rows], corner], axis=0)
             else:
-                scores = scores + bias_ref[0]
+                scores = scores + bias
             prob = jnp.exp(scores - stat_ref[0, h : h + 1, b * rows : (b + 1) * rows])
             grad_prob = dot(values[:seen], one_grad, NT)
             inner = jnp.sum(prob * grad_prob, axis=0, keepdims=True)
@@ -587,7 +589,7 @@
     if causal:
         prior_ref[...] = jnp.zeros_like(prior_ref)
     else:
-        prior_ref[0] = jnp.sum(prior_sum[...], axis=1, keepdims=True)
+        prior_ref[0] = column_sum(prior_sum[...].T)
 
 
 def pick(array, place):
@@ -648,18 +650,18 @@
             pl.BlockSpec((1, heads, length), lambda s: (s, 0, 0)),
             pl.BlockSpec(memory_space=pl.ANY)
             if causal
-            else pl.BlockSpec((1, key_rows, 1), lambda s: (s, 0, 0)),
+            else pl.BlockSpec((1, 1, key_rows), lambda s: (s, 0, 0)),
             pl.BlockSpec(memory_space=pl.ANY),
         ],
         out_specs=[
             pl.BlockSpec((count, 1, tile, width), lambda s: (0, s, 0, 0)),
             pl.BlockSpec((count, 2, 1, key_tile, width), lambda s: (0, 0, s, 0, 0)),
-            pl.BlockSpec((1, key_rows, 1), lambda s: (s, 0, 0)),
+            pl.BlockSpec((1, 1, key_rows), lambda s: (s, 0, 0)),
         ],
         out_shape=[
             shape((count, seqs, tile, width), jnp.bfloat16),
             shape((count, 2, seqs, key_tile, width), jnp.bfloat16),
-            shape((seqs, key_rows, 1), jnp.float32),
+            shape((seqs, 1, key_rows), jnp.float32),
         ],
         scratch_shapes=[
             pltpu.VMEM((key_rows, width), jnp.float32),
@@ -883,29 +885,13 @@
     bias_ref,
     grad_ref,
     wide_ref,
-    mine_ref,
-    other_ref,
-    mixed_out,
-    layer_out,
-    wide_grad,
-    mine_grad,
-    other_grad,
-    dbias_ref,
-    second_grad,
-    cross_low,
-    mixed_grad,
-    stat_out,
-    columns,
-    contracts,
-    active,
-    slope,
-    low,
-    third_low,
-    second_in,
-    total,
-    wide_sem,
-    contract_sem,
+    *refs,
 ):
+    contract_refs, refs = refs[:8], refs[8:]
+    mixed_out, layer_out, wide_grad = refs[:3]
+    contract_grads, refs = refs[3:11], refs[11:]
+    dbias_ref, second_grad, cross_low, mixed_grad, stat_out, columns, contracts = refs[:7]
+    active, slope, low, third_low, second_in, total, wide_sem, contract_sem = refs[7:]
     blocks, count, groups, rows, block = columns.shape
     part = block // CHIPS
     depth = vector_ref.shape[1]
@@ -921,16 +907,22 @@
             result.append(pltpu.make_async_copy(*ends, wide_sem.at[t, k]))
         return result
 
-    def contract_copy(t, mine, other, outward):
-        there = (mine, other)[t % 2].at[t // 2]
-        here = contracts.at[t]
-        ends = (here, there) if outward else (there, here)
-        return pltpu.make_async_copy(*ends, contract_sem.at[t])
+    def contract_copies(t, pieces, outward):
+        near, far = divmod(DP_ORDER[t // 2], 2)
+        first = pieces[t % 2 * 4 + far].at[near]
+        last = pieces[t % 2 * 4 + 2 + near].at[far]
+        result = []
+        for half, there in enumerate((first, last)):
+            here = contracts.at[t, pl.ds(half * CHIPS // 2, CHIPS // 2)]
+            ends = (here, there) if outward else (there, here)
+            result.append(pltpu.make_async_copy(*ends, contract_sem.at[t, half]))
+        return result
 
     for t in range(blocks):
         for copy in wide_copies(t, wide_ref, False):
             copy.start()
-        contract_copy(t, mine_ref, other_ref, False).start()
+        for copy in contract_copies(t, contract_refs, False):
+            copy.start()
 
     mixed = join(mixed_ref)
     mixed_out[...] = mixed
@@ -955,7 +947,8 @@
         out = (inner * phi).astype(jnp.bfloat16)
         active[t] = out
         slope[t] = phi + inner * jnp.exp(-0.5 * inner * inner) * 0.3989422804014327
-        contract_copy(t, mine_ref, other_ref, False).wait()
+        for copy in contract_copies(t, contract_refs, False):
+            copy.wait()
         total[...] += dot(out, contracts[t].reshape(block, depth), NN)
 
     unit, inverse = norm_parts(total[...])
@@ -980,7 +973,8 @@
         contracts[t] = (
             dot(active[t], third_low[...], TN).astype(jnp.bfloat16).reshape(CHIPS, part, depth)
         )
-        contract_copy(t, mine_grad, other_grad, True).start()
+        for copy in contract_copies(t, contract_grads, True):
+            copy.start()
         total[...] += times_back(inner_low, columns.at[t])
         result = dot(turned, inner_low, NN).astype(jnp.bfloat16)
         for d in range(groups):
@@ -1001,8 +995,7 @@
     stat_out[9:10] = column_sum(grad_second * unit)
     stat_out[10:11] = column_sum(grad_second)
     for t in range(blocks):
-        contract_copy(t, mine_grad, other_grad, True).wait()
-        for copy in wide_copies(t, wide_grad, True):
+        for copy in contract_copies(t, contract_grads, True) + wide_copies(t, wide_grad, True):
             copy.wait()
 
 
@@ -1029,16 +1022,12 @@
                 whole(vectors),
                 whole(bias),
                 full,
-                anywhere,
-                anywhere,
-                anywhere,
+                *[anywhere] * 9,
             ],
             out_specs=[
                 full,
                 full,
-                anywhere,
-                anywhere,
-                anywhere,
+                *[anywhere] * 9,
                 whole(bias),
                 full,
                 full,
@@ -1047,7 +1036,7 @@
             ],
             scratch_shapes=[
                 pltpu.VMEM((blocks, count, groups, part, block), jnp.bfloat16),
-                pltpu.VMEM((blocks,) + contract[0].shape[1:], jnp.bfloat16),
+                pltpu.VMEM((blocks, CHIPS) + contract[0].shape[2:], jnp.bfloat16),
                 pltpu.VMEM((blocks, rows, block), jnp.bfloat16),
                 pltpu.VMEM((blocks, rows, block), jnp.float32),
                 pltpu.VMEM((rows, depth), jnp.bfloat16),
@@ -1055,15 +1044,14 @@
                 pltpu.VMEM((rows, depth), jnp.float32),
                 pltpu.VMEM((rows, depth), jnp.float32),
                 pltpu.SemaphoreType.DMA((blocks, CHIPS)),
-                pltpu.SemaphoreType.DMA((blocks,)),
+                pltpu.SemaphoreType.DMA((blocks, 2)),
             ],
         ),
         out_shape=[
             shape((rows, depth), jnp.bfloat16),
             shape((rows, depth), jnp.bfloat16),
             shape((count, groups, all_rows - part, depth), jnp.bfloat16),
-            shape(contract[0].shape, jnp.bfloat16),
-            shape(contract[0].shape, jnp.bfloat16),
+            *[shape(piece.shape, jnp.bfloat16) for piece in contract],
             shape(bias.shape, jnp.float32),
             shape((rows, depth), jnp.float32),
             shape((rows, depth), jnp.bfloat16),
@@ -1209,20 +1197,14 @@
     def first(self):
         return jnp.stack(self.parts[2:]).astype(jnp.bfloat16)
 
-    def second(self, sent):
-        self.got = exchange_dp(sent, 1)
-        return low_sum(self.parts[1], self.got[1])
-
-    def finish(self, sent):
-        last = exchange_dp(sent, 2)
-        return sum(
-            one.astype(jnp.float32) for one in (self.parts[0], self.got[0], last)
-        )
-
-
-def sum_dp(pieces):
-    halves = HalvingDp(pieces)
-    return halves.finish(halves.second(halves.first()))
+    def second(self, got):
+        self.got = got
+        return (
+            self.parts[1].astype(jnp.float32) + self.got[1].astype(jnp.float32)
+        ).astype(jnp.bfloat16)
+
+    def finish(self, last):
+        return sum(one.astype(jnp.float32) for one in (self.parts[0], self.got[0], last))
 
 
 def relative_order():
@@ -1241,52 +1223,145 @@
     return lax.ppermute(piece, "dp", [(i, i ^ flip) for i in range(size)])
 
 
-def low_sum(*parts):
-    return sum(part.astype(jnp.float32) for part in parts).astype(jnp.bfloat16)
+def add_kernel(*refs):
+    total = sum(ref[...].astype(jnp.float32) for ref in refs[:-1])
+    refs[-1][...] = total.astype(jnp.bfloat16)
+
+
+def add(*terms):
+    flat, specs = [], []
+    first = terms[0]
+    dims = first[0].shape[1:] if isinstance(first, tuple) else first.shape
+    rows = 1
+    for size in dims[:-1]:
+        rows *= size
+    block = min(rows, 256)
+    for term in terms:
+        array, entry = term if isinstance(term, tuple) else (term, 0)
+        flat.append(array.reshape(-1, dims[-1]))
+        start = entry * rows // block
+        specs.append(pl.BlockSpec((block, dims[-1]), lambda i, start=start: (start + i, 0)))
+    return pl.pallas_call(
+        add_kernel,
+        grid=(rows // block,),
+        in_specs=specs,
+        out_specs=pl.BlockSpec((block, dims[-1]), lambda i: (i, 0)),
+        out_shape=shape((rows, dims[-1]), jnp.bfloat16),
+        compiler_params=params(),
+        cost_estimate=cost(0, 0),
+        name="add",
+    )(*flat).reshape(dims)
+
+
+def halves_kernel(*refs):
+    count = (len(refs) - 2) // 2
+    for half in range(2):
+        total = sum(ref[...].astype(jnp.float32) for ref in refs[half * count : (half + 1) * count])
+        refs[2 * count + half][...] = total.astype(jnp.bfloat16)
 
 
 class Halving:
-    def __init__(self, mine, other):
-        self.pair = (mine, exchange(other, 1))
-        middle = mine.shape[2] // 2
-        self.top, self.low = slice(0, middle), slice(middle, None)
-
-    def total(self, k, rows, *more):
-        result = sum(one[k, :, rows].astype(jnp.float32) for one in self.pair)
-        return sum((one.astype(jnp.float32) for one in more), result)
+    def __init__(self, *parts):
+        self.parts = [part.reshape(CHIPS, -1, part.shape[-1]) for part in parts]
+        self.middle = self.parts[0].shape[1] // 2
+
+    def total(self, k, half, *more):
+        rows = slice(half * self.middle, (half + 1) * self.middle)
+        return sum(one.astype(jnp.float32) for one in [p[k, rows] for p in self.parts] + [*more])
 
     def first(self):
+        depth = self.parts[0].shape[2]
+        block = (1, self.middle, depth)
+        top = pl.BlockSpec(block, lambda e: (2 * e + 1, 0, 0))
+        low = pl.BlockSpec(block, lambda e: (2 + e, 1, 0))
+        out = pl.BlockSpec(block, lambda e: (e, 0, 0))
+        count = len(self.parts)
+        return pl.pallas_call(
+            halves_kernel,
+            grid=(2,),
+            in_specs=[top] * count + [low] * count,
+            out_specs=[out, out],
+            out_shape=[shape((2, self.middle, depth), jnp.bfloat16)] * 2,
+            compiler_params=params(),
+            cost_estimate=cost(0, 0),
+            name="halves",
+        )(*self.parts, *self.parts)
+
+    def second(self, top, low):
+        self.got = top, low
         return [
-            jnp.stack([self.total(k, rows) for k in blocks]).astype(jnp.bfloat16)
-            for blocks, rows in (((1, 3), self.top), ((2, 3), self.low))
+            self.total(2, 0, top[1]).astype(jnp.bfloat16),
+            self.total(1, 1, low[1]).astype(jnp.bfloat16),
         ]
 
-    def send(self, sent):
-        return [exchange(sent[0], 2), exchange(sent[1], 4)]
-
-    def second(self, got):
-        self.got = got
-        return [
-            self.total(2, self.top, self.got[0][1]).astype(jnp.bfloat16),
-            self.total(1, self.low, self.got[1][1]).astype(jnp.bfloat16),
-        ]
-
-    def finish(self, sent):
-        last = exchange(sent[0], 4), exchange(sent[1], 2)
+    def finish(self, top, low):
         return jnp.concatenate(
-            [
-                self.total(0, self.top, self.got[0][0], last[0]),
-                self.total(0, self.low, self.got[1][0], last[1]),
-            ],
-            axis=1,
+            [self.total(0, 0, self.got[0][0], top), self.total(0, 1, self.got[1][0], low)], axis=0
         )
 
 
-def small_sum(values):
+def seconds_kernel(*refs):
+    top_out, low_out = refs[-2:]
+    start = 0
+    ins = refs[:-2]
+    while ins:
+        (top, top_got, low, low_got), ins = (ins[0:2], ins[2], ins[3:5], ins[5]), ins[6:]
+        rows = top_got.shape[1]
+        for parts, got, out_ref in ((top, top_got, top_out), (low, low_got, low_out)):
+            total = sum(ref[0].astype(jnp.float32) for ref in (*parts, got))
+            out_ref[start : start + rows] = total.astype(jnp.bfloat16)
+        start += rows
+
+
+def seconds(*sums):
+    arrays, specs = [], []
+    for one, top, low in sums:
+        one.got = top, low
+        block = (1, one.middle, top.shape[2])
+        for k, half, got in ((2, 0, top), (1, 1, low)):
+            arrays += [*one.parts, got]
+            specs += [pl.BlockSpec(block, lambda i, k=k, half=half: (k, half, 0))] * 2
+            specs += [pl.BlockSpec(block, lambda i: (1, 0, 0))]
+    out = shape((sum(one[0].middle for one in sums), arrays[0].shape[2]), jnp.bfloat16)
+    return pl.pallas_call(
+        seconds_kernel,
+        grid=(1,),
+        in_specs=specs,
+        out_specs=[whole(out)] * 2,
+        out_shape=[out] * 2,
+        compiler_params=params(),
+        cost_estimate=cost(0, 0),
+        name="seconds",
+    )(*arrays)
+
+
+def send_first(top, low):
+    return [exchange(top, 2), exchange(low, 4)]
+
+
+def send_last(top, low):
+    return [exchange(top, 4), exchange(low, 2)]
+
+
+def merge(first, second):
+    return [jnp.concatenate(pair, axis=-2) for pair in zip(first, second)]
+
+
+def split_rows(arrays, rows):
+    return [a[..., :rows, :] for a in arrays], [a[..., rows:, :] for a in arrays]
+
+
+def small_send(values):
     size = lax.axis_size("index")
     flat = jnp.pad(values.reshape(-1), (0, 1024 - values.size)).reshape(1, 8, 128)
-    arrived = swap(jnp.broadcast_to(flat, (size, 8, 128)))
-    return jnp.sum(arrived, axis=0).reshape(-1)[: values.size].reshape(values.shape)
+    return swap(jnp.broadcast_to(flat, (size, 8, 128)))
+
+
+def small_take(arrived, dims):
+    size = 1
+    for dim in dims:
+        size *= dim
+    return jnp.sum(arrived, axis=0).reshape(-1)[:size].reshape(dims)
 
 
 def hold_kernel(*_):
@@ -1377,13 +1452,15 @@
     memory_rows = (rows_all, memory_block, 0, memory_here)
     square = attention_low[3:5].transpose(1, 0, 2).reshape(part, 2 * depth)
     received = swap(package)
-    arrived = hold(send_dp(square), received)
-    (received,) = hold([received], *arrived)
-    square = lax.all_gather(place_dp(square, arrived), "index", axis=0, tiled=False)
+    square_arrived = hold(send_dp(square), received)
+    (received,) = hold([received], *square_arrived)
     received_sent = send_dp(received)
     (contract,) = hold([contract_weight.astype(low)], received)
-    contract = jnp.stack([contract] + [exchange(contract, 2 * k) for k in range(1, CHIPS)])
-    slices = place_dp(received, hold(received_sent, contract))
+    contract = [contract] + [exchange(contract, 2 * k) for k in range(1, CHIPS)]
+    slices_arrived = hold(received_sent, *contract[1:])
+    square_arrived = hold(square_arrived, *slices_arrived)
+    square = lax.all_gather(place_dp(square, square_arrived), "index", axis=0, tiled=False)
+    slices = place_dp(received, slices_arrived)
     vectors = (
         slices[:, :, 5 * part :]
         .reshape(groups, count, extra_rows * width)[:, :, : vector_rows * vector_width]
@@ -1412,11 +1489,10 @@
         ],
         axis=0,
     )
-    (late,) = hold([late], slices)
-    across = exchange_dp(jnp.concatenate([late, contract.reshape(-1, depth)], axis=0), 2)
-    late_arrived = send_dp(late)
-    late_arrived[1] = across
-
+    (late,) = hold([late], *slices_arrived)
+    late_sent = send_dp(late)
+
+    (passage_ids,) = hold([passage_ids], *slices_arrived)
     passages_here = passage_vectors.shape[0]
     local_ids = passage_ids - place * passages_here
     owned_slot = (local_ids >= 0) & (local_ids < passages_here)
@@ -1426,7 +1502,7 @@
     )
     slots = passage_ids.shape[1]
     usable = jnp.arange(slots)[None, :] < valid_count[:, None]
-    scores = small_sum(jnp.where(owned_slot, local_scores, 0.0))
+    scores = small_take(small_send(jnp.where(owned_slot, local_scores, 0.0)), local_scores.shape)
     masked = jnp.where(usable, scores, negative_fill)
     maximum = jnp.max(masked, axis=1)
     exponent = jnp.where(usable, jnp.exp(masked - maximum[:, None]), 0.0)
@@ -1444,16 +1520,17 @@
     x_rows = decoder_input.reshape(rows, depth)
     qkv = project_columns("self_qkv", *input_rows, slices, 0, 3, qkv_bias)
     self_out, self_stat = attend(True, qkv, 0, qkv, 1, 2, key_bias[:, None, :])
+    self_out, *late_arrived = hold([self_out, *late_sent])
     self_got = swap(self_out)
+    late = lax.all_gather(place_dp(late, late_arrived), "index", axis=0, tiled=False)
+    ahead, across = hold([jnp.stack(contract[:2]), jnp.stack(contract[2:])], *late_arrived)
+    self_got, ahead_far, across_far, slices = hold(
+        [self_got, exchange_dp(ahead, 2), exchange_dp(across, 1), slices]
+    )
     memory_kv = project_columns("memory_kv", *memory_rows, slices, 3, 2, kv_bias)
-    late_arrived = list(hold(late_arrived, self_got))
-    across = late_arrived[1][late.shape[0] :]
-    late_arrived[1] = late_arrived[1][: late.shape[0]]
-    contract = jnp.stack([contract, across.reshape(contract.shape)])
-    late = place_dp(late, late_arrived)
-    late = lax.all_gather(late, "index", axis=0, tiled=False)
-    (self_got,) = hold([self_got], contract)
-    contract_far = exchange_dp(contract, 1)
+    ahead = jnp.stack([ahead, ahead_far])
+    across = jnp.stack([across, across_far])
+    contract_sent = [exchange_dp(ahead, 1), exchange_dp(across, 2)]
     self_mixed, first_in, first_low, cross_query = first_forward(
         self_got, x_rows, square, vectors, memory_kv
     )
@@ -1461,14 +1538,15 @@
     cross_out, cross_stat = attend(
         False, cross_query, 0, memory_kv, 0, 1, key_bias[:, None, :]
     )
-    contract = jnp.concatenate([contract, *hold([contract_far], cross_out)], axis=0)
+    ahead_far, across_far = hold(contract_sent, cross_out)
+    contract = [ahead, ahead_far, across, across_far]
+    contract += [exchange(piece, 1) for piece in contract]
     places = lax.axis_index("dp") ^ jnp.array(DP_ORDER, jnp.int32)
     (
         cross_mixed,
         layer_output,
         wide_grad,
-        contract_mine,
-        contract_other,
+        *contract_grads,
         inner_total,
         second_grad,
         cross_low,
@@ -1479,7 +1557,7 @@
         swap(cross_out),
         first_in,
         late,
-        (contract, exchange(contract, 1)),
+        contract,
         vectors,
         vectors[6:10].reshape(groups * count, -1),
         output_grad.reshape(rows, depth),
@@ -1487,11 +1565,12 @@
     third_stat, second_stat = stats[:8], stats[8:]
 
     expand_part_sum = lax.psum_scatter(wide_grad, "index", scatter_dimension=0, tiled=False)
-    contract_pair = (contract_mine, exchange(contract_other, 1))
-    contract_sent = low_sum(*(one[2:] for one in contract_pair))
-    cross_mix_got, contract_sent = hold([swap(cross_mix_grad), contract_sent])
-    contract_got = exchange_dp(contract_sent, 1)
-    contract_next = low_sum(*(one[1] for one in contract_pair), contract_got[1])
+    ahead, ahead_far, across, across_far = contract_grads[:4]
+    cores = [exchange(piece, 1) for piece in contract_grads[4:]]
+    cross_mix_got, *contract_sent = hold(
+        [swap(cross_mix_grad), add(ahead_far, cores[1]), add(across_far, cores[3])]
+    )
+    contract_got = [exchange_dp(contract_sent[0], 1), exchange_dp(contract_sent[1], 2)]
     cross_dq, cross_dkv, prior_rows = attend_back(
         False,
         cross_query,
@@ -1501,18 +1580,24 @@
         1,
         cross_mix_got,
         cross_stat,
-        key_bias[:, :, None],
-        contract_sent,
+        key_bias[:, None, :],
+        contract_sent[0],
     )
     memory_mine, memory_other, kv_grads, kv_total = project_columns_back(
         "memory_kv_back", order, *memory_rows, [cross_dkv], slices, 3, 2
     )
-    cross_dq_got, contract_next = hold([swap(cross_dq), contract_next], memory_mine)
-    contract_last = exchange_dp(contract_next, 2)
+    cross_dq, *contract_got = hold([cross_dq, *contract_got], memory_mine)
+    contract_next = [
+        add((ahead, 1), (cores[0], 1), (contract_got[0], 1)),
+        add((across, 1), (cores[2], 1), (contract_got[1], 1)),
+    ]
+    cross_dq_got, *contract_next = hold([swap(cross_dq), *contract_next])
+    contract_last = [exchange_dp(contract_next[0], 2), exchange_dp(contract_next[1], 1)]
     query_low, first_grad, self_low, self_mix_grad, first_stat = first_back(
         cross_dq_got, second_grad, first_in, square, vectors, memory_mine
     )
-    memory_sum = Halving(memory_mine, memory_other)
+    kv_far = HalvingDp(kv_grads)
+    memory_sum = Halving(memory_mine, exchange(memory_other, 1))
     memory_sent = memory_sum.first()
     square_mine, square_other = weight_grads(
         (count, groups, part, depth),
@@ -1524,16 +1609,33 @@
         cross_mixed,
         cross_low,
     )
-    square_sum = Halving(square_mine, square_other)
-    (self_mix_got,) = hold([swap(self_mix_grad)], *memory_sent)
+    square_sum = Halving(square_mine, exchange(square_other, 1))
+    square_sent = square_sum.first()
+    self_mix_got, *contract_last = hold(
+        [swap(self_mix_grad), *contract_last], *memory_sent, *square_sent
+    )
+    memory_got = send_first(*memory_sent)
+    square_got = send_first(*square_sent)
     self_dq, self_dkv, _ = attend_back(
         True, qkv, 0, qkv, 1, 2, self_mix_got, self_stat, self_stat, square_mine
     )
-    square_sent = square_sum.first()
-    self_dq, expand_part_sum = hold([self_dq, expand_part_sum], *square_sent)
+    expand_sum = HalvingDp(expand_part_sum)
+    self_dq, expand_sent = hold([self_dq, expand_sum.first()])
+    expand_got = exchange_dp(expand_sent, 1)
     dx_mine, dx_other, qkv_slice_grads, qkv_total = project_columns_back(
         "self_qkv_back", order, *input_rows, [self_dq, self_dkv], slices, 0, 3
     )
+    dx_mine, dx_other, expand_got, *got = hold(
+        [dx_mine, dx_other, expand_got, *memory_got, *square_got]
+    )
+    dx_got = exchange(dx_other, 1)
+    square_rows = square_sum.middle
+    last = seconds((square_sum, *got[2:]), (memory_sum, *got[:2]))
+    qkv_slice_grads, qkv_total, kv_total, prior_rows, expand_got, *contract_last = hold(
+        [qkv_slice_grads, qkv_total, kv_total, prior_rows, expand_got, *contract_last], *last
+    )
+    last = send_last(*last)
+    expand_last = exchange_dp(expand_sum.second(expand_got), 2)
     own = jnp.concatenate(
         [qkv_total[:, :width], qkv_total[:, 2 * width :], kv_total[:, width:]], axis=0
     )
@@ -1568,47 +1670,41 @@
     slice_sum = HalvingDp(
         jnp.concatenate([qkv_slice_grads, kv_grads, vector_send.astype(low)], axis=2)
     )
-    (
-        dx_mine,
-        dx_other,
-        slice_sent,
-        expand_part_sum,
-        contract_last,
-        memory_top,
-        memory_low,
-        square_top,
-        square_low,
-    ) = hold(
-        [
-            dx_mine,
-            dx_other,
-            slice_sum.first(),
-            expand_part_sum,
-            contract_last,
-            *memory_sum.send(memory_sent),
-            *square_sum.send(square_sent),
-        ]
-    )
-    square_last = square_sum.second([square_top, square_low])
-    memory_last = memory_sum.second([memory_top, memory_low])
-    expand_sum = HalvingDp(expand_part_sum)
-    expand_sent = expand_sum.first()
-    dx_sum = Halving(dx_mine, dx_other)
-    dx_sent = dx_sum.first()
-    dx_last = dx_sum.second(dx_sum.send(dx_sent))
-    memory_last = hold(memory_last, *dx_sent)
-    memory_gradient = memory_sum.finish(memory_last).reshape(encoder_memory.shape)
-    contract_four = low_sum(*(one[0] for one in contract_pair), contract_got[0], contract_last)
-    (contract_four,) = hold([contract_four], *dx_sent)
-    contract_sum = sum(
-        (exchange(contract_four[k], 2 * k).astype(jnp.float32) for k in range(1, CHIPS)),
-        contract_four[0].astype(jnp.float32),
-    )
-    square_part = square_sum.finish(square_last).astype(low)
-    input_gradient = first_grad + dx_sum.finish(dx_last).reshape(rows, depth)
-
-    prior_part = prior_rows.reshape(seqs, slots, MEM_P).sum(axis=-1)
-    prior_grad = jnp.where(usable, small_sum(prior_part), 0.0)
+    slice_got = exchange_dp(slice_sum.first(), 1)
+    prior_arrived = small_send(prior_rows.reshape(seqs, slots, MEM_P).sum(axis=-1))
+    dx_got, expand_last, prior_arrived, *last = hold(
+        [dx_got, expand_last, prior_arrived, *last]
+    )
+    square_last, memory_last = split_rows(last, square_rows)
+    square_far = HalvingDp(square_sum.finish(*square_last).reshape(groups, 3 * part, depth))
+    square_sent = square_far.first()
+    dx_sum = Halving(dx_mine, dx_got)
+    contract_sum = Halving(
+        jnp.concatenate(
+            [
+                add((one, 0), (core, 0), (got, 0), last)
+                for one, core, got, last in zip(
+                    (ahead, across), (cores[0], cores[2]), contract_got, contract_last
+                )
+            ],
+            axis=0,
+        )
+    )
+    got = send_first(*merge(dx_sum.first(), contract_sum.first()))
+    square_got = exchange_dp(square_sent, 1)
+    memory_gradient = memory_sum.finish(*memory_last).reshape(encoder_memory.shape)
+    square_got, slice_got, *got = hold([square_got, slice_got, *got], memory_gradient)
+    dx_got, contract_got = split_rows(got, dx_sum.middle)
+    last = send_last(*merge(dx_sum.second(*dx_got), contract_sum.second(*contract_got)))
+    square_last = exchange_dp(square_far.second(square_got), 2)
+    slice_last = exchange_dp(slice_sum.second(slice_got), 2)
+    slice_last, *last = hold([slice_last, *last])
+    dx_last, contract_last = split_rows(last, dx_sum.middle)
+    input_gradient = first_grad + dx_sum.finish(*dx_last)
+    contract_sum = contract_sum.finish(*contract_last)
+    slice_sum = slice_sum.finish(slice_last)
+
+    prior_grad = jnp.where(usable, small_take(prior_arrived, (seqs, slots)), 0.0)
     score_doc = jnp.where(
         usable, prior_grad - passage_prob * jnp.sum(prior_grad, axis=1, keepdims=True), 0.0
     )
@@ -1619,11 +1715,6 @@
         precision=lax.Precision.HIGHEST,
     )
 
-    square_far = HalvingDp(square_part)
-    (square_sent,) = hold([square_far.first()], *dx_sent)
-    square_next = square_far.second(square_sent)
-    (slice_next,) = hold([slice_sum.second(slice_sent)], *dx_last)
-    slice_sum = slice_sum.finish(slice_next)
     question_send = (
         question_part.reshape(seqs, count, question_width)
         .transpose(1, 0, 2)
@@ -1636,10 +1727,7 @@
     slice_sum = jnp.concatenate(
         [slice_sum[:, : 5 * part], slice_sum[:, 5 * part :] + question_send], axis=1
     )
-    (slice_send,) = hold(
-        [slice_sum.astype(low)], contract_sum, memory_gradient, input_gradient
-    )
-    arrived = swap(slice_send).astype(jnp.float32)
+    arrived = swap(slice_sum.astype(low)).astype(jnp.float32)
     split_grads = (
         arrived[:, : 5 * part]
         .reshape(count, 5, part, width)
@@ -1653,12 +1741,12 @@
     )
 
     expand_sum = (
-        expand_sum.finish(expand_sum.second(expand_sent))
+        expand_sum.finish(expand_last)
         .reshape(hidden // depth, part, depth)
         .transpose(1, 0, 2)
         .reshape(part, hidden)
     )
-    square_total = square_far.finish(square_next).reshape(3, part, depth)
+    square_total = square_far.finish(square_last).reshape(3, part, depth)
     attention_sum = jnp.concatenate(
         [split_grads[:3], square_total[:2], split_grads[3:], square_total[2:]], axis=0
     )

time: 558 us -> 521 us (0.934)
  waiting for transfers between devices: 136 us -> 103 us
  Pallas kernels: 159 us -> 188 us
  other arithmetic: 77.4 us -> 50.5 us
    ppermute x8 -> x9, waiting for transfers between devices: 54.8 us -> 11.9 us  [send_dp(): lax.ppermute(piece, 'dp', [(i, (i + shift) % size) for i in range(size)])]
    pallas_call x0 -> x11, Pallas kernels: none -> 29.9 us  [the longest x6 15.4 us: add(): pl.pallas_call(add_kernel, grid=(rows // block,), in_specs=specs, out_spe...]
    convert_element_type x10 -> x7, other arithmetic: 23.9 us -> 7.66 us  [the longest x3 3.95 us: second(): return (self.parts[1].astype(jnp.float32) + self.got[1].astype(jnp.float3...]
    another operation x16 -> x8, other arithmetic: 17.1 us -> 3.04 us  [the longest x1 1.23 us: head_body(): across = jnp.stack([across, across_far])]
    ppermute x10 -> x14, waiting for transfers between devices: 26.6 us -> 40.5 us  [exchange_dp(): return lax.ppermute(piece, 'dp', [(i, i ^ flip) for i in range(size)])]
    unnamed x155 -> x190, local copies, waits for them, and re-layouts: 14.9 us -> 26 us
    ppermute x8 -> x9, starting transfers between devices: 19.6 us -> 21.4 us  [send_dp(): lax.ppermute(piece, 'dp', [(i, (i + shift) % size) for i in range(size)])]
    ppermute x23 -> x24, starting transfers between devices: 20.5 us -> 19.1 us  [exchange(): return lax.ppermute(piece, 'index', [(i, i ^ flip) for i in range(size)])]
  transfers between devices with their start and end apart: 54 -> 60, of which waited for: 22 -> 22; matrix products, arithmetic and copies ran while one was open for 19% -> 12% of each run, Pallas kernels for 24% -> 32%
where the time goes in v2:
time: 521 us; the launch traced here: 512 us
  Pallas kernels  188 us (36%)
  waiting for transfers between devices  103 us (20%)
  starting transfers between devices  92.9 us (18%)
  other arithmetic  50.5 us (10%)
  local copies, waits for them, and re-layouts  48.1 us (9%)
  between operations  15.6 us (3%)
  blocking collectives  13.3 us (3%)
    pallas_call x2, Pallas kernels, attend_back(): pl.pallas_call(partial(attend_backward_kernel, causal, head_width), grid=...  41.2 us
    ppermute x14, waiting for transfers between devices, exchange_dp(): return lax.ppermute(piece, 'dp', [(i, i ^ flip) for i in range(size)])  40.5 us
    all_to_all x9, starting transfers between devices, swap(): return lax.all_to_all(pieces, 'index', 0, 0, tiled=True)  34.1 us
    all_to_all x9, waiting for transfers between devices, swap(): return lax.all_to_all(pieces, 'index', 0, 0, tiled=True)  32.9 us
    pallas_call x2, Pallas kernels, attend(): pl.pallas_call(partial(attend_forward_kernel, causal, head_width), grid=(...  29.7 us
    pallas_call x1, Pallas kernels, ffn(): pl.pallas_call(ffn_kernel, grid_spec=pltpu.PrefetchScalarGridSpec(num_sca...  26.2 us
    unnamed x190, local copies, waits for them, and re-layouts  26 us
    pallas_call x2, Pallas kernels, project_columns_back(): pl.pallas_call(partial(columns_back_kernel, first), grid_spec=pltpu.Prefe...  25.6 us
  transfers between devices with their start and end apart: 60, of which 22 were waited for; matrix products, arithmetic and copies ran while one was open for 12% of the time, Pallas kernels for 32%

profile of v2, /device:TPU:0, one launch (start us, length us, event | category | flops | bytes accessed | tf_op | source)
XLA Modules:
  0.0 511.7 jit_solution(629782557634467033)
XLA Ops:
  8.5 2.7 fusion.1
  13.0 5.2 %all-to-all-start = ((bf16[8,176,128]{2,1,0:T(8,128)(2,1)}), bf16[8,176,128]{2,1,0:T(8,128)(2,1)S(1)}, u32[]{:S(2)}, u32[]{:S(2)}) async-start(bf16[8,176,128]{2,1,0:T(8,128)(2,1)} %pad_maximum_fusion.16), calls=%async_computation | async-start | bytes 720896 | tf_op jit(solution)/shard_map/all_to_all | solution.py:1384
  19.9 2.6 collective-permute-start.1
  26.5 5.2 %collective-permute-done.1.__1_ = bf16[32,2048]{1,0:T(8,128)(2,1)S(1)} collective-permute-done((bf16[32,2048]{1,0:T(8,128)(2,1)S(1)}, bf16[32,2048]{1,0:T(8,128)(2,1)S(1)}, u32[]{:S(2)}, u32[]{:S(2)}) %collective-permute-start.1) | collective-permute-done | bytes 131104 | tf_op jit(solution)/shard_map/ppermute | solution.py:1176
  34.9 3.2 collective-permute-start.3
  41.9 5.8 %collective-permute-done.6.__3_ = bf16[128,1024]{1,0:T(8,128)(2,1)S(1)} collective-permute-done((bf16[128,1024]{1,0:T(8,128)(2,1)}, bf16[128,1024]{1,0:T(8,128)(2,1)S(1)}, u32[]{:S(2)}, u32[]{:S(2)}) %collective-permute-start.6) | collective-permute-done | bytes 262176 | tf_op jit(solution)/shard_map/ppermute | solution.py:1218
  49.6 8.3 %collective-permute-done.8.__5_ = bf16[128,1024]{1,0:T(8,128)(2,1)S(1)} collective-permute-done((bf16[128,1024]{1,0:T(8,128)(2,1)}, bf16[128,1024]{1,0:T(8,128)(2,1)S(1)}, u32[]{:S(2)}, u32[]{:S(2)}) %collective-permute-start.8) | collective-permute-done | bytes 262176 | tf_op jit(solution)/shard_map/ppermute | solution.py:1218
  57.9 4.7 collective-permute-done.4.__1_
  69.3 6.6 %collective-permute-start.10 = (bf16[160,1024]{1,0:T(8,128)(2,1)}, bf16[160,1024]{1,0:T(8,128)(2,1)S(1)}, u32[]{:S(2)}, u32[]{:S(2)}) collective-permute-start(bf16[160,1024]{1,0:T(8,128)(2,1)} %hold.26), channel_id=1, source_target_pairs={{0,16},{8,24},{16,0},{24,8},{1,17},{9,25},{17,1},{25,9},{2,18},{10... | collective-permute-start | bytes 983048 | tf_op jit(solution)/shard_map/ppermute | solution.py:1176
  75.9 3.3 collective-permute-start.11
  80.3 4.2 gather_fusion
  86.1 3.3 all-to-all-start.1
  95.6 8.2 %self_qkv.1.q_ref.k_ref.v_ref = bf16[8,3,2,128,128]{4,3,2,1,0:T(8,128)(2,1)} custom-call(bf16[8,2,384,1024]{3,2,1,0:T(8,128)(2,1)} %bitcast.205, bf16[4,8,176,128]{3,2,1,0:T(8,128)(2,1)} %copy-done.1, f32[1,384]{1,0:T(1,128)} %fusion.19.bias_ref), custom_call_target="tpu_custom_call" | custom-call | flops 100663296 | bytes 262144 | tf_op jit(solution)/shard_map/self_qkv/pallas_call | solution.py:709
  103.8 10.1 %attend_self.1 = (bf16[8,2,128,128]{3,2,1,0:T(8,128)(2,1)}, f32[2,2,1024]{2,1,0:T(2,128)}) custom-call(bf16[8,3,2,128,128]{4,3,2,1,0:T(8,128)(2,1)} %self_qkv.1.q_ref.k_ref.v_ref, bf16[8,3,2,128,128]{4,3,2,1,0:T(8,128)(2,1)} %self_qkv.1.q_ref.k_ref.v_ref, bf16[8,3,2,128,128]{4,3,2,1,0:T(8,128)(2,1)} %self_qkv.1.q_ref.k_ref.v_ref, ...), custom_call_target="tpu_custom_call" | custom-call | flops 268435456 | bytes 131072 | tf_op jit(solution)/shard_map/attend_self/pallas_call | solution.py:606
  122.1 2.7 collective-permute-start.13
  124.8 13.3 %all_to_all.50.__0_ = bf16[8,2,128,128]{3,2,1,0:T(8,128)(2,1)} all-to-all(bf16[8,2,128,128]{3,2,1,0:T(8,128)(2,1)S(1)} %copy-done.49), channel_id=1, replica_groups=mesh['dp'=4,'index'=8] {'index'}, dimensions={0} | all-to-all | bytes 1048576 | tf_op jit(solution)/shard_map/all_to_all | solution.py:1384
  138.1 8.7 %collective-permute-done.12.__1_ = bf16[2,128,1024]{2,1,0:T(8,128)(2,1)S(1)} collective-permute-done((bf16[2,128,1024]{2,1,0:T(8,128)(2,1)}, bf16[2,128,1024]{2,1,0:T(8,128)(2,1)S(1)}, u32[]{:S(2)}, u32[]{:S(2)}) %collective-permute-start.12) | collective-permute-done | bytes 524320 | tf_op jit(solution)/shard_map/ppermute | solution.py:1223
  154.2 9.0 %memory_kv.1._.k_ref.v_ref = bf16[8,2,2,240,128]{4,3,2,1,0:T(8,128)(2,1)} custom-call(bf16[8,2,384,1024]{3,2,1,0:T(8,128)(2,1)} %bitcast.206, bf16[4,8,176,128]{3,2,1,0:T(8,128)(2,1)} %get-tuple-element.148.slice_ref.refs_1_.refs_2_, f32[1,256]{1,0:T(1,128)} %concatenate.96.bias_ref), custom_call_target="tpu_custom_call" | custom-call | flops 125829120 | bytes 491520 | tf_op jit(solution)/shard_map/memory_kv/pallas_call | solution.py:709
  163.2 5.0 first_forward.1
  168.2 3.5 all-to-all-start.3
  172.3 15.0 %all-to-all-done.3 = bf16[8,2,128,128]{3,2,1,0:T(8,128)(2,1)S(1)} async-done(((bf16[8,2,128,128]{3,2,1,0:T(8,128)(2,1)}), bf16[8,2,128,128]{3,2,1,0:T(8,128)(2,1)S(1)}, u32[]{:S(2)}, u32[]{:S(2)}) %all-to-all-start.3) | async-done | bytes 524320 | tf_op jit(solution)/shard_map/all_to_all | solution.py:1384
  188.1 19.6 %attend_memory.1 = (bf16[8,2,128,128]{3,2,1,0:T(8,128)(2,1)}, f32[2,2,1024]{2,1,0:T(2,128)}) custom-call(bf16[8,1,2,128,128]{4,3,2,1,0:T(8,128)(2,1)} %bitcast.244, bf16[8,2,2,240,128]{4,3,2,1,0:T(8,128)(2,1)} %memory_kv.1._.k_ref.v_ref, bf16[8,2,2,240,128]{4,3,2,1,0:T(8,128)(2,1)} %memory_kv.1._.k_ref.v_ref, f32[2,1,1920]{2,1,0:T(1,128)} %broadcast_in_dim_reshape.6.bias_ref), custom_call_target="tpu_custom_call" | custom-call | flops 503316480 | bytes 188416 | tf_op jit(solution)/shard_map/attend_memory/pallas_call | solution.py:606
  208.4 3.5 all-to-all-start.4
  213.9 7.6 %all-to-all-done.4.mixed_ref = bf16[8,2,128,128]{3,2,1,0:T(8,128)(2,1)S(1)} async-done(((bf16[8,2,128,128]{3,2,1,0:T(8,128)(2,1)}), bf16[8,2,128,128]{3,2,1,0:T(8,128)(2,1)S(1)}, u32[]{:S(2)}, u32[]{:S(2)}) %all-to-all-start.4) | async-done | bytes 524320 | tf_op jit(solution)/shard_map/all_to_all | solution.py:1384
  222.3 26.2 %ffn.1 = (bf16[256,1024]{1,0:T(8,128)(2,1)}, bf16[256,1024]{1,0:T(8,128)(2,1)}, bf16[8,4,128,1024]{3,2,1,0:T(8,128)(2,1)}, bf16[2,2,128,1024]{3,2,1,0:T(8,128)(2...) custom-call(s32[8]{0:T(128)} %pad_add_fusion.order._, ...), custom_call_target="tpu_custom_call" | custom-call | flops 805306368 | bytes 4194304 | tf_op jit(solution)/shard_map/ffn/pallas_call | solution.py:1013
  249.2 3.5 all-to-all-start.5
  253.7 2.6 add.499
  257.3 2.8 add.498
  265.5 29.3 %attend_memory_back.1 = (bf16[8,2,128,128]{3,2,1,0:T(8,128)(2,1)}, bf16[8,2,2,240,128]{4,3,2,1,0:T(8,128)(2,1)}, f32[2,1,1920]{2,1,0:T(1,128)}) custom-call(bf16[8,1,2,128,128]{4,3,2,1,0:T(8,128)(2,1)} %bitcast.245, bf16[8,2,2,240,128]{4,3,2,1,0:T(8,128)(2,1)} %memory_kv.1._.k_ref.v_ref, bf16[8,2,2,240,128]{4,3,2,1,0:T(8,128)(2,1)} %memory_kv.1._.k_ref.v_ref, ...), custom_call_target="tpu_custom_call" | custom-call | flops 1258291200 | bytes 376832 | tf_op jit(solution)/shard_map/attend_memory_back/pallas_call | solution.py:642
  294.8 13.7 %memory_kv_back.1 = (bf16[4,1,480,1024]{3,2,1,0:T(8,128)(2,1)}, bf16[4,1,480,1024]{3,2,1,0:T(8,128)(2,1)}, bf16[4,8,64,128]{3,2,1,0:T(8,128)(2,1)}, f32[1,256]{1,0:T(1,128)}) custom-call(s32[8]{0:T(128)} %pad_add_fusion.order._, bf16[8,2,384,1024]{3,2,1,0:T(8,128)(2,1)} %bitcast.207, bf16[8,2,2,240,128]{4,3,2,1,0:T(8,128)(2,1)} %get-tuple-element.167.refs_0_, ...), custom_call_target="tpu_custom_call" | custom-call | flops 251658240 | bytes 983040 | tf_op jit(solution)/shard_map/memory_kv_back/pallas_call | solution.py:791
  311.1 4.0 all-to-all-start.6
  320.9 3.9 all-to-all-done.6.__0_
  325.6 5.7 %first_back.1 = (bf16[256,1024]{1,0:T(8,128)(2,1)}, f32[256,1024]{1,0:T(8,128)}, bf16[256,1024]{1,0:T(8,128)(2,1)}, bf16[8,2,128,128]{3,2,1,0:T(8,128)(2,1)}, f32[8,1024]{1,0:T(8,128)}) custom-call(bf16[8,2,128,128]{3,2,1,0:T(8,128)(2,1)} %get-tuple-element.176.dq_ref, f32[256,1024]{1,0:T(8,128)} %get-tuple-element.177.second_grad, ...), custom_call_target="tpu_custom_call" | custom-call | flops 67108864 | bytes 262144 | tf_op jit(solution)/shard_map/first_back/pallas_call | solution.py:1100
  331.4 7.0 %weight_grads.1 = (bf16[4,4,96,1024]{3,2,1,0:T(8,128)(2,1)}, bf16[4,4,96,1024]{3,2,1,0:T(8,128)(2,1)}) custom-call(s32[8]{0:T(128)} %pad_add_fusion.order._, bf16[256,1024]{1,0:T(8,128)(2,1)} %get-tuple-element.185.mixed, bf16[256,1024]{1,0:T(8,128)(2,1)} %get-tuple-element.186.self_low, bf16[256,1024]{1,0:T(8,128)(2,1)} %get-tuple-element.187.first_low, ...), custom_call_target="tpu_custom_call" | custom-call | flops 100663296 | bytes 393216 | tf_op jit(solution)/shard_map/weight_grads/pallas_call | solution.py:1157
  340.4 4.2 all-to-all-start.7
  344.5 3.2 halves.4
  352.8 2.9 halves.5
  356.2 7.8 %collective-permute-done.26.__1_ = bf16[2,128,1024]{2,1,0:T(8,128)(2,1)} collective-permute-done((bf16[2,128,1024]{2,1,0:T(8,128)(2,1)}, bf16[2,128,1024]{2,1,0:T(8,128)(2,1)}, u32[]{:S(2)}, u32[]{:S(2)}) %collective-permute-start.26) | collective-permute-done | bytes 524320 | tf_op jit(solution)/shard_map/ppermute | solution.py:1223
  364.6 12.0 %attend_self_back.1 = (bf16[8,2,128,128]{3,2,1,0:T(8,128)(2,1)}, bf16[8,2,2,128,128]{4,3,2,1,0:T(8,128)(2,1)}, f32[2,1,1024]{2,1,0:T(1,128)}) custom-call(bf16[8,3,2,128,128]{4,3,2,1,0:T(8,128)(2,1)} %self_qkv.1.q_ref.k_ref.v_ref, bf16[8,3,2,128,128]{4,3,2,1,0:T(8,128)(2,1)} %self_qkv.1.q_ref.k_ref.v_ref, ...), custom_call_target="tpu_custom_call" | custom-call | flops 671088640 | bytes 262144 | tf_op jit(solution)/shard_map/attend_self_back/pallas_call | solution.py:642
  378.5 12.0 %self_qkv_back.1 = (bf16[4,1,256,1024]{3,2,1,0:T(8,128)(2,1)}, bf16[4,1,256,1024]{3,2,1,0:T(8,128)(2,1)}, bf16[4,8,96,128]{3,2,1,0:T(8,128)(2,1)}, f32[1,384]{1,0:T(1,128)}) custom-call(s32[8]{0:T(128)} %pad_add_fusion.order._, bf16[8,2,384,1024]{3,2,1,0:T(8,128)(2,1)} %bitcast.208, bf16[8,2,128,128]{3,2,1,0:T(8,128)(2,1)} %get-tuple-element.199.refs_0_, ...), custom_call_target="tpu_custom_call" | custom-call | flops 201326592 | bytes 524288 | tf_op jit(solution)/shard_map/self_qkv_back/pallas_call | solution.py:791
  394.4 4.1 seconds.1
  405.8 3.5 all-to-all-start.8
  411.9 2.6 add.503
  442.6 2.8 bitcast_add_fusion.1
  463.7 14.1 %collective-permute-done.46 = bf16[96,1024]{1,0:T(8,128)(2,1)S(1)} collective-permute-done((bf16[96,1024]{1,0:T(8,128)(2,1)S(1)}, bf16[96,1024]{1,0:T(8,128)(2,1)S(1)}, u32[]{:S(2)}, u32[]{:S(2)}) %collective-permute-start.46) | collective-permute-done | bytes 196640 | tf_op jit(solution)/shard_map/ppermute | solution.py:1223
  478.8 6.2 %collective-permute-done.43.__0_ = bf16[8,176,128]{2,1,0:T(8,128)(2,1)S(1)} collective-permute-done((bf16[8,176,128]{2,1,0:T(8,128)(2,1)S(1)}, bf16[8,176,128]{2,1,0:T(8,128)(2,1)S(1)}, u32[]{:S(2)}, u32[]{:S(2)}) %collective-permute-start.43) | collective-permute-done | bytes 360480 | tf_op jit(solution)/shard_map/ppermute | solution.py:1223
  488.1 3.4 all-to-all-start.9
  501.2 3.8 multiply_subtract_fusion
  (488 shorter events, 153.3 us)
Async XLA Ops:
  7.2 88.4 %all-gather.9.cloned.1.call-start = ((), (), s32[]{:S(2)}) async-start(), calls=%async_computation.14 | async-start | bytes 14155776 | tf_op jit(solution)/shard_map/all_gather | solution.py:1439
  13.0 18.7 %all-to-all-start = ((bf16[8,176,128]{2,1,0:T(8,128)(2,1)}), bf16[8,176,128]{2,1,0:T(8,128)(2,1)S(1)}, u32[]{:S(2)}, u32[]{:S(2)}) async-start(bf16[8,176,128]{2,1,0:T(8,128)(2,1)} %pad_maximum_fusion.16), calls=%async_computation | async-start | bytes 720896 | tf_op jit(solution)/shard_map/all_to_all | solution.py:1384
  18.2 145.0 %all-gather.5.cloned.1.call-start = ((), (), s32[]{:S(2)}) async-start(), calls=%async_computation.11 | async-start | bytes 4718592 | tf_op jit(solution)/shard_map/all_gather | solution.py:1462
  33.2 14.6 %collective-permute-start.6 = (bf16[128,1024]{1,0:T(8,128)(2,1)}, bf16[128,1024]{1,0:T(8,128)(2,1)S(1)}, u32[]{:S(2)}, u32[]{:S(2)}) collective-permute-start(bf16[128,1024]{1,0:T(8,128)(2,1)} %hold.23), channel_id=1, source_target_pairs={{0,2},{1,3},{2,0},{3,1},{4,6},{5,7},{6,4},{7,5},{8,10},{9,11},{10,... | collective-permute-start | bytes 786440 | tf_op jit(solution)/shard_map/ppermute | solution.py:1218
  34.9 23.1 %collective-permute-start.3 = (bf16[8,176,128]{2,1,0:T(8,128)(2,1)}, bf16[8,176,128]{2,1,0:T(8,128)(2,1)S(1)}, u32[]{:S(2)}, u32[]{:S(2)}) collective-permute-start(bf16[8,176,128]{2,1,0:T(8,128)(2,1)} %hold.22.__1_), channel_id=1, source_target_pairs={{0,8},{8,16},{16,24},{24,0},{1,9},{9,17},{17,25},{25,1},{2,10},{10... | collective-permute-start | bytes 1081352 | tf_op jit(solution)/shard_map/ppermute | solution.py:1176
  38.1 24.5 %collective-permute-start.4 = (bf16[8,176,128]{2,1,0:T(8,128)(2,1)}, bf16[8,176,128]{2,1,0:T(8,128)(2,1)S(1)}, u32[]{:S(2)}, u32[]{:S(2)}) collective-permute-start(bf16[8,176,128]{2,1,0:T(8,128)(2,1)} %hold.22.__1_), channel_id=1, source_target_pairs={{0,16},{8,24},{16,0},{24,8},{1,17},{9,25},{17,1},{25,9},{2,18},{10... | collective-permute-start | bytes 1081352 | tf_op jit(solution)/shard_map/ppermute | solution.py:1176
  39.8 22.9 %collective-permute-start.5 = (bf16[8,176,128]{2,1,0:T(8,128)(2,1)}, bf16[8,176,128]{2,1,0:T(8,128)(2,1)S(1)}, u32[]{:S(2)}, u32[]{:S(2)}) collective-permute-start(bf16[8,176,128]{2,1,0:T(8,128)(2,1)} %hold.22.__1_), channel_id=1, source_target_pairs={{0,24},{8,0},{16,8},{24,16},{1,25},{9,1},{17,9},{25,17},{2,26},{10... | collective-permute-start | bytes 1081352 | tf_op jit(solution)/shard_map/ppermute | solution.py:1176
  69.3 44.6 %collective-permute-start.10 = (bf16[160,1024]{1,0:T(8,128)(2,1)}, bf16[160,1024]{1,0:T(8,128)(2,1)S(1)}, u32[]{:S(2)}, u32[]{:S(2)}) collective-permute-start(bf16[160,1024]{1,0:T(8,128)(2,1)} %hold.26), channel_id=1, source_target_pairs={{0,16},{8,24},{16,0},{24,8},{1,17},{9,25},{17,1},{25,9},{2,18},{10... | collective-permute-start | bytes 983048 | tf_op jit(solution)/shard_map/ppermute | solution.py:1176
  75.9 38.0 %collective-permute-start.11 = (bf16[160,1024]{1,0:T(8,128)(2,1)}, bf16[160,1024]{1,0:T(8,128)(2,1)S(1)}, u32[]{:S(2)}, u32[]{:S(2)}) collective-permute-start(bf16[160,1024]{1,0:T(8,128)(2,1)} %hold.26), channel_id=1, source_target_pairs={{0,24},{8,0},{16,8},{24,16},{1,25},{9,1},{17,9},{25,17},{2,26},{10... | collective-permute-start | bytes 983048 | tf_op jit(solution)/shard_map/ppermute | solution.py:1176
  79.2 34.7 %collective-permute-start.9 = (bf16[160,1024]{1,0:T(8,128)(2,1)}, bf16[160,1024]{1,0:T(8,128)(2,1)}, u32[]{:S(2)}, u32[]{:S(2)}) collective-permute-start(bf16[160,1024]{1,0:T(8,128)(2,1)} %hold.26), channel_id=1, source_target_pairs={{0,8},{8,16},{16,24},{24,0},{1,9},{9,17},{17,25},{25,1},{2,10},{10... | collective-permute-start | bytes 983048 | tf_op jit(solution)/shard_map/ppermute | solution.py:1176
  89.4 132.1 %all-gather.7.cloned.1.call-start = ((), (), s32[]{:S(2)}) async-start(), calls=%async_computation.12 | async-start | bytes 11796480 | tf_op jit(solution)/shard_map/all_gather | solution.py:1525
  120.8 26.0 %collective-permute-start.12 = (bf16[2,128,1024]{2,1,0:T(8,128)(2,1)}, bf16[2,128,1024]{2,1,0:T(8,128)(2,1)S(1)}, u32[]{:S(2)}, u32[]{:S(2)}) collective-permute-start(bf16[2,128,1024]{2,1,0:T(8,128)(2,1)} %get-tuple-element.142), channel_id=1, source_target_pairs={{0,16},{8,24},{16,0},{24,8},{1,17},{9,25},{17,1},{25,9},{2,18},{10... | collective-permute-start | bytes 1572872 | tf_op jit(solution)/shard_map/ppermute | solution.py:1223
  122.1 24.7 %collective-permute-start.13 = (bf16[2,128,1024]{2,1,0:T(8,128)(2,1)}, bf16[2,128,1024]{2,1,0:T(8,128)(2,1)S(1)}, u32[]{:S(2)}, u32[]{:S(2)}) collective-permute-start(bf16[2,128,1024]{2,1,0:T(8,128)(2,1)} %get-tuple-element.143), channel_id=1, source_target_pairs={{0,8},{8,0},{16,24},{24,16},{1,9},{9,1},{17,25},{25,17},{2,10},{10... | collective-permute-start | bytes 1572872 | tf_op jit(solution)/shard_map/ppermute | solution.py:1223
  149.6 58.1 %collective-permute-start.15 = (bf16[2,2,128,1024]{3,2,1,0:T(8,128)(2,1)S(1)}, bf16[2,2,128,1024]{3,2,1,0:T(8,128)(2,1)}, u32[]{:S(2)}, u32[]{:S(2)}) collective-permute-start(bf16[2,2,128,1024]{3,2,1,0:T(8,128)(2,1)S(1)} %pad_maximum_fusion.3.refs_2_), channel_id=1, source_target_pairs={{0,16},{8,24},{16,0},{24,8},{1,17},{9,25},{17,1},{25,9},{2,18},{10... | collective-permute-start | bytes 3145736 | tf_op jit(solution)/shard_map/ppermute | solution.py:1223
  151.0 56.7 %collective-permute-start.14 = (bf16[2,2,128,1024]{3,2,1,0:T(8,128)(2,1)S(1)}, bf16[2,2,128,1024]{3,2,1,0:T(8,128)(2,1)}, u32[]{:S(2)}, u32[]{:S(2)}) collective-permute-start(bf16[2,2,128,1024]{3,2,1,0:T(8,128)(2,1)S(1)} %pad_maximum_fusion.2.refs_0_), channel_id=1, source_target_pairs={{0,8},{8,0},{16,24},{24,16},{1,9},{9,1},{17,25},{25,17},{2,10},{10... | collective-permute-start | bytes 3145736 | tf_op jit(solution)/shard_map/ppermute | solution.py:1223
  168.2 19.2 %all-to-all-start.3 = ((bf16[8,2,128,128]{3,2,1,0:T(8,128)(2,1)}), bf16[8,2,128,128]{3,2,1,0:T(8,128)(2,1)S(1)}, u32[]{:S(2)}, u32[]{:S(2)}) async-start(bf16[8,2,128,128]{3,2,1,0:T(8,128)(2,1)} %get-tuple-element.149), calls=%async_computation.3 | async-start | bytes 1048576 | tf_op jit(solution)/shard_map/all_to_all | solution.py:1384
  171.7 49.8 %collective-permute-start.18 = (bf16[2,2,128,1024]{3,2,1,0:T(8,128)(2,1)S(1)}, bf16[2,2,128,1024]{3,2,1,0:T(8,128)(2,1)}, u32[]{:S(2)}, u32[]{:S(2)}) collective-permute-start(bf16[2,2,128,1024]{3,2,1,0:T(8,128)(2,1)S(1)} %pad_maximum_fusion.3.refs_2_), channel_id=1, source_target_pairs={{0,1},{1,0},{2,3},{3,2},{4,5},{5,4},{6,7},{7,6},{8,9},{9,8},{10,11... | collective-permute-start | bytes 3145736 | tf_op jit(solution)/shard_map/ppermute | solution.py:1218
  172.1 49.4 %collective-permute-start.16 = (bf16[2,2,128,1024]{3,2,1,0:T(8,128)(2,1)S(1)}, bf16[2,2,128,1024]{3,2,1,0:T(8,128)(2,1)}, u32[]{:S(2)}, u32[]{:S(2)}) collective-permute-start(bf16[2,2,128,1024]{3,2,1,0:T(8,128)(2,1)S(1)} %pad_maximum_fusion.2.refs_0_), channel_id=1, source_target_pairs={{0,1},{1,0},{2,3},{3,2},{4,5},{5,4},{6,7},{7,6},{8,9},{9,8},{10,11... | collective-permute-start | bytes 3145736 | tf_op jit(solution)/shard_map/ppermute | solution.py:1218
  207.8 13.8 %collective-permute-start.17 = (bf16[2,2,128,1024]{3,2,1,0:T(8,128)(2,1)}, bf16[2,2,128,1024]{3,2,1,0:T(8,128)(2,1)}, u32[]{:S(2)}, u32[]{:S(2)}) collective-permute-start(bf16[2,2,128,1024]{3,2,1,0:T(8,128)(2,1)} %get-tuple-element.154.refs_1_), channel_id=1, source_target_pairs={{0,1},{1,0},{2,3},{3,2},{4,5},{5,4},{6,7},{7,6},{8,9},{9,8},{10,11... | collective-permute-start | bytes 3145736 | tf_op jit(solution)/shard_map/ppermute | solution.py:1218
  207.9 13.7 %collective-permute-start.19 = (bf16[2,2,128,1024]{3,2,1,0:T(8,128)(2,1)}, bf16[2,2,128,1024]{3,2,1,0:T(8,128)(2,1)}, u32[]{:S(2)}, u32[]{:S(2)}) collective-permute-start(bf16[2,2,128,1024]{3,2,1,0:T(8,128)(2,1)} %get-tuple-element.155.refs_3_), channel_id=1, source_target_pairs={{0,1},{1,0},{2,3},{3,2},{4,5},{5,4},{6,7},{7,6},{8,9},{9,8},{10,11... | collective-permute-start | bytes 3145736 | tf_op jit(solution)/shard_map/ppermute | solution.py:1218
  211.9 164.7 %reduce-scatter.2.cloned.1.call-start = ((), (), s32[]{:S(2)}) async-start(), calls=%async_computation.13 | async-start | bytes 9437184 | tf_op jit(solution)/shard_map/reduce_scatter | solution.py:1567
  249.2 13.2 %all-to-all-start.5 = ((bf16[8,2,128,128]{3,2,1,0:T(8,128)(2,1)}), bf16[8,2,128,128]{3,2,1,0:T(8,128)(2,1)S(1)}, u32[]{:S(2)}, u32[]{:S(2)}) async-start(bf16[8,2,128,128]{3,2,1,0:T(8,128)(2,1)} %get-tuple-element.157), calls=%async_computation.5 | async-start | bytes 1048576 | tf_op jit(solution)/shard_map/all_to_all | solution.py:1384
  263.1 45.5 %collective-permute-start.22 = (bf16[2,2,128,1024]{3,2,1,0:T(8,128)(2,1)}, bf16[2,2,128,1024]{3,2,1,0:T(8,128)(2,1)S(1)}, u32[]{:S(2)}, u32[]{:S(2)}) collective-permute-start(bf16[2,2,128,1024]{3,2,1,0:T(8,128)(2,1)} %get-tuple-element.164._), channel_id=1, source_target_pairs={{0,8},{8,0},{16,24},{24,16},{1,9},{9,1},{17,25},{25,17},{2,10},{10... | collective-permute-start | bytes 3145736 | tf_op jit(solution)/shard_map/ppermute | solution.py:1223
  263.4 46.7 %collective-permute-start.23 = (bf16[2,2,128,1024]{3,2,1,0:T(8,128)(2,1)}, bf16[2,2,128,1024]{3,2,1,0:T(8,128)(2,1)S(1)}, u32[]{:S(2)}, u32[]{:S(2)}) collective-permute-start(bf16[2,2,128,1024]{3,2,1,0:T(8,128)(2,1)} %get-tuple-element.166), channel_id=1, source_target_pairs={{0,16},{8,24},{16,0},{24,8},{1,17},{9,25},{17,1},{25,9},{2,18},{10... | collective-permute-start | bytes 3145736 | tf_op jit(solution)/shard_map/ppermute | solution.py:1223
  265.0 50.1 %collective-permute-start.25 = (bf16[2,2,128,1024]{3,2,1,0:T(8,128)(2,1)}, bf16[2,2,128,1024]{3,2,1,0:T(8,128)(2,1)S(1)}, u32[]{:S(2)}, u32[]{:S(2)}) collective-permute-start(bf16[2,2,128,1024]{3,2,1,0:T(8,128)(2,1)} %get-tuple-element.174), channel_id=1, source_target_pairs={{0,1},{1,0},{2,3},{3,2},{4,5},{5,4},{6,7},{7,6},{8,9},{9,8},{10,11... | collective-permute-start | bytes 3145736 | tf_op jit(solution)/shard_map/ppermute | solution.py:1218
  265.0 53.5 %collective-permute-start.24 = (bf16[2,2,128,1024]{3,2,1,0:T(8,128)(2,1)}, bf16[2,2,128,1024]{3,2,1,0:T(8,128)(2,1)}, u32[]{:S(2)}, u32[]{:S(2)}) collective-permute-start(bf16[2,2,128,1024]{3,2,1,0:T(8,128)(2,1)} %get-tuple-element.171), channel_id=1, source_target_pairs={{0,1},{1,0},{2,3},{3,2},{4,5},{5,4},{6,7},{7,6},{8,9},{9,8},{10,11... | collective-permute-start | bytes 3145736 | tf_op jit(solution)/shard_map/ppermute | solution.py:1218
  308.5 36.0 %collective-permute-start.28 = (bf16[4,1,480,1024]{3,2,0,1:T(8,128)(2,1)}, bf16[4,1,480,1024]{3,2,0,1:T(8,128)(2,1)}, u32[]{:S(2)}, u32[]{:S(2)}) collective-permute-start(bf16[4,1,480,1024]{3,2,0,1:T(8,128)(2,1)} %bitcast.297), channel_id=1, source_target_pairs={{0,1},{1,0},{2,3},{3,2},{4,5},{5,4},{6,7},{7,6},{8,9},{9,8},{10,11... | collective-permute-start | bytes 11796488 | tf_op jit(solution)/shard_map/ppermute | solution.py:1218
  311.1 13.7 %all-to-all-start.6 = ((bf16[8,2,128,128]{3,2,1,0:T(8,128)(2,1)}), bf16[8,2,128,128]{3,2,1,0:T(8,128)(2,1)S(1)}, u32[]{:S(2)}, u32[]{:S(2)}) async-start(bf16[8,2,128,128]{3,2,1,0:T(8,128)(2,1)} %get-tuple-element.169), calls=%async_computation.6 | async-start | bytes 1048576 | tf_op jit(solution)/shard_map/all_to_all | solution.py:1384
  338.3 25.7 %collective-permute-start.26 = (bf16[2,128,1024]{2,1,0:T(8,128)(2,1)}, bf16[2,128,1024]{2,1,0:T(8,128)(2,1)}, u32[]{:S(2)}, u32[]{:S(2)}) collective-permute-start(bf16[2,128,1024]{2,1,0:T(8,128)(2,1)} %get-tuple-element.180), channel_id=1, source_target_pairs={{0,16},{8,24},{16,0},{24,8},{1,17},{9,25},{17,1},{25,9},{2,18},{10... | collective-permute-start | bytes 1572872 | tf_op jit(solution)/shard_map/ppermute | solution.py:1223
  338.7 25.9 %collective-permute-start.27 = (bf16[2,128,1024]{2,1,0:T(8,128)(2,1)}, bf16[2,128,1024]{2,1,0:T(8,128)(2,1)}, u32[]{:S(2)}, u32[]{:S(2)}) collective-permute-start(bf16[2,128,1024]{2,1,0:T(8,128)(2,1)} %get-tuple-element.181), channel_id=1, source_target_pairs={{0,8},{8,0},{16,24},{24,16},{1,9},{9,1},{17,25},{25,17},{2,10},{10... | collective-permute-start | bytes 1572872 | tf_op jit(solution)/shard_map/ppermute | solution.py:1223
  340.4 24.3 %all-to-all-start.7 = ((bf16[8,2,128,128]{3,2,1,0:T(8,128)(2,1)}), bf16[8,2,128,128]{3,2,1,0:T(8,128)(2,1)}, u32[]{:S(2)}, u32[]{:S(2)}) async-start(bf16[8,2,128,128]{3,2,1,0:T(8,128)(2,1)} %get-tuple-element.179), calls=%async_computation.7 | async-start | bytes 1048576 | tf_op jit(solution)/shard_map/all_to_all | solution.py:1384
  347.8 42.7 %collective-permute-start.31 = (bf16[2,240,1024]{2,1,0:T(8,128)(2,1)}, bf16[2,240,1024]{2,1,0:T(8,128)(2,1)}, u32[]{:S(2)}, u32[]{:S(2)}) collective-permute-start(bf16[2,240,1024]{2,1,0:T(8,128)(2,1)} %get-tuple-element.183.__3_), channel_id=1, source_target_pairs={{0,2},{1,3},{2,0},{3,1},{4,6},{5,7},{6,4},{7,5},{8,10},{9,11},{10,... | collective-permute-start | bytes 2949128 | tf_op jit(solution)/shard_map/ppermute | solution.py:1218
  349.6 40.9 %collective-permute-start.32 = (bf16[2,240,1024]{2,1,0:T(8,128)(2,1)}, bf16[2,240,1024]{2,1,0:T(8,128)(2,1)}, u32[]{:S(2)}, u32[]{:S(2)}) collective-permute-start(bf16[2,240,1024]{2,1,0:T(8,128)(2,1)} %get-tuple-element.184.__4_), channel_id=1, source_target_pairs={{0,4},{1,5},{2,6},{3,7},{4,0},{5,1},{6,2},{7,3},{8,12},{9,13},{10,... | collective-permute-start | bytes 2949128 | tf_op jit(solution)/shard_map/ppermute | solution.py:1218
  355.7 35.5 %collective-permute-start.33 = (bf16[2,192,1024]{2,1,0:T(8,128)(2,1)}, bf16[2,192,1024]{2,1,0:T(8,128)(2,1)S(1)}, u32[]{:S(2)}, u32[]{:S(2)}) collective-permute-start(bf16[2,192,1024]{2,1,0:T(8,128)(2,1)} %get-tuple-element.193.__5_), channel_id=1, source_target_pairs={{0,2},{1,3},{2,0},{3,1},{4,6},{5,7},{6,4},{7,5},{8,10},{9,11},{10,... | collective-permute-start | bytes 2359304 | tf_op jit(solution)/shard_map/ppermute | solution.py:1218
  364.0 27.6 %collective-permute-start.34 = (bf16[2,192,1024]{2,1,0:T(8,128)(2,1)}, bf16[2,192,1024]{2,1,0:T(8,128)(2,1)S(1)}, u32[]{:S(2)}, u32[]{:S(2)}) collective-permute-start(bf16[2,192,1024]{2,1,0:T(8,128)(2,1)} %get-tuple-element.194.__6_), channel_id=1, source_target_pairs={{0,4},{1,5},{2,6},{3,7},{4,0},{5,1},{6,2},{7,3},{8,12},{9,13},{10,... | collective-permute-start | bytes 2359304 | tf_op jit(solution)/shard_map/ppermute | solution.py:1218
  378.5 13.8 %collective-permute-start.30 = (bf16[2,128,1024]{2,1,0:T(8,128)(2,1)}, bf16[2,128,1024]{2,1,0:T(8,128)(2,1)S(1)}, u32[]{:S(2)}, u32[]{:S(2)}) collective-permute-start(bf16[2,128,1024]{2,1,0:T(8,128)(2,1)} %get-tuple-element.203), channel_id=1, source_target_pairs={{0,8},{8,0},{16,24},{24,16},{1,9},{9,1},{17,25},{25,17},{2,10},{10... | collective-permute-start | bytes 1572872 | tf_op jit(solution)/shard_map/ppermute | solution.py:1223
  393.1 29.4 %collective-permute-start.35 = (bf16[4,1,256,1024]{3,2,1,0:T(8,128)(2,1)}, bf16[4,1,256,1024]{3,2,1,0:T(8,128)(2,1)S(1)}, u32[]{:S(2)}, u32[]{:S(2)}) collective-permute-start(bf16[4,1,256,1024]{3,2,1,0:T(8,128)(2,1)} %get-tuple-element.205), channel_id=1, source_target_pairs={{0,1},{1,0},{2,3},{3,2},{4,5},{5,4},{6,7},{7,6},{8,9},{9,8},{10,11... | collective-permute-start | bytes 6291464 | tf_op jit(solution)/shard_map/ppermute | solution.py:1218
  398.6 23.8 %collective-permute-start.37 = (bf16[432,1024]{1,0:T(8,128)(2,1)}, bf16[432,1024]{1,0:T(8,128)(2,1)}, u32[]{:S(2)}, u32[]{:S(2)}) collective-permute-start(bf16[432,1024]{1,0:T(8,128)(2,1)} %get-tuple-element.217.__7_), channel_id=1, source_target_pairs={{0,4},{1,5},{2,6},{3,7},{4,0},{5,1},{6,2},{7,3},{8,12},{9,13},{10,... | collective-permute-start | bytes 2654216 | tf_op jit(solution)/shard_map/ppermute | solution.py:1218
  400.1 22.4 %collective-permute-start.38 = (bf16[432,1024]{1,0:T(8,128)(2,1)}, bf16[432,1024]{1,0:T(8,128)(2,1)}, u32[]{:S(2)}, u32[]{:S(2)}) collective-permute-start(bf16[432,1024]{1,0:T(8,128)(2,1)} %get-tuple-element.218.__8_), channel_id=1, source_target_pairs={{0,2},{1,3},{2,0},{3,1},{4,6},{5,7},{6,4},{7,5},{8,10},{9,11},{10,... | collective-permute-start | bytes 2654216 | tf_op jit(solution)/shard_map/ppermute | solution.py:1218
  402.4 20.0 %collective-permute-start.36 = (bf16[128,1024]{1,0:T(8,128)(2,1)}, bf16[128,1024]{1,0:T(8,128)(2,1)}, u32[]{:S(2)}, u32[]{:S(2)}) collective-permute-start(bf16[128,1024]{1,0:T(8,128)(2,1)} %fusion.6), channel_id=1, source_target_pairs={{0,16},{8,24},{16,0},{24,8},{1,17},{9,25},{17,1},{25,9},{2,18},{10... | collective-permute-start | bytes 786440 | tf_op jit(solution)/shard_map/ppermute | solution.py:1223
  405.8 16.6 %all-to-all-start.8 = ((f32[8,8,128]{2,1,0:T(8,128)}), f32[8,8,128]{2,1,0:T(8,128)S(1)}, u32[]{:S(2)}, u32[]{:S(2)}) async-start(f32[8,8,128]{2,1,0:T(8,128)} %broadcast_in_dim.99), calls=%async_computation.9 | async-start | bytes 65536 | tf_op jit(solution)/shard_map/all_to_all | solution.py:1384
  421.2 25.6 %collective-permute-start.40 = (bf16[2,8,176,128]{3,2,1,0:T(8,128)(2,1)}, bf16[2,8,176,128]{3,2,1,0:T(8,128)(2,1)}, u32[]{:S(2)}, u32[]{:S(2)}) collective-permute-start(bf16[2,8,176,128]{3,2,1,0:T(8,128)(2,1)} %pad_maximum_fusion.8), channel_id=1, source_target_pairs={{0,8},{8,0},{16,24},{24,16},{1,9},{9,1},{17,25},{25,17},{2,10},{10... | collective-permute-start | bytes 2162696 | tf_op jit(solution)/shard_map/ppermute | solution.py:1223
  429.0 19.8 %collective-permute-start.42 = (bf16[2,192,1024]{2,1,0:T(8,128)(2,1)}, bf16[2,192,1024]{2,1,0:T(8,128)(2,1)S(1)}, u32[]{:S(2)}, u32[]{:S(2)}) collective-permute-start(bf16[2,192,1024]{2,1,0:T(8,128)(2,1)} %pad_maximum_fusion.7), channel_id=1, source_target_pairs={{0,4},{1,5},{2,6},{3,7},{4,0},{5,1},{6,2},{7,3},{8,12},{9,13},{10,... | collective-permute-start | bytes 2359304 | tf_op jit(solution)/shard_map/ppermute | solution.py:1218
  431.9 19.2 %collective-permute-start.41 = (bf16[2,192,1024]{2,1,0:T(8,128)(2,1)}, bf16[2,192,1024]{2,1,0:T(8,128)(2,1)S(1)}, u32[]{:S(2)}, u32[]{:S(2)}) collective-permute-start(bf16[2,192,1024]{2,1,0:T(8,128)(2,1)} %pad_maximum_fusion.6), channel_id=1, source_target_pairs={{0,2},{1,3},{2,0},{3,1},{4,6},{5,7},{6,4},{7,5},{8,10},{9,11},{10,... | collective-permute-start | bytes 2359304 | tf_op jit(solution)/shard_map/ppermute | solution.py:1218
  456.3 28.7 %collective-permute-start.45 = (bf16[192,1024]{1,0:T(8,128)(2,1)S(1)}, bf16[192,1024]{1,0:T(8,128)(2,1)S(1)}, u32[]{:S(2)}, u32[]{:S(2)}) collective-permute-start(bf16[192,1024]{1,0:T(8,128)(2,1)S(1)} %pad_maximum_fusion.15), channel_id=1, source_target_pairs={{0,2},{1,3},{2,0},{3,1},{4,6},{5,7},{6,4},{7,5},{8,10},{9,11},{10,... | collective-permute-start | bytes 1179656 | tf_op jit(solution)/shard_map/ppermute | solution.py:1218
  457.9 27.2 %collective-permute-start.44 = (bf16[192,1024]{1,0:T(8,128)(2,1)S(1)}, bf16[192,1024]{1,0:T(8,128)(2,1)}, u32[]{:S(2)}, u32[]{:S(2)}) collective-permute-start(bf16[192,1024]{1,0:T(8,128)(2,1)S(1)} %pad_maximum_fusion.14), channel_id=1, source_target_pairs={{0,4},{1,5},{2,6},{3,7},{4,0},{5,1},{6,2},{7,3},{8,12},{9,13},{10,... | collective-permute-start | bytes 1179656 | tf_op jit(solution)/shard_map/ppermute | solution.py:1218
  459.5 18.3 %collective-permute-start.46 = (bf16[96,1024]{1,0:T(8,128)(2,1)S(1)}, bf16[96,1024]{1,0:T(8,128)(2,1)S(1)}, u32[]{:S(2)}, u32[]{:S(2)}) collective-permute-start(bf16[96,1024]{1,0:T(8,128)(2,1)S(1)} %fusion.10), channel_id=1, source_target_pairs={{0,16},{8,24},{16,0},{24,8},{1,17},{9,25},{17,1},{25,9},{2,18},{10... | collective-permute-start | bytes 589832 | tf_op jit(solution)/shard_map/ppermute | solution.py:1223
  461.5 23.6 %collective-permute-start.43 = (bf16[8,176,128]{2,1,0:T(8,128)(2,1)S(1)}, bf16[8,176,128]{2,1,0:T(8,128)(2,1)S(1)}, u32[]{:S(2)}, u32[]{:S(2)}) collective-permute-start(bf16[8,176,128]{2,1,0:T(8,128)(2,1)S(1)} %fusion.7), channel_id=1, source_target_pairs={{0,16},{8,24},{16,0},{24,8},{1,17},{9,25},{17,1},{25,9},{2,18},{10... | collective-permute-start | bytes 1081352 | tf_op jit(solution)/shard_map/ppermute | solution.py:1223
  (104 other events, 456.5 us)
Sparse Core Ops, SparseCore 0:
  11.3 81.0 all-gather.8
  94.8 37.2 all-gather.4
  134.0 73.1 all-gather.6
  248.7 68.3 reduce-scatter.1

commit v3 on v2

--- a/solution.py
+++ b/solution.py
@@ -1187,6 +1187,21 @@
     return result
 
 
+def to_chips(block):
+    return [exchange(block, 2 * k) for k in range(1, CHIPS)]
+
+
+def gather_index(mine):
+    size, me = lax.axis_size("index"), lax.axis_index("index")
+    block = mine[0]
+    other = exchange(jnp.stack(mine), 1)
+    result = jnp.zeros((size,) + block.shape, block.dtype)
+    for k in range(CHIPS):
+        result = lax.dynamic_update_index_in_dim(result, mine[k], me ^ (2 * k), 0)
+        result = lax.dynamic_update_index_in_dim(result, other[k], me ^ (2 * k) ^ 1, 0)
+    return result
+
+
 class HalvingDp:
     def __init__(self, pieces):
         me = lax.axis_index("dp")
@@ -1253,46 +1268,62 @@
     )(*flat).reshape(dims)
 
 
-def halves_kernel(*refs):
-    count = (len(refs) - 2) // 2
-    for half in range(2):
-        total = sum(ref[...].astype(jnp.float32) for ref in refs[half * count : (half + 1) * count])
-        refs[2 * count + half][...] = total.astype(jnp.bfloat16)
+def combine_kernel(plan, *refs):
+    ins, outs = list(refs[: -len(plan)]), refs[-len(plan) :]
+    for out_ref, entries in zip(outs, plan):
+        for e, segments in enumerate(entries):
+            start = 0
+            for count, rows in segments:
+                terms, ins = ins[:count], ins[count:]
+                total = sum(ref[0].astype(jnp.float32) for ref in terms)
+                out_ref[e, start : start + rows] = total.astype(jnp.bfloat16)
+                start += rows
+
+
+def combine(*outputs):
+    arrays, specs, plan, shapes = [], [], [], []
+    for entries in outputs:
+        plan.append([])
+        for segments in entries:
+            plan[-1].append([])
+            for terms in segments:
+                plan[-1][-1].append((len(terms), terms[0][2]))
+                for array, e, rows, place in terms:
+                    arrays.append(array)
+                    specs.append(
+                        pl.BlockSpec(
+                            (1, rows, array.shape[2]), lambda i, e=e, place=place: (e, place, 0)
+                        )
+                    )
+        rows = sum(rows for _, rows in plan[-1][0])
+        shapes.append(shape((len(entries), rows, arrays[0].shape[2]), jnp.bfloat16))
+    return pl.pallas_call(
+        partial(combine_kernel, plan),
+        grid=(1,),
+        in_specs=specs,
+        out_specs=[whole(out) for out in shapes],
+        out_shape=shapes,
+        compiler_params=params(),
+        cost_estimate=cost(0, 0),
+        name="combine",
+    )(*arrays)
 
 
 class Halving:
-    def __init__(self, *parts):
-        self.parts = [part.reshape(CHIPS, -1, part.shape[-1]) for part in parts]
-        self.middle = self.parts[0].shape[1] // 2
+    def __init__(self, chips):
+        self.chips = chips
+        self.middle = chips[0][0][0].shape[1] // 2
+
+    def terms(self, k, half, *more):
+        middle = self.middle
+        return [(array, e, middle, half) for array, e in self.chips[k]] + [
+            (array, e, middle, 0) for array, e in more
+        ]
 
     def total(self, k, half, *more):
         rows = slice(half * self.middle, (half + 1) * self.middle)
-        return sum(one.astype(jnp.float32) for one in [p[k, rows] for p in self.parts] + [*more])
-
-    def first(self):
-        depth = self.parts[0].shape[2]
-        block = (1, self.middle, depth)
-        top = pl.BlockSpec(block, lambda e: (2 * e + 1, 0, 0))
-        low = pl.BlockSpec(block, lambda e: (2 + e, 1, 0))
-        out = pl.BlockSpec(block, lambda e: (e, 0, 0))
-        count = len(self.parts)
-        return pl.pallas_call(
-            halves_kernel,
-            grid=(2,),
-            in_specs=[top] * count + [low] * count,
-            out_specs=[out, out],
-            out_shape=[shape((2, self.middle, depth), jnp.bfloat16)] * 2,
-            compiler_params=params(),
-            cost_estimate=cost(0, 0),
-            name="halves",
-        )(*self.parts, *self.parts)
-
-    def second(self, top, low):
-        self.got = top, low
-        return [
-            self.total(2, 0, top[1]).astype(jnp.bfloat16),
-            self.total(1, 1, low[1]).astype(jnp.bfloat16),
-        ]
+        parts = [array[e, rows] for array, e in self.chips[k]] + [*more]
+        return sum(one.astype(jnp.float32) for one in parts)
 
     def finish(self, top, low):
         return jnp.concatenate(
@@ -1300,39 +1331,26 @@
         )
 
 
-def seconds_kernel(*refs):
-    top_out, low_out = refs[-2:]
-    start = 0
-    ins = refs[:-2]
-    while ins:
-        (top, top_got, low, low_got), ins = (ins[0:2], ins[2], ins[3:5], ins[5]), ins[6:]
-        rows = top_got.shape[1]
-        for parts, got, out_ref in ((top, top_got, top_out), (low, low_got, low_out)):
-            total = sum(ref[0].astype(jnp.float32) for ref in (*parts, got))
-            out_ref[start : start + rows] = total.astype(jnp.bfloat16)
-        start += rows
+def both_cores(mine, other):
+    parts = [part.reshape(CHIPS, -1, part.shape[-1]) for part in (mine, other)]
+    return Halving([[(part, k) for part in parts] for k in range(CHIPS)])
+
+
+def firsts(*sums):
+    return combine(
+        [[one.terms(k, 0) for one in sums] for k in (1, 3)],
+        [[one.terms(k, 1) for one in sums] for k in (2, 3)],
+    )
 
 
 def seconds(*sums):
-    arrays, specs = [], []
     for one, top, low in sums:
         one.got = top, low
-        block = (1, one.middle, top.shape[2])
-        for k, half, got in ((2, 0, top), (1, 1, low)):
-            arrays += [*one.parts, got]
-            specs += [pl.BlockSpec(block, lambda i, k=k, half=half: (k, half, 0))] * 2
-            specs += [pl.BlockSpec(block, lambda i: (1, 0, 0))]
-    out = shape((sum(one[0].middle for one in sums), arrays[0].shape[2]), jnp.bfloat16)
-    return pl.pallas_call(
-        seconds_kernel,
-        grid=(1,),
-        in_specs=specs,
-        out_specs=[whole(out)] * 2,
-        out_shape=[out] * 2,
-        compiler_params=params(),
-        cost_estimate=cost(0, 0),
-        name="seconds",
-    )(*arrays)
+    top, low = combine(
+        [[one.terms(2, 0, (top, 1)) for one, top, _ in sums]],
+        [[one.terms(1, 1, (low, 1)) for one, _, low in sums]],
+    )
+    return top[0], low[0]
 
 
 def send_first(top, low):
@@ -1341,10 +1359,6 @@
 
 def send_last(top, low):
     return [exchange(top, 4), exchange(low, 2)]
-
-
-def merge(first, second):
-    return [jnp.concatenate(pair, axis=-2) for pair in zip(first, second)]
 
 
 def split_rows(arrays, rows):
@@ -1455,12 +1469,12 @@
     square_arrived = hold(send_dp(square), received)
     (received,) = hold([received], *square_arrived)
     received_sent = send_dp(received)
-    (contract,) = hold([contract_weight.astype(low)], received)
-    contract = [contract] + [exchange(contract, 2 * k) for k in range(1, CHIPS)]
-    slices_arrived = hold(received_sent, *contract[1:])
-    square_arrived = hold(square_arrived, *slices_arrived)
-    square = lax.all_gather(place_dp(square, square_arrived), "index", axis=0, tiled=False)
+    square = place_dp(square, square_arrived)
+    *slices_arrived, x, y, xy = hold([*received_sent, *to_chips(square)])
     slices = place_dp(received, slices_arrived)
+    square = [square, x, y, xy]
+    (contract,) = hold([contract_weight.astype(low)], x)
+    contract_sent = to_chips(contract)
     vectors = (
         slices[:, :, 5 * part :]
         .reshape(groups, count, extra_rows * width)[:, :, : vector_rows * vector_width]
@@ -1518,22 +1532,27 @@
     qkv_bias = jnp.concatenate([vector_here[0:1], no_bias, vector_here[1:2]], axis=1)
     kv_bias = jnp.concatenate([no_bias, vector_here[4:5]], axis=1)
     x_rows = decoder_input.reshape(rows, depth)
+    (slices,) = hold([slices], key_bias)
     qkv = project_columns("self_qkv", *input_rows, slices, 0, 3, qkv_bias)
+    qkv, *late_arrived = hold([qkv, *late_sent])
+    late = lax.all_gather(place_dp(late, late_arrived), "index", axis=0, tiled=False)
     self_out, self_stat = attend(True, qkv, 0, qkv, 1, 2, key_bias[:, None, :])
-    self_out, *late_arrived = hold([self_out, *late_sent])
+    self_out, *contract_sent = hold([self_out, *contract_sent])
+    contract = [contract, *contract_sent]
     self_got = swap(self_out)
-    late = lax.all_gather(place_dp(late, late_arrived), "index", axis=0, tiled=False)
-    ahead, across = hold([jnp.stack(contract[:2]), jnp.stack(contract[2:])], *late_arrived)
-    self_got, ahead_far, across_far, slices = hold(
-        [self_got, exchange_dp(ahead, 2), exchange_dp(across, 1), slices]
-    )
-    memory_kv = project_columns("memory_kv", *memory_rows, slices, 3, 2, kv_bias)
+    square = gather_index(hold(square, self_out))
+    ahead, across = hold([jnp.stack(contract[:2]), jnp.stack(contract[2:])], self_out)
+    self_got, ahead_far, across_far, square = hold(
+        [self_got, exchange_dp(ahead, 2), exchange_dp(across, 1), square]
+    )
     ahead = jnp.stack([ahead, ahead_far])
     across = jnp.stack([across, across_far])
     contract_sent = [exchange_dp(ahead, 1), exchange_dp(across, 2)]
     self_mixed, first_in, first_low, cross_query = first_forward(
-        self_got, x_rows, square, vectors, memory_kv
-    )
+        self_got, x_rows, square, vectors, ahead_far
+    )
+    (slices,) = hold([slices], first_low)
+    memory_kv = project_columns("memory_kv", *memory_rows, slices, 3, 2, kv_bias)
     cross_query = swap(cross_query)[:, None]
     cross_out, cross_stat = attend(
         False, cross_query, 0, memory_kv, 0, 1, key_bias[:, None, :]
@@ -1596,9 +1615,8 @@
     query_low, first_grad, self_low, self_mix_grad, first_stat = first_back(
         cross_dq_got, second_grad, first_in, square, vectors, memory_mine
     )
-    kv_far = HalvingDp(kv_grads)
-    memory_sum = Halving(memory_mine, exchange(memory_other, 1))
-    memory_sent = memory_sum.first()
+    memory_sum = both_cores(memory_mine, exchange(memory_other, 1))
+    memory_sent = firsts(memory_sum)
     square_mine, square_other = weight_grads(
         (count, groups, part, depth),
         order,
@@ -1609,8 +1627,8 @@
         cross_mixed,
         cross_low,
     )
-    square_sum = Halving(square_mine, exchange(square_other, 1))
-    square_sent = square_sum.first()
+    square_sum = both_cores(square_mine, exchange(square_other, 1))
+    square_sent = firsts(square_sum)
     self_mix_got, *contract_last = hold(
         [swap(self_mix_grad), *contract_last], *memory_sent, *square_sent
     )
@@ -1625,17 +1643,7 @@
     dx_mine, dx_other, qkv_slice_grads, qkv_total = project_columns_back(
         "self_qkv_back", order, *input_rows, [self_dq, self_dkv], slices, 0, 3
     )
-    dx_mine, dx_other, expand_got, *got = hold(
-        [dx_mine, dx_other, expand_got, *memory_got, *square_got]
-    )
-    dx_got = exchange(dx_other, 1)
-    square_rows = square_sum.middle
-    last = seconds((square_sum, *got[2:]), (memory_sum, *got[:2]))
-    qkv_slice_grads, qkv_total, kv_total, prior_rows, expand_got, *contract_last = hold(
-        [qkv_slice_grads, qkv_total, kv_total, prior_rows, expand_got, *contract_last], *last
-    )
-    last = send_last(*last)
-    expand_last = exchange_dp(expand_sum.second(expand_got), 2)
+    dx_mine, dx_other, *got = hold([dx_mine, dx_other, *memory_got, *square_got])
     own = jnp.concatenate(
         [qkv_total[:, :width], qkv_total[:, 2 * width :], kv_total[:, width:]], axis=0
     )
@@ -1670,35 +1678,43 @@
     slice_sum = HalvingDp(
         jnp.concatenate([qkv_slice_grads, kv_grads, vector_send.astype(low)], axis=2)
     )
-    slice_got = exchange_dp(slice_sum.first(), 1)
+    slice_sent = slice_sum.first()
+    slice_got = exchange_dp(slice_sent, 1)
+    dx_other, *got = hold([dx_other, *got], slice_sent)
+    dx_got = exchange(dx_other, 1)
+    square_rows = square_sum.middle
+    last = seconds((square_sum, *got[2:]), (memory_sum, *got[:2]))
+    prior_rows, expand_got, *contract_last = hold(
+        [prior_rows, expand_got, *contract_last], *last
+    )
+    last = send_last(*last)
+    expand_last = exchange_dp(expand_sum.second(expand_got), 2)
     prior_arrived = small_send(prior_rows.reshape(seqs, slots, MEM_P).sum(axis=-1))
-    dx_got, expand_last, prior_arrived, *last = hold(
-        [dx_got, expand_last, prior_arrived, *last]
-    )
+    dx_got, expand_last, prior_arrived, slice_got, *last = hold(
+        [dx_got, expand_last, prior_arrived, slice_got, *last]
+    )
+    slice_last = exchange_dp(slice_sum.second(slice_got), 2)
+    dx_sum = both_cores(dx_mine, dx_got)
+    contract_sum = Halving(
+        [
+            [(one.reshape((-1,) + one.shape[-2:]), k % 2) for one in parts]
+            for k, parts in enumerate(
+                [(ahead, cores[0], contract_got[0], contract_last[0])] * 2
+                + [(across, cores[2], contract_got[1], contract_last[1])] * 2
+            )
+        ]
+    )
+    dx_sent = firsts(dx_sum, contract_sum)
+    got = send_first(*dx_sent)
+    last = hold(last, *dx_sent)
     square_last, memory_last = split_rows(last, square_rows)
     square_far = HalvingDp(square_sum.finish(*square_last).reshape(groups, 3 * part, depth))
-    square_sent = square_far.first()
-    dx_sum = Halving(dx_mine, dx_got)
-    contract_sum = Halving(
-        jnp.concatenate(
-            [
-                add((one, 0), (core, 0), (got, 0), last)
-                for one, core, got, last in zip(
-                    (ahead, across), (cores[0], cores[2]), contract_got, contract_last
-                )
-            ],
-            axis=0,
-        )
-    )
-    got = send_first(*merge(dx_sum.first(), contract_sum.first()))
-    square_got = exchange_dp(square_sent, 1)
+    square_got = exchange_dp(square_far.first(), 1)
     memory_gradient = memory_sum.finish(*memory_last).reshape(encoder_memory.shape)
-    square_got, slice_got, *got = hold([square_got, slice_got, *got], memory_gradient)
+    square_got, slice_last, *got = hold([square_got, slice_last, *got], memory_gradient)
     dx_got, contract_got = split_rows(got, dx_sum.middle)
-    last = send_last(*merge(dx_sum.second(*dx_got), contract_sum.second(*contract_got)))
+    last = send_last(*seconds((dx_sum, *dx_got), (contract_sum, *contract_got)))
     square_last = exchange_dp(square_far.second(square_got), 2)
-    slice_last = exchange_dp(slice_sum.second(slice_got), 2)
-    slice_last, *last = hold([slice_last, *last])
     dx_last, contract_last = split_rows(last, dx_sum.middle)
     input_gradient = first_grad + dx_sum.finish(*dx_last)
     contract_sum = contract_sum.finish(*contract_last)

time: 521 us -> 545 us (1.046)
  local copies, waits for them, and re-layouts: 48.1 us -> 74 us
  waiting for transfers between devices: 103 us -> 115 us
  starting transfers between devices: 92.9 us -> 82.2 us
    dynamic_update_slice x0 -> x8, local copies, waits for them, and re-layouts: none -> 11 us  [the longest x4 7.58 us: gather_index(): lax.dynamic_update_index_in_dim(result, other[k], me ^ 2 * k ^ 1, 0)]
    ppermute x9, starting transfers between devices: 21.4 us -> 12.6 us  [send_dp(): lax.ppermute(piece, 'dp', [(i, (i + shift) % size) for i in range(size)])]
    slice x0 -> x4, local copies, waits for them, and re-layouts: none -> 6.2 us  [the longest x2 3.81 us: split_rows(): a[..., :rows, :]]
    pallas_call x6 -> x4, Pallas kernels: 15.4 us -> 10.2 us  [add(): pl.pallas_call(add_kernel, grid=(rows // block,), in_specs=specs, out_spe...]
    ppermute x24 -> x28, waiting for transfers between devices: 18.1 us -> 22.6 us  [exchange(): return lax.ppermute(piece, 'index', [(i, i ^ flip) for i in range(size)])]
    unnamed x190 -> x186, local copies, waits for them, and re-layouts: 26 us -> 24.8 us
    ppermute x24 -> x28, starting transfers between devices: 19.1 us -> 20 us  [exchange(): return lax.ppermute(piece, 'index', [(i, i ^ flip) for i in range(size)])]
  transfers between devices with their start and end apart: 60 -> 63, of which waited for: 22 -> 24; matrix products, arithmetic and copies ran while one was open for 12% -> 15% of each run, Pallas kernels for 32% -> 29%
where the time goes in v3:
time: 545 us; the launch traced here: 534 us
  Pallas kernels  186 us (34%)
  waiting for transfers between devices  115 us (21%)
  starting transfers between devices  82.2 us (15%)
  local copies, waits for them, and re-layouts  74 us (14%)
  other arithmetic  52.8 us (10%)
  between operations  15.4 us (3%)
  blocking collectives  9.21 us (2%)
    ppermute x14, waiting for transfers between devices, exchange_dp(): return lax.ppermute(piece, 'dp', [(i, i ^ flip) for i in range(size)])  44.6 us
    pallas_call x2, Pallas kernels, attend_back(): pl.pallas_call(partial(attend_backward_kernel, causal, head_width), grid=...  41.3 us
    all_to_all x9, starting transfers between devices, swap(): return lax.all_to_all(pieces, 'index', 0, 0, tiled=True)  34.6 us
    all_to_all x9, waiting for transfers between devices, swap(): return lax.all_to_all(pieces, 'index', 0, 0, tiled=True)  30.8 us
    pallas_call x2, Pallas kernels, attend(): pl.pallas_call(partial(attend_forward_kernel, causal, head_width), grid=(...  29.8 us
    pallas_call x1, Pallas kernels, ffn(): pl.pallas_call(ffn_kernel, grid_spec=pltpu.PrefetchScalarGridSpec(num_sca...  26.4 us
    pallas_call x2, Pallas kernels, project_columns_back(): pl.pallas_call(partial(columns_back_kernel, first), grid_spec=pltpu.Prefe...  25.7 us
    unnamed x186, local copies, waits for them, and re-layouts  24.8 us
  transfers between devices with their start and end apart: 63, of which 24 were waited for; matrix products, arithmetic and copies ran while one was open for 15% of the time, Pallas kernels for 29%

profile of v3, /device:TPU:0, one launch (start us, length us, event | category | flops | bytes accessed | tf_op | source)
XLA Modules:
  0.0 534.2 jit_solution(1602063887914802103)
XLA Ops:
  11.4 3.1 collective-permute-start
  19.6 3.7 all-to-all-start
  25.7 9.8 %all-to-all-done.__3_.__0_ = bf16[8,176,128]{2,1,0:T(8,128)(2,1)S(1)} async-done(((bf16[8,176,128]{2,1,0:T(8,128)(2,1)}), bf16[8,176,128]{2,1,0:T(8,128)(2,1)S(1)}, u32[]{:S(2)}, u32[]{:S(2)}) %all-to-all-start) | async-done | bytes 360480 | tf_op jit(solution)/shard_map/all_to_all | solution.py:1398
  50.4 10.9 %collective-permute-done.4.__1_ = bf16[8,176,128]{2,1,0:T(8,128)(2,1)} collective-permute-done((bf16[8,176,128]{2,1,0:T(8,128)(2,1)}, bf16[8,176,128]{2,1,0:T(8,128)(2,1)}, u32[]{:S(2)}, u32[]{:S(2)}) %collective-permute-start.4) | collective-permute-done | bytes 360480 | tf_op jit(solution)/shard_map/ppermute | solution.py:1176
  61.6 16.4 %collective-permute-done.8.__5_ = bf16[4,32,2048]{2,1,0:T(8,128)(2,1)S(1)} collective-permute-done((bf16[4,32,2048]{2,1,0:T(8,128)(2,1)S(1)}, bf16[4,32,2048]{2,1,0:T(8,128)(2,1)S(1)}, u32[]{:S(2)}, u32[]{:S(2)}) %collective-permute-start.8) | collective-permute-done | bytes 524320 | tf_op jit(solution)/shard_map/ppermute | solution.py:1233
  87.0 4.2 gather_fusion
  92.8 3.3 all-to-all-start.1
  97.0 4.2 all-to-all-done.1
  105.6 8.2 %self_qkv.1.__0_ = bf16[8,3,2,128,128]{4,3,2,1,0:T(8,128)(2,1)} custom-call(bf16[8,2,384,1024]{3,2,1,0:T(8,128)(2,1)} %bitcast.218, bf16[4,8,176,128]{3,2,1,0:T(8,128)(2,1)} %hold.29.slice_ref.__0_, f32[1,384]{1,0:T(1,128)} %fusion.15.bias_ref), custom_call_target="tpu_custom_call" | custom-call | flops 100663296 | bytes 262144 | tf_op jit(solution)/shard_map/self_qkv/pallas_call | solution.py:709
  122.9 10.2 %attend_self.1 = (bf16[8,2,128,128]{3,2,1,0:T(8,128)(2,1)}, f32[2,2,1024]{2,1,0:T(2,128)}) custom-call(bf16[8,3,2,128,128]{4,3,2,1,0:T(8,128)(2,1)} %get-tuple-element.146.q_ref.k_ref.v_ref, bf16[8,3,2,128,128]{4,3,2,1,0:T(8,128)(2,1)} %get-tuple-element.146.q_ref.k_ref.v_ref, bf16[8,3,2,128,128]{4,3,2,1,0:T(8,128)(2,1)} %get-tuple-element.146.q_ref.k_ref.v_ref, ...), custom_call_target="tpu_custom_call" | custom-call | flops 268435456 | bytes 131072 | tf_op jit(solution)/shard_map/attend_self/pallas_call | solution.py:606
  133.6 5.7 %collective-permute-done.14.__3_ = bf16[128,1024]{1,0:T(8,128)(2,1)S(1)} collective-permute-done((bf16[128,1024]{1,0:T(8,128)(2,1)}, bf16[128,1024]{1,0:T(8,128)(2,1)S(1)}, u32[]{:S(2)}, u32[]{:S(2)}) %collective-permute-start.14) | collective-permute-done | bytes 262176 | tf_op jit(solution)/shard_map/ppermute | solution.py:1233
  140.0 3.2 pad_maximum_fusion
  143.3 5.2 all-to-all-start.2
  165.1 11.8 %collective-permute-done.15.__1_ = bf16[2,128,1024]{2,1,0:T(8,128)(2,1)S(1)} collective-permute-done((bf16[2,128,1024]{2,1,0:T(8,128)(2,1)}, bf16[2,128,1024]{2,1,0:T(8,128)(2,1)S(1)}, u32[]{:S(2)}, u32[]{:S(2)}) %collective-permute-start.15) | collective-permute-done | bytes 524320 | tf_op jit(solution)/shard_map/ppermute | solution.py:1238
  182.8 5.0 first_forward.1
  187.7 3.8 all-to-all-start.3
  192.7 9.0 %memory_kv.1.k_ref.v_ref = bf16[8,2,2,240,128]{4,3,2,1,0:T(8,128)(2,1)} custom-call(bf16[8,2,384,1024]{3,2,1,0:T(8,128)(2,1)} %bitcast.219, bf16[4,8,176,128]{3,2,1,0:T(8,128)(2,1)} %hold.37.slice_ref.refs_1_.refs_2_, f32[1,256]{1,0:T(1,128)} %concatenate.81.bias_ref), custom_call_target="tpu_custom_call" | custom-call | flops 125829120 | bytes 491520 | tf_op jit(solution)/shard_map/memory_kv/pallas_call | solution.py:709
  202.5 19.6 %attend_memory.1 = (bf16[8,2,128,128]{3,2,1,0:T(8,128)(2,1)}, f32[2,2,1024]{2,1,0:T(2,128)}) custom-call(bf16[8,1,2,128,128]{4,3,2,1,0:T(8,128)(2,1)} %bitcast.286, bf16[8,2,2,240,128]{4,3,2,1,0:T(8,128)(2,1)} %memory_kv.1.k_ref.v_ref, bf16[8,2,2,240,128]{4,3,2,1,0:T(8,128)(2,1)} %memory_kv.1.k_ref.v_ref, f32[2,1,1920]{2,1,0:T(1,128)} %broadcast_in_dim_reshape.6.bias_ref), custom_call_target="tpu_custom_call" | custom-call | flops 503316480 | bytes 188416 | tf_op jit(solution)/shard_map/attend_memory/pallas_call | solution.py:606
  222.1 4.7 collective-permute-done.19.__1_
  228.3 3.5 all-to-all-start.4
  233.9 7.6 %all-to-all-done.4.mixed_ref = bf16[8,2,128,128]{3,2,1,0:T(8,128)(2,1)S(1)} async-done(((bf16[8,2,128,128]{3,2,1,0:T(8,128)(2,1)}), bf16[8,2,128,128]{3,2,1,0:T(8,128)(2,1)S(1)}, u32[]{:S(2)}, u32[]{:S(2)}) %all-to-all-start.4) | async-done | bytes 524320 | tf_op jit(solution)/shard_map/all_to_all | solution.py:1398
  242.3 26.4 %ffn.1 = (bf16[256,1024]{1,0:T(8,128)(2,1)}, bf16[256,1024]{1,0:T(8,128)(2,1)}, bf16[8,4,128,1024]{3,2,1,0:T(8,128)(2,1)}, bf16[2,2,128,1024]{3,2,1,0:T(8,128)(2...) custom-call(s32[8]{0:T(128)} %pad_add_fusion.order._, ...), custom_call_target="tpu_custom_call" | custom-call | flops 805306368 | bytes 4194304 | tf_op jit(solution)/shard_map/ffn/pallas_call | solution.py:1013
  269.4 3.5 all-to-all-start.5
  286.3 29.3 %attend_memory_back.1 = (bf16[8,2,128,128]{3,2,1,0:T(8,128)(2,1)}, bf16[8,2,2,240,128]{4,3,2,1,0:T(8,128)(2,1)}, f32[2,1,1920]{2,1,0:T(1,128)}) custom-call(bf16[8,1,2,128,128]{4,3,2,1,0:T(8,128)(2,1)} %bitcast.287, bf16[8,2,2,240,128]{4,3,2,1,0:T(8,128)(2,1)} %memory_kv.1.k_ref.v_ref, bf16[8,2,2,240,128]{4,3,2,1,0:T(8,128)(2,1)} %memory_kv.1.k_ref.v_ref, ...), custom_call_target="tpu_custom_call" | custom-call | flops 1258291200 | bytes 376832 | tf_op jit(solution)/shard_map/attend_memory_back/pallas_call | solution.py:642
  315.6 13.7 %memory_kv_back.1 = (bf16[4,1,480,1024]{3,2,1,0:T(8,128)(2,1)}, bf16[4,1,480,1024]{3,2,1,0:T(8,128)(2,1)}, bf16[4,8,64,128]{3,2,1,0:T(8,128)(2,1)}, f32[1,256]{1,0:T(1,128)}) custom-call(s32[8]{0:T(128)} %pad_add_fusion.order._, bf16[8,2,384,1024]{3,2,1,0:T(8,128)(2,1)} %bitcast.220, bf16[8,2,2,240,128]{4,3,2,1,0:T(8,128)(2,1)} %get-tuple-element.185.refs_0_, ...), custom_call_target="tpu_custom_call" | custom-call | flops 251658240 | bytes 983040 | tf_op jit(solution)/shard_map/memory_kv_back/pallas_call | solution.py:791
  331.4 3.8 all-to-all-start.6
  340.9 4.0 all-to-all-done.6.__0_
  345.8 5.7 %first_back.1 = (bf16[256,1024]{1,0:T(8,128)(2,1)}, f32[256,1024]{1,0:T(8,128)}, bf16[256,1024]{1,0:T(8,128)(2,1)}, bf16[8,2,128,128]{3,2,1,0:T(8,128)(2,1)}, f32[8,1024]{1,0:T(8,128)}) custom-call(bf16[8,2,128,128]{3,2,1,0:T(8,128)(2,1)} %get-tuple-element.194.dq_ref, f32[256,1024]{1,0:T(8,128)} %get-tuple-element.195.second_grad, ...), custom_call_target="tpu_custom_call" | custom-call | flops 67108864 | bytes 262144 | tf_op jit(solution)/shard_map/first_back/pallas_call | solution.py:1100
  351.5 7.1 %weight_grads.1 = (bf16[4,4,96,1024]{3,2,1,0:T(8,128)(2,1)}, bf16[4,4,96,1024]{3,2,1,0:T(8,128)(2,1)}) custom-call(s32[8]{0:T(128)} %pad_add_fusion.order._, bf16[256,1024]{1,0:T(8,128)(2,1)} %get-tuple-element.203.mixed, bf16[256,1024]{1,0:T(8,128)(2,1)} %get-tuple-element.204.self_low, bf16[256,1024]{1,0:T(8,128)(2,1)} %get-tuple-element.165.__1_.first_low, ...), custom_call_target="tpu_custom_call" | custom-call | flops 100663296 | bytes 393216 | tf_op jit(solution)/shard_map/weight_grads/pallas_call | solution.py:1157
  360.7 4.2 all-to-all-start.7
  365.8 3.6 combine.5
  374.4 3.2 combine.6
  378.2 6.3 %collective-permute-done.30.__1_ = bf16[2,128,1024]{2,1,0:T(8,128)(2,1)} collective-permute-done((bf16[2,128,1024]{2,1,0:T(8,128)(2,1)}, bf16[2,128,1024]{2,1,0:T(8,128)(2,1)}, u32[]{:S(2)}, u32[]{:S(2)}) %collective-permute-start.30) | collective-permute-done | bytes 524320 | tf_op jit(solution)/shard_map/ppermute | solution.py:1238
  385.0 12.0 %attend_self_back.1 = (bf16[8,2,128,128]{3,2,1,0:T(8,128)(2,1)}, bf16[8,2,2,128,128]{4,3,2,1,0:T(8,128)(2,1)}, f32[2,1,1024]{2,1,0:T(1,128)}) custom-call(bf16[8,3,2,128,128]{4,3,2,1,0:T(8,128)(2,1)} %get-tuple-element.146.q_ref.k_ref.v_ref, bf16[8,3,2,128,128]{4,3,2,1,0:T(8,128)(2,1)} %get-tuple-element.146.q_ref.k_ref.v_ref, ...), custom_call_target="tpu_custom_call" | custom-call | flops 671088640 | bytes 262144 | tf_op jit(solution)/shard_map/attend_self_back/pallas_call | solution.py:642
  398.9 12.0 %self_qkv_back.1 = (bf16[4,1,256,1024]{3,2,1,0:T(8,128)(2,1)}, bf16[4,1,256,1024]{3,2,1,0:T(8,128)(2,1)}, bf16[4,8,96,128]{3,2,1,0:T(8,128)(2,1)}, f32[1,384]{1,0:T(1,128)}) custom-call(s32[8]{0:T(128)} %pad_add_fusion.order._, bf16[8,2,384,1024]{3,2,1,0:T(8,128)(2,1)} %bitcast.221, bf16[8,2,128,128]{3,2,1,0:T(8,128)(2,1)} %get-tuple-element.216.refs_0_, ...), custom_call_target="tpu_custom_call" | custom-call | flops 201326592 | bytes 524288 | tf_op jit(solution)/shard_map/self_qkv_back/pallas_call | solution.py:791
  417.5 4.0 combine.7
  425.5 6.9 %collective-permute-done.39.__1_ = bf16[2,128,1024]{2,1,0:T(8,128)(2,1)} collective-permute-done((bf16[2,128,1024]{2,1,0:T(8,128)(2,1)S(1)}, bf16[2,128,1024]{2,1,0:T(8,128)(2,1)}, u32[]{:S(2)}, u32[]{:S(2)}) %collective-permute-start.39) | collective-permute-done | bytes 524320 | tf_op jit(solution)/shard_map/ppermute | solution.py:1238
  435.4 9.2 %all_to_all.50.__2_ = f32[8,8,128]{2,1,0:T(8,128)} all-to-all(f32[8,8,128]{2,1,0:T(8,128)S(1)} %broadcast_in_dim.131), channel_id=1, replica_groups=mesh['dp'=4,'index'=8] {'index'}, dimensions={0} | all-to-all | bytes 65536 | tf_op jit(solution)/shard_map/all_to_all | solution.py:1398
  444.6 7.6 %collective-permute-done.41.__3_ = bf16[2,8,176,128]{3,2,1,0:T(8,128)(2,1)} collective-permute-done((bf16[2,8,176,128]{3,2,1,0:T(8,128)(2,1)}, bf16[2,8,176,128]{3,2,1,0:T(8,128)(2,1)}, u32[]{:S(2)}, u32[]{:S(2)}) %collective-permute-start.41) | collective-permute-done | bytes 720928 | tf_op jit(solution)/shard_map/ppermute | solution.py:1238
  454.6 3.6 combine.8
  458.2 4.3 bitcast_add_fusion.1
  477.7 2.9 multiply_subtract_fusion.2
  481.9 3.0 pad_maximum_fusion.1
  494.6 3.0 combine.9
  504.5 3.4 all-to-all-start.9
  508.0 3.1 collective-permute-done.50
  513.0 2.9 all-to-all-done.9
  517.5 3.8 multiply_subtract_fusion
  (498 shorter events, 173.0 us)
Async XLA Ops:
  7.2 98.4 %all-gather.6.cloned.1.call-start = ((), (), s32[]{:S(2)}) async-start(), calls=%async_computation.13 | async-start | bytes 14155776 | tf_op jit(solution)/shard_map/all_gather | solution.py:1453
  19.6 15.8 %all-to-all-start = ((bf16[8,176,128]{2,1,0:T(8,128)(2,1)}), bf16[8,176,128]{2,1,0:T(8,128)(2,1)S(1)}, u32[]{:S(2)}, u32[]{:S(2)}) async-start(bf16[8,176,128]{2,1,0:T(8,128)(2,1)} %pad_maximum_fusion.12), calls=%async_computation | async-start | bytes 720896 | tf_op jit(solution)/shard_map/all_to_all | solution.py:1398
  39.4 22.2 %collective-permute-start.6 = (bf16[4,32,2048]{2,1,0:T(8,128)(2,1)S(1)}, bf16[4,32,2048]{2,1,0:T(8,128)(2,1)S(1)}, u32[]{:S(2)}, u32[]{:S(2)}) collective-permute-start(bf16[4,32,2048]{2,1,0:T(8,128)(2,1)S(1)} %bitcast_dynamic-update-slice_fusion.9.__0_), channel_id=1, source_target_pairs={{0,2},{1,3},{2,0},{3,1},{4,6},{5,7},{6,4},{7,5},{8,10},{9,11},{10,... | collective-permute-start | bytes 1572872 | tf_op jit(solution)/shard_map/ppermute | solution.py:1233
  39.5 22.1 %collective-permute-start.7 = (bf16[4,32,2048]{2,1,0:T(8,128)(2,1)S(1)}, bf16[4,32,2048]{2,1,0:T(8,128)(2,1)S(1)}, u32[]{:S(2)}, u32[]{:S(2)}) collective-permute-start(bf16[4,32,2048]{2,1,0:T(8,128)(2,1)S(1)} %bitcast_dynamic-update-slice_fusion.9.__0_), channel_id=1, source_target_pairs={{0,4},{1,5},{2,6},{3,7},{4,0},{5,1},{6,2},{7,3},{8,12},{9,13},{10,... | collective-permute-start | bytes 1572872 | tf_op jit(solution)/shard_map/ppermute | solution.py:1233
  40.6 37.4 %collective-permute-start.8 = (bf16[4,32,2048]{2,1,0:T(8,128)(2,1)S(1)}, bf16[4,32,2048]{2,1,0:T(8,128)(2,1)S(1)}, u32[]{:S(2)}, u32[]{:S(2)}) collective-permute-start(bf16[4,32,2048]{2,1,0:T(8,128)(2,1)S(1)} %bitcast_dynamic-update-slice_fusion.9.__0_), channel_id=1, source_target_pairs={{0,6},{1,7},{2,4},{3,5},{4,2},{5,3},{6,0},{7,1},{8,14},{9,15},{10,... | collective-permute-start | bytes 1572872 | tf_op jit(solution)/shard_map/ppermute | solution.py:1233
  44.5 16.8 %collective-permute-start.4 = (bf16[8,176,128]{2,1,0:T(8,128)(2,1)}, bf16[8,176,128]{2,1,0:T(8,128)(2,1)}, u32[]{:S(2)}, u32[]{:S(2)}) collective-permute-start(bf16[8,176,128]{2,1,0:T(8,128)(2,1)} %hold.26), channel_id=1, source_target_pairs={{0,16},{8,24},{16,0},{24,8},{1,17},{9,25},{17,1},{25,9},{2,18},{10... | collective-permute-start | bytes 1081352 | tf_op jit(solution)/shard_map/ppermute | solution.py:1176
  46.7 14.8 %collective-permute-start.5 = (bf16[8,176,128]{2,1,0:T(8,128)(2,1)}, bf16[8,176,128]{2,1,0:T(8,128)(2,1)}, u32[]{:S(2)}, u32[]{:S(2)}) collective-permute-start(bf16[8,176,128]{2,1,0:T(8,128)(2,1)} %hold.26), channel_id=1, source_target_pairs={{0,24},{8,0},{16,8},{24,16},{1,25},{9,1},{17,9},{25,17},{2,26},{10... | collective-permute-start | bytes 1081352 | tf_op jit(solution)/shard_map/ppermute | solution.py:1176
  78.8 35.0 %collective-permute-start.10 = (bf16[160,1024]{1,0:T(8,128)(2,1)}, bf16[160,1024]{1,0:T(8,128)(2,1)}, u32[]{:S(2)}, u32[]{:S(2)}) collective-permute-start(bf16[160,1024]{1,0:T(8,128)(2,1)} %hold.30), channel_id=1, source_target_pairs={{0,16},{8,24},{16,0},{24,8},{1,17},{9,25},{17,1},{25,9},{2,18},{10... | collective-permute-start | bytes 983048 | tf_op jit(solution)/shard_map/ppermute | solution.py:1176
  80.1 33.7 %collective-permute-start.11 = (bf16[160,1024]{1,0:T(8,128)(2,1)}, bf16[160,1024]{1,0:T(8,128)(2,1)}, u32[]{:S(2)}, u32[]{:S(2)}) collective-permute-start(bf16[160,1024]{1,0:T(8,128)(2,1)} %hold.30), channel_id=1, source_target_pairs={{0,24},{8,0},{16,8},{24,16},{1,25},{9,1},{17,9},{25,17},{2,26},{10... | collective-permute-start | bytes 983048 | tf_op jit(solution)/shard_map/ppermute | solution.py:1176
  82.6 31.2 %collective-permute-start.9 = (bf16[160,1024]{1,0:T(8,128)(2,1)}, bf16[160,1024]{1,0:T(8,128)(2,1)}, u32[]{:S(2)}, u32[]{:S(2)}) collective-permute-start(bf16[160,1024]{1,0:T(8,128)(2,1)} %hold.30), channel_id=1, source_target_pairs={{0,8},{8,16},{16,24},{24,0},{1,9},{9,17},{17,25},{25,1},{2,10},{10... | collective-permute-start | bytes 983048 | tf_op jit(solution)/shard_map/ppermute | solution.py:1176
  96.2 145.4 %all-gather.4.cloned.1.call-start = ((), (), s32[]{:S(2)}) async-start(), calls=%async_computation.11 | async-start | bytes 11796480 | tf_op jit(solution)/shard_map/all_gather | solution.py:1538
  118.7 14.4 %collective-permute-start.12 = (bf16[128,1024]{1,0:T(8,128)(2,1)}, bf16[128,1024]{1,0:T(8,128)(2,1)S(1)}, u32[]{:S(2)}, u32[]{:S(2)}) collective-permute-start(bf16[128,1024]{1,0:T(8,128)(2,1)} %hold.32), channel_id=1, source_target_pairs={{0,2},{1,3},{2,0},{3,1},{4,6},{5,7},{6,4},{7,5},{8,10},{9,11},{10,... | collective-permute-start | bytes 786440 | tf_op jit(solution)/shard_map/ppermute | solution.py:1233
  119.8 13.7 %collective-permute-start.13 = (bf16[128,1024]{1,0:T(8,128)(2,1)}, bf16[128,1024]{1,0:T(8,128)(2,1)S(1)}, u32[]{:S(2)}, u32[]{:S(2)}) collective-permute-start(bf16[128,1024]{1,0:T(8,128)(2,1)} %hold.32), channel_id=1, source_target_pairs={{0,4},{1,5},{2,6},{3,7},{4,0},{5,1},{6,2},{7,3},{8,12},{9,13},{10,... | collective-permute-start | bytes 786440 | tf_op jit(solution)/shard_map/ppermute | solution.py:1233
  120.4 18.9 %collective-permute-start.14 = (bf16[128,1024]{1,0:T(8,128)(2,1)}, bf16[128,1024]{1,0:T(8,128)(2,1)S(1)}, u32[]{:S(2)}, u32[]{:S(2)}) collective-permute-start(bf16[128,1024]{1,0:T(8,128)(2,1)} %hold.32), channel_id=1, source_target_pairs={{0,6},{1,7},{2,4},{3,5},{4,2},{5,3},{6,0},{7,1},{8,14},{9,15},{10,... | collective-permute-start | bytes 786440 | tf_op jit(solution)/shard_map/ppermute | solution.py:1233
  143.3 21.8 %all-to-all-start.2 = ((bf16[8,2,128,128]{3,2,1,0:T(8,128)(2,1)}), bf16[8,2,128,128]{3,2,1,0:T(8,128)(2,1)S(1)}, u32[]{:S(2)}, u32[]{:S(2)}) async-start(bf16[8,2,128,128]{3,2,1,0:T(8,128)(2,1)} %get-tuple-element.149.__2_.__4_), calls=%async_computation.2 | async-start | bytes 1048576 | tf_op jit(solution)/shard_map/all_to_all | solution.py:1398
  150.2 26.7 %collective-permute-start.15 = (bf16[2,128,1024]{2,1,0:T(8,128)(2,1)}, bf16[2,128,1024]{2,1,0:T(8,128)(2,1)S(1)}, u32[]{:S(2)}, u32[]{:S(2)}) collective-permute-start(bf16[2,128,1024]{2,1,0:T(8,128)(2,1)} %get-tuple-element.153), channel_id=1, source_target_pairs={{0,16},{8,24},{16,0},{24,8},{1,17},{9,25},{17,1},{25,9},{2,18},{10... | collective-permute-start | bytes 1572872 | tf_op jit(solution)/shard_map/ppermute | solution.py:1238
  150.2 26.7 %collective-permute-start.16 = (bf16[2,128,1024]{2,1,0:T(8,128)(2,1)}, bf16[2,128,1024]{2,1,0:T(8,128)(2,1)S(1)}, u32[]{:S(2)}, u32[]{:S(2)}) collective-permute-start(bf16[2,128,1024]{2,1,0:T(8,128)(2,1)} %get-tuple-element.154), channel_id=1, source_target_pairs={{0,8},{8,0},{16,24},{24,16},{1,9},{9,1},{17,25},{25,17},{2,10},{10... | collective-permute-start | bytes 1572872 | tf_op jit(solution)/shard_map/ppermute | solution.py:1238
  179.8 47.0 %collective-permute-start.19 = (bf16[2,2,128,1024]{3,2,1,0:T(8,128)(2,1)S(1)}, bf16[2,2,128,1024]{3,2,1,0:T(8,128)(2,1)}, u32[]{:S(2)}, u32[]{:S(2)}) collective-permute-start(bf16[2,2,128,1024]{3,2,1,0:T(8,128)(2,1)S(1)} %pad_maximum_fusion.4.refs_2_), channel_id=1, source_target_pairs={{0,16},{8,24},{16,0},{24,8},{1,17},{9,25},{17,1},{25,9},{2,18},{10... | collective-permute-start | bytes 3145736 | tf_op jit(solution)/shard_map/ppermute | solution.py:1238
  180.6 47.2 %collective-permute-start.18 = (bf16[2,2,128,1024]{3,2,1,0:T(8,128)(2,1)S(1)}, bf16[2,2,128,1024]{3,2,1,0:T(8,128)(2,1)}, u32[]{:S(2)}, u32[]{:S(2)}) collective-permute-start(bf16[2,2,128,1024]{3,2,1,0:T(8,128)(2,1)S(1)} %pad_maximum_fusion.3.refs_0_), channel_id=1, source_target_pairs={{0,8},{8,0},{16,24},{24,16},{1,9},{9,1},{17,25},{25,17},{2,10},{10... | collective-permute-start | bytes 3145736 | tf_op jit(solution)/shard_map/ppermute | solution.py:1238
  187.7 14.0 %all-to-all-start.3 = ((bf16[8,2,128,128]{3,2,1,0:T(8,128)(2,1)}), bf16[8,2,128,128]{3,2,1,0:T(8,128)(2,1)S(1)}, u32[]{:S(2)}, u32[]{:S(2)}) async-start(bf16[8,2,128,128]{3,2,1,0:T(8,128)(2,1)} %get-tuple-element.164), calls=%async_computation.3 | async-start | bytes 1048576 | tf_op jit(solution)/shard_map/all_to_all | solution.py:1398
  192.1 49.4 %collective-permute-start.22 = (bf16[2,2,128,1024]{3,2,1,0:T(8,128)(2,1)S(1)}, bf16[2,2,128,1024]{3,2,1,0:T(8,128)(2,1)}, u32[]{:S(2)}, u32[]{:S(2)}) collective-permute-start(bf16[2,2,128,1024]{3,2,1,0:T(8,128)(2,1)S(1)} %pad_maximum_fusion.4.refs_2_), channel_id=1, source_target_pairs={{0,1},{1,0},{2,3},{3,2},{4,5},{5,4},{6,7},{7,6},{8,9},{9,8},{10,11... | collective-permute-start | bytes 3145736 | tf_op jit(solution)/shard_map/ppermute | solution.py:1233
  192.6 48.9 %collective-permute-start.20 = (bf16[2,2,128,1024]{3,2,1,0:T(8,128)(2,1)S(1)}, bf16[2,2,128,1024]{3,2,1,0:T(8,128)(2,1)}, u32[]{:S(2)}, u32[]{:S(2)}) collective-permute-start(bf16[2,2,128,1024]{3,2,1,0:T(8,128)(2,1)S(1)} %pad_maximum_fusion.3.refs_0_), channel_id=1, source_target_pairs={{0,1},{1,0},{2,3},{3,2},{4,5},{5,4},{6,7},{7,6},{8,9},{9,8},{10,11... | collective-permute-start | bytes 3145736 | tf_op jit(solution)/shard_map/ppermute | solution.py:1233
  231.8 165.1 %reduce-scatter.2.cloned.1.call-start = ((), (), s32[]{:S(2)}) async-start(), calls=%async_computation.12 | async-start | bytes 9437184 | tf_op jit(solution)/shard_map/reduce_scatter | solution.py:1586
  283.4 46.1 %collective-permute-start.26 = (bf16[2,2,128,1024]{3,2,1,0:T(8,128)(2,1)}, bf16[2,2,128,1024]{3,2,1,0:T(8,128)(2,1)S(1)}, u32[]{:S(2)}, u32[]{:S(2)}) collective-permute-start(bf16[2,2,128,1024]{3,2,1,0:T(8,128)(2,1)} %get-tuple-element.182._), channel_id=1, source_target_pairs={{0,8},{8,0},{16,24},{24,16},{1,9},{9,1},{17,25},{25,17},{2,10},{10... | collective-permute-start | bytes 3145736 | tf_op jit(solution)/shard_map/ppermute | solution.py:1238
  283.5 46.9 %collective-permute-start.27 = (bf16[2,2,128,1024]{3,2,1,0:T(8,128)(2,1)}, bf16[2,2,128,1024]{3,2,1,0:T(8,128)(2,1)S(1)}, u32[]{:S(2)}, u32[]{:S(2)}) collective-permute-start(bf16[2,2,128,1024]{3,2,1,0:T(8,128)(2,1)} %get-tuple-element.184), channel_id=1, source_target_pairs={{0,16},{8,24},{16,0},{24,8},{1,17},{9,25},{17,1},{25,9},{2,18},{10... | collective-permute-start | bytes 3145736 | tf_op jit(solution)/shard_map/ppermute | solution.py:1238
  285.7 49.5 %collective-permute-start.29 = (bf16[2,2,128,1024]{3,2,1,0:T(8,128)(2,1)}, bf16[2,2,128,1024]{3,2,1,0:T(8,128)(2,1)S(1)}, u32[]{:S(2)}, u32[]{:S(2)}) collective-permute-start(bf16[2,2,128,1024]{3,2,1,0:T(8,128)(2,1)} %get-tuple-element.192), channel_id=1, source_target_pairs={{0,1},{1,0},{2,3},{3,2},{4,5},{5,4},{6,7},{7,6},{8,9},{9,8},{10,11... | collective-permute-start | bytes 3145736 | tf_op jit(solution)/shard_map/ppermute | solution.py:1233
  285.7 52.8 %collective-permute-start.28 = (bf16[2,2,128,1024]{3,2,1,0:T(8,128)(2,1)}, bf16[2,2,128,1024]{3,2,1,0:T(8,128)(2,1)}, u32[]{:S(2)}, u32[]{:S(2)}) collective-permute-start(bf16[2,2,128,1024]{3,2,1,0:T(8,128)(2,1)} %get-tuple-element.189), channel_id=1, source_target_pairs={{0,1},{1,0},{2,3},{3,2},{4,5},{5,4},{6,7},{7,6},{8,9},{9,8},{10,11... | collective-permute-start | bytes 3145736 | tf_op jit(solution)/shard_map/ppermute | solution.py:1233
  329.3 36.5 %collective-permute-start.32 = (bf16[4,1,480,1024]{3,2,0,1:T(8,128)(2,1)}, bf16[4,1,480,1024]{3,2,0,1:T(8,128)(2,1)}, u32[]{:S(2)}, u32[]{:S(2)}) collective-permute-start(bf16[4,1,480,1024]{3,2,0,1:T(8,128)(2,1)} %bitcast.331), channel_id=1, source_target_pairs={{0,1},{1,0},{2,3},{3,2},{4,5},{5,4},{6,7},{7,6},{8,9},{9,8},{10,11... | collective-permute-start | bytes 11796488 | tf_op jit(solution)/shard_map/ppermute | solution.py:1233
  358.6 14.2 %collective-permute-start.33 = (bf16[4,4,96,1024]{3,2,1,0:T(8,128)(2,1)}, bf16[4,4,96,1024]{3,2,1,0:T(8,128)(2,1)S(1)}, u32[]{:S(2)}, u32[]{:S(2)}) collective-permute-start(bf16[4,4,96,1024]{3,2,1,0:T(8,128)(2,1)} %get-tuple-element.209), channel_id=1, source_target_pairs={{0,1},{1,0},{2,3},{3,2},{4,5},{5,4},{6,7},{7,6},{8,9},{9,8},{10,11... | collective-permute-start | bytes 9437192 | tf_op jit(solution)/shard_map/ppermute | solution.py:1233
  358.6 25.8 %collective-permute-start.30 = (bf16[2,128,1024]{2,1,0:T(8,128)(2,1)}, bf16[2,128,1024]{2,1,0:T(8,128)(2,1)}, u32[]{:S(2)}, u32[]{:S(2)}) collective-permute-start(bf16[2,128,1024]{2,1,0:T(8,128)(2,1)} %get-tuple-element.198), channel_id=1, source_target_pairs={{0,16},{8,24},{16,0},{24,8},{1,17},{9,25},{17,1},{25,9},{2,18},{10... | collective-permute-start | bytes 1572872 | tf_op jit(solution)/shard_map/ppermute | solution.py:1238
  358.9 26.1 %collective-permute-start.31 = (bf16[2,128,1024]{2,1,0:T(8,128)(2,1)}, bf16[2,128,1024]{2,1,0:T(8,128)(2,1)}, u32[]{:S(2)}, u32[]{:S(2)}) collective-permute-start(bf16[2,128,1024]{2,1,0:T(8,128)(2,1)} %get-tuple-element.199), channel_id=1, source_target_pairs={{0,8},{8,0},{16,24},{24,16},{1,9},{9,1},{17,25},{25,17},{2,10},{10... | collective-permute-start | bytes 1572872 | tf_op jit(solution)/shard_map/ppermute | solution.py:1238
  360.7 24.3 %all-to-all-start.7 = ((bf16[8,2,128,128]{3,2,1,0:T(8,128)(2,1)}), bf16[8,2,128,128]{3,2,1,0:T(8,128)(2,1)}, u32[]{:S(2)}, u32[]{:S(2)}) async-start(bf16[8,2,128,128]{3,2,1,0:T(8,128)(2,1)} %get-tuple-element.197), calls=%async_computation.7 | async-start | bytes 1048576 | tf_op jit(solution)/shard_map/all_to_all | solution.py:1398
  369.4 45.8 %collective-permute-start.34 = (bf16[2,240,1024]{2,1,0:T(8,128)(2,1)}, bf16[2,240,1024]{2,1,0:T(8,128)(2,1)}, u32[]{:S(2)}, u32[]{:S(2)}) collective-permute-start(bf16[2,240,1024]{2,1,0:T(8,128)(2,1)} %get-tuple-element.201.__3_), channel_id=1, source_target_pairs={{0,2},{1,3},{2,0},{3,1},{4,6},{5,7},{6,4},{7,5},{8,10},{9,11},{10,... | collective-permute-start | bytes 2949128 | tf_op jit(solution)/shard_map/ppermute | solution.py:1233
  371.3 44.0 %collective-permute-start.35 = (bf16[2,240,1024]{2,1,0:T(8,128)(2,1)}, bf16[2,240,1024]{2,1,0:T(8,128)(2,1)}, u32[]{:S(2)}, u32[]{:S(2)}) collective-permute-start(bf16[2,240,1024]{2,1,0:T(8,128)(2,1)} %get-tuple-element.202.__4_), channel_id=1, source_target_pairs={{0,4},{1,5},{2,6},{3,7},{4,0},{5,1},{6,2},{7,3},{8,12},{9,13},{10,... | collective-permute-start | bytes 2949128 | tf_op jit(solution)/shard_map/ppermute | solution.py:1233
  377.6 37.6 %collective-permute-start.36 = (bf16[2,192,1024]{2,1,0:T(8,128)(2,1)}, bf16[2,192,1024]{2,1,0:T(8,128)(2,1)S(1)}, u32[]{:S(2)}, u32[]{:S(2)}) collective-permute-start(bf16[2,192,1024]{2,1,0:T(8,128)(2,1)} %get-tuple-element.210.__5_), channel_id=1, source_target_pairs={{0,2},{1,3},{2,0},{3,1},{4,6},{5,7},{6,4},{7,5},{8,10},{9,11},{10,... | collective-permute-start | bytes 2359304 | tf_op jit(solution)/shard_map/ppermute | solution.py:1233
  384.4 30.8 %collective-permute-start.37 = (bf16[2,192,1024]{2,1,0:T(8,128)(2,1)}, bf16[2,192,1024]{2,1,0:T(8,128)(2,1)S(1)}, u32[]{:S(2)}, u32[]{:S(2)}) collective-permute-start(bf16[2,192,1024]{2,1,0:T(8,128)(2,1)} %get-tuple-element.211.__6_), channel_id=1, source_target_pairs={{0,4},{1,5},{2,6},{3,7},{4,0},{5,1},{6,2},{7,3},{8,12},{9,13},{10,... | collective-permute-start | bytes 2359304 | tf_op jit(solution)/shard_map/ppermute | solution.py:1233
  416.4 35.8 %collective-permute-start.38 = (bf16[4,1,256,1024]{3,2,1,0:T(8,128)(2,1)}, bf16[4,1,256,1024]{3,2,1,0:T(8,128)(2,1)S(1)}, u32[]{:S(2)}, u32[]{:S(2)}) collective-permute-start(bf16[4,1,256,1024]{3,2,1,0:T(8,128)(2,1)} %get-tuple-element.233), channel_id=1, source_target_pairs={{0,1},{1,0},{2,3},{3,2},{4,5},{5,4},{6,7},{7,6},{8,9},{9,8},{10,11... | collective-permute-start | bytes 6291464 | tf_op jit(solution)/shard_map/ppermute | solution.py:1233
  417.5 14.9 %collective-permute-start.39 = (bf16[2,128,1024]{2,1,0:T(8,128)(2,1)S(1)}, bf16[2,128,1024]{2,1,0:T(8,128)(2,1)}, u32[]{:S(2)}, u32[]{:S(2)}) collective-permute-start(bf16[2,128,1024]{2,1,0:T(8,128)(2,1)S(1)} %copy-done.46), channel_id=1, source_target_pairs={{0,8},{8,0},{16,24},{24,16},{1,9},{9,1},{17,25},{25,17},{2,10},{10... | collective-permute-start | bytes 1572872 | tf_op jit(solution)/shard_map/ppermute | solution.py:1238
  421.5 30.7 %collective-permute-start.42 = (bf16[432,1024]{1,0:T(8,128)(2,1)}, bf16[432,1024]{1,0:T(8,128)(2,1)S(1)}, u32[]{:S(2)}, u32[]{:S(2)}) collective-permute-start(bf16[432,1024]{1,0:T(8,128)(2,1)} %bitcast.315), channel_id=1, source_target_pairs={{0,4},{1,5},{2,6},{3,7},{4,0},{5,1},{6,2},{7,3},{8,12},{9,13},{10,... | collective-permute-start | bytes 2654216 | tf_op jit(solution)/shard_map/ppermute | solution.py:1233
  422.9 29.3 %collective-permute-start.43 = (bf16[432,1024]{1,0:T(8,128)(2,1)}, bf16[432,1024]{1,0:T(8,128)(2,1)}, u32[]{:S(2)}, u32[]{:S(2)}) collective-permute-start(bf16[432,1024]{1,0:T(8,128)(2,1)} %bitcast.313), channel_id=1, source_target_pairs={{0,2},{1,3},{2,0},{3,1},{4,6},{5,7},{6,4},{7,5},{8,10},{9,11},{10,... | collective-permute-start | bytes 2654216 | tf_op jit(solution)/shard_map/ppermute | solution.py:1233
  423.5 28.7 %collective-permute-start.41 = (bf16[2,8,176,128]{3,2,1,0:T(8,128)(2,1)}, bf16[2,8,176,128]{3,2,1,0:T(8,128)(2,1)}, u32[]{:S(2)}, u32[]{:S(2)}) collective-permute-start(bf16[2,8,176,128]{3,2,1,0:T(8,128)(2,1)} %pad_maximum_fusion.6.__5_), channel_id=1, source_target_pairs={{0,8},{8,0},{16,24},{24,16},{1,9},{9,1},{17,25},{25,17},{2,10},{10... | collective-permute-start | bytes 2162696 | tf_op jit(solution)/shard_map/ppermute | solution.py:1238
  433.5 18.7 %collective-permute-start.40 = (bf16[128,1024]{1,0:T(8,128)(2,1)S(1)}, bf16[128,1024]{1,0:T(8,128)(2,1)S(1)}, u32[]{:S(2)}, u32[]{:S(2)}) collective-permute-start(bf16[128,1024]{1,0:T(8,128)(2,1)S(1)} %fusion.6), channel_id=1, source_target_pairs={{0,16},{8,24},{16,0},{24,8},{1,17},{9,25},{17,1},{25,9},{2,18},{10... | collective-permute-start | bytes 786440 | tf_op jit(solution)/shard_map/ppermute | solution.py:1238
  464.7 22.6 %collective-permute-start.46 = (bf16[2,192,1024]{2,1,0:T(8,128)(2,1)}, bf16[2,192,1024]{2,1,0:T(8,128)(2,1)S(1)}, u32[]{:S(2)}, u32[]{:S(2)}) collective-permute-start(bf16[2,192,1024]{2,1,0:T(8,128)(2,1)} %get-tuple-element.251.__2_), channel_id=1, source_target_pairs={{0,2},{1,3},{2,0},{3,1},{4,6},{5,7},{6,4},{7,5},{8,10},{9,11},{10,... | collective-permute-start | bytes 2359304 | tf_op jit(solution)/shard_map/ppermute | solution.py:1233
  465.3 21.9 %collective-permute-start.47 = (bf16[2,192,1024]{2,1,0:T(8,128)(2,1)}, bf16[2,192,1024]{2,1,0:T(8,128)(2,1)S(1)}, u32[]{:S(2)}, u32[]{:S(2)}) collective-permute-start(bf16[2,192,1024]{2,1,0:T(8,128)(2,1)} %get-tuple-element.252.__3_), channel_id=1, source_target_pairs={{0,4},{1,5},{2,6},{3,7},{4,0},{5,1},{6,2},{7,3},{8,12},{9,13},{10,... | collective-permute-start | bytes 2359304 | tf_op jit(solution)/shard_map/ppermute | solution.py:1233
  468.7 17.5 %collective-permute-start.45 = (bf16[8,176,128]{2,1,0:T(8,128)(2,1)}, bf16[8,176,128]{2,1,0:T(8,128)(2,1)S(1)}, u32[]{:S(2)}, u32[]{:S(2)}) collective-permute-start(bf16[8,176,128]{2,1,0:T(8,128)(2,1)} %fusion.7), channel_id=1, source_target_pairs={{0,16},{8,24},{16,0},{24,8},{1,17},{9,25},{17,1},{25,9},{2,18},{10... | collective-permute-start | bytes 1081352 | tf_op jit(solution)/shard_map/ppermute | solution.py:1238
  470.8 16.5 %collective-permute-start.44 = (bf16[2,96,1024]{2,1,0:T(8,128)(2,1)}, bf16[2,96,1024]{2,1,0:T(8,128)(2,1)}, u32[]{:S(2)}, u32[]{:S(2)}) collective-permute-start(bf16[2,96,1024]{2,1,0:T(8,128)(2,1)} %pad_maximum_fusion.11), channel_id=1, source_target_pairs={{0,8},{8,0},{16,24},{24,16},{1,9},{9,1},{17,25},{25,17},{2,10},{10... | collective-permute-start | bytes 1179656 | tf_op jit(solution)/shard_map/ppermute | solution.py:1238
  497.6 23.8 %collective-permute-start.48 = (bf16[192,1024]{1,0:T(8,128)(2,1)}, bf16[192,1024]{1,0:T(8,128)(2,1)}, u32[]{:S(2)}, u32[]{:S(2)}) collective-permute-start(bf16[192,1024]{1,0:T(8,128)(2,1)} %bitcast.334), channel_id=1, source_target_pairs={{0,4},{1,5},{2,6},{3,7},{4,0},{5,1},{6,2},{7,3},{8,12},{9,13},{10,... | collective-permute-start | bytes 1179656 | tf_op jit(solution)/shard_map/ppermute | solution.py:1233
  498.2 23.1 %collective-permute-start.49 = (bf16[192,1024]{1,0:T(8,128)(2,1)}, bf16[192,1024]{1,0:T(8,128)(2,1)}, u32[]{:S(2)}, u32[]{:S(2)}) collective-permute-start(bf16[192,1024]{1,0:T(8,128)(2,1)} %bitcast.333), channel_id=1, source_target_pairs={{0,2},{1,3},{2,0},{3,1},{4,6},{5,7},{6,4},{7,5},{8,10},{9,11},{10,... | collective-permute-start | bytes 1179656 | tf_op jit(solution)/shard_map/ppermute | solution.py:1233
  (105 other events, 656.6 us)
Sparse Core Ops, SparseCore 0:
  11.3 94.2 all-gather.5
  118.1 69.3 all-gather.3
  268.9 68.8 reduce-scatter.1

commit v4 on v3

--- a/solution.py
+++ b/solution.py
@@ -1191,6 +1191,18 @@
     return [exchange(block, 2 * k) for k in range(1, CHIPS)]
 
 
+def sends_dp(pieces):
+    size, me = lax.axis_size("dp"), lax.axis_index("dp")
+    own, *others = [
+        lax.dynamic_index_in_dim(pieces, lax.rem(me + shift, size), 0, keepdims=False)
+        for shift in range(size)
+    ]
+    return own, [
+        lax.ppermute(piece, "dp", [(i, (i + shift) % size) for i in range(size)])
+        for shift, piece in enumerate(others, 1)
+    ]
+
+
 def gather_index(mine):
     size, me = lax.axis_size("index"), lax.axis_index("index")
     block = mine[0]
@@ -1317,7 +1329,7 @@
     def terms(self, k, half, *more):
         middle = self.middle
         return [(array, e, middle, half) for array, e in self.chips[k]] + [
-            (array, e, middle, 0) for array, e in more
+            (array, e, middle, start // middle) for array, e, start in more
         ]
 
     def total(self, k, half, *more):
@@ -1344,11 +1356,12 @@
 
 
 def seconds(*sums):
-    for one, top, low in sums:
-        one.got = top, low
+    for one, top, low, start in sums:
+        rows = slice(start, start + one.middle)
+        one.got = top[:, rows], low[:, rows]
     top, low = combine(
-        [[one.terms(2, 0, (top, 1)) for one, top, _ in sums]],
-        [[one.terms(1, 1, (low, 1)) for one, _, low in sums]],
+        [[one.terms(2, 0, (top, 1, start)) for one, top, _, start in sums]],
+        [[one.terms(1, 1, (low, 1, start)) for one, _, low, start in sums]],
     )
     return top[0], low[0]
 
@@ -1532,19 +1545,19 @@
     qkv_bias = jnp.concatenate([vector_here[0:1], no_bias, vector_here[1:2]], axis=1)
     kv_bias = jnp.concatenate([no_bias, vector_here[4:5]], axis=1)
     x_rows = decoder_input.reshape(rows, depth)
-    (slices,) = hold([slices], key_bias)
+    slices, *contract_sent = hold([slices, *contract_sent], key_bias)
+    contract = [contract, *contract_sent]
+    ahead, across = jnp.stack(contract[:2]), jnp.stack(contract[2:])
     qkv = project_columns("self_qkv", *input_rows, slices, 0, 3, qkv_bias)
     qkv, *late_arrived = hold([qkv, *late_sent])
     late = lax.all_gather(place_dp(late, late_arrived), "index", axis=0, tiled=False)
     self_out, self_stat = attend(True, qkv, 0, qkv, 1, 2, key_bias[:, None, :])
-    self_out, *contract_sent = hold([self_out, *contract_sent])
-    contract = [contract, *contract_sent]
+    self_out, ahead_far, across_far = hold(
+        [self_out, exchange_dp(ahead, 2), exchange_dp(across, 1)]
+    )
     self_got = swap(self_out)
     square = gather_index(hold(square, self_out))
-    ahead, across = hold([jnp.stack(contract[:2]), jnp.stack(contract[2:])], self_out)
-    self_got, ahead_far, across_far, square = hold(
-        [self_got, exchange_dp(ahead, 2), exchange_dp(across, 1), square]
-    )
+    self_got, square = hold([self_got, square])
     ahead = jnp.stack([ahead, ahead_far])
     across = jnp.stack([across, across_far])
     contract_sent = [exchange_dp(ahead, 1), exchange_dp(across, 2)]
@@ -1615,6 +1628,8 @@
     query_low, first_grad, self_low, self_mix_grad, first_stat = first_back(
         cross_dq_got, second_grad, first_in, square, vectors, memory_mine
     )
+    kv_sum = HalvingDp(kv_grads)
+    kv_got = exchange_dp(kv_sum.first(), 1)
     memory_sum = both_cores(memory_mine, exchange(memory_other, 1))
     memory_sent = firsts(memory_sum)
     square_mine, square_other = weight_grads(
@@ -1629,17 +1644,19 @@
     )
     square_sum = both_cores(square_mine, exchange(square_other, 1))
     square_sent = firsts(square_sum)
-    self_mix_got, *contract_last = hold(
-        [swap(self_mix_grad), *contract_last], *memory_sent, *square_sent
-    )
+    self_mix_got, kv_got = hold(
+        [swap(self_mix_grad), kv_got], *memory_sent, *square_sent
+    )
+    kv_last = exchange_dp(kv_sum.second(kv_got), 2)
     memory_got = send_first(*memory_sent)
     square_got = send_first(*square_sent)
     self_dq, self_dkv, _ = attend_back(
         True, qkv, 0, qkv, 1, 2, self_mix_got, self_stat, self_stat, square_mine
     )
     expand_sum = HalvingDp(expand_part_sum)
-    self_dq, expand_sent = hold([self_dq, expand_sum.first()])
-    expand_got = exchange_dp(expand_sent, 1)
+    self_dq, expand_sent, kv_last, *contract_last = hold(
+        [self_dq, expand_sum.first(), kv_last, *contract_last]
+    )
     dx_mine, dx_other, qkv_slice_grads, qkv_total = project_columns_back(
         "self_qkv_back", order, *input_rows, [self_dq, self_dkv], slices, 0, 3
     )
@@ -1675,25 +1692,16 @@
     vector_send = jnp.pad(
         vector_send, ((0, 0), (0, 0), (0, extra_rows * width - vector_size))
     ).reshape(groups, count, extra_rows, width)
-    slice_sum = HalvingDp(
-        jnp.concatenate([qkv_slice_grads, kv_grads, vector_send.astype(low)], axis=2)
-    )
-    slice_sent = slice_sum.first()
-    slice_got = exchange_dp(slice_sent, 1)
-    dx_other, *got = hold([dx_other, *got], slice_sent)
+    slice_grads = jnp.concatenate([qkv_slice_grads, vector_send.astype(low)], axis=2)
+    slice_own, slice_sent = sends_dp(slice_grads)
+    dx_other, *got = hold([dx_other, *got], slice_grads)
     dx_got = exchange(dx_other, 1)
     square_rows = square_sum.middle
-    last = seconds((square_sum, *got[2:]), (memory_sum, *got[:2]))
-    prior_rows, expand_got, *contract_last = hold(
-        [prior_rows, expand_got, *contract_last], *last
-    )
+    last = seconds((square_sum, *got[2:], 0), (memory_sum, *got[:2], 0))
+    prior_rows, *contract_last = hold([prior_rows, *contract_last], *last)
     last = send_last(*last)
-    expand_last = exchange_dp(expand_sum.second(expand_got), 2)
     prior_arrived = small_send(prior_rows.reshape(seqs, slots, MEM_P).sum(axis=-1))
-    dx_got, expand_last, prior_arrived, slice_got, *last = hold(
-        [dx_got, expand_last, prior_arrived, slice_got, *last]
-    )
-    slice_last = exchange_dp(slice_sum.second(slice_got), 2)
+    dx_got, *last = hold([dx_got, *last])
     dx_sum = both_cores(dx_mine, dx_got)
     contract_sum = Halving(
         [
@@ -1706,20 +1714,15 @@
     )
     dx_sent = firsts(dx_sum, contract_sum)
     got = send_first(*dx_sent)
-    last = hold(last, *dx_sent)
-    square_last, memory_last = split_rows(last, square_rows)
+    square_last, memory_last = split_rows(hold(last, *dx_sent), square_rows)
     square_far = HalvingDp(square_sum.finish(*square_last).reshape(groups, 3 * part, depth))
     square_got = exchange_dp(square_far.first(), 1)
-    memory_gradient = memory_sum.finish(*memory_last).reshape(encoder_memory.shape)
-    square_got, slice_last, *got = hold([square_got, slice_last, *got], memory_gradient)
-    dx_got, contract_got = split_rows(got, dx_sum.middle)
-    last = send_last(*seconds((dx_sum, *dx_got), (contract_sum, *contract_got)))
-    square_last = exchange_dp(square_far.second(square_got), 2)
-    dx_last, contract_last = split_rows(last, dx_sum.middle)
-    input_gradient = first_grad + dx_sum.finish(*dx_last)
-    contract_sum = contract_sum.finish(*contract_last)
-    slice_sum = slice_sum.finish(slice_last)
-
+    expand_got = exchange_dp(hold([expand_sent], *dx_sent)[0], 1)
+    slice_sum = sum(
+        (one.astype(jnp.float32) for one in hold(slice_sent, *dx_sent)),
+        slice_own.astype(jnp.float32),
+    )
+    (prior_arrived,) = hold([prior_arrived], *dx_sent)
     prior_grad = jnp.where(usable, small_take(prior_arrived, (seqs, slots)), 0.0)
     score_doc = jnp.where(
         usable, prior_grad - passage_prob * jnp.sum(prior_grad, axis=1, keepdims=True), 0.0
@@ -1741,9 +1744,26 @@
         ((0, 0), (vector_size, extra_rows * width - vector_size - question_size)),
     ).reshape(count, extra_rows, width)
     slice_sum = jnp.concatenate(
-        [slice_sum[:, : 5 * part], slice_sum[:, 5 * part :] + question_send], axis=1
-    )
-    arrived = swap(slice_sum.astype(low)).astype(jnp.float32)
+        [
+            slice_sum[:, : 3 * part],
+            kv_sum.finish(kv_last),
+            slice_sum[:, 3 * part :] + question_send,
+        ],
+        axis=1,
+    )
+    arrived, square_got, expand_got, *got = hold(
+        [swap(slice_sum.astype(low)), square_got, expand_got, *got]
+    )
+    expand_last = exchange_dp(expand_sum.second(expand_got), 2)
+    start = dx_sum.middle
+    last = send_last(*seconds((dx_sum, *got, 0), (contract_sum, *got, start)))
+    square_last = exchange_dp(square_far.second(square_got), 2)
+    dx_last, contract_last = split_rows(last, start)
+    input_gradient = first_grad + dx_sum.finish(*dx_last)
+    contract_sum = contract_sum.finish(*contract_last)
+    memory_last = hold(memory_last, *got)
+    memory_gradient = memory_sum.finish(*memory_last).reshape(encoder_memory.shape)
+    arrived = arrived.astype(jnp.float32)
     split_grads = (
         arrived[:, : 5 * part]
         .reshape(count, 5, part, width)

time: 545 us -> 547 us (level)
  starting transfers between devices: 82.2 us -> 110 us
  waiting for transfers between devices: 115 us -> 104 us
  blocking collectives: 9.21 us -> 0 us
    ppermute x14, waiting for transfers between devices: 44.6 us -> 28.7 us  [exchange_dp(): return lax.ppermute(piece, 'dp', [(i, i ^ flip) for i in range(size)])]
    reduce_scatter x1, starting transfers between devices: 0.21 us -> 13.1 us  [head_body(): lax.psum_scatter(wide_grad, 'index', scatter_dimension=0, tiled=False)]
    all_to_all x1 -> x0, blocking collectives: 9.21 us -> none  [swap(): return lax.all_to_all(pieces, 'index', 0, 0, tiled=True)]
    ppermute x0 -> x3, starting transfers between devices: none -> 6.41 us  [sends_dp(): lax.ppermute(piece, 'dp', [(i, (i + shift) % size) for i in range(size)])]
    all_gather x1, waiting for transfers between devices: 1.86 us -> 8.17 us  [head_body(): lax.all_gather(jnp.concatenate([jnp.pad(encoder_memory, ((0, 0), (0, memo...]
    all_to_all x9 -> x10, starting transfers between devices: 34.6 us -> 37.9 us  [swap(): return lax.all_to_all(pieces, 'index', 0, 0, tiled=True)]
    unnamed x186 -> x187, local copies, waits for them, and re-layouts: 24.8 us -> 23.1 us
    all_to_all x9 -> x10, waiting for transfers between devices: 30.8 us -> 30.4 us  [swap(): return lax.all_to_all(pieces, 'index', 0, 0, tiled=True)]
  transfers between devices with their start and end apart: 63 -> 67, of which waited for: 24 -> 17; matrix products, arithmetic and copies ran while one was open for 15% -> 17% of each run, Pallas kernels for 29% -> 29%
where the time goes in v4:
time: 547 us; the launch traced here: 539 us
  Pallas kernels  186 us (34%)
  starting transfers between devices  110 us (20%)
  waiting for transfers between devices  104 us (19%)
  local copies, waits for them, and re-layouts  72.3 us (13%)
  other arithmetic  51 us (9%)
  between operations  15.6 us (3%)
    pallas_call x2, Pallas kernels, attend_back(): pl.pallas_call(partial(attend_backward_kernel, causal, head_width), grid=...  41.2 us
    all_to_all x10, starting transfers between devices, swap(): return lax.all_to_all(pieces, 'index', 0, 0, tiled=True)  37.9 us
    all_to_all x10, waiting for transfers between devices, swap(): return lax.all_to_all(pieces, 'index', 0, 0, tiled=True)  30.4 us
    pallas_call x2, Pallas kernels, attend(): pl.pallas_call(partial(attend_forward_kernel, causal, head_width), grid=(...  29.7 us
    ppermute x14, waiting for transfers between devices, exchange_dp(): return lax.ppermute(piece, 'dp', [(i, i ^ flip) for i in range(size)])  28.7 us
    pallas_call x1, Pallas kernels, ffn(): pl.pallas_call(ffn_kernel, grid_spec=pltpu.PrefetchScalarGridSpec(num_sca...  26.2 us
    pallas_call x2, Pallas kernels, project_columns_back(): pl.pallas_call(partial(columns_back_kernel, first), grid_spec=pltpu.Prefe...  25.9 us
    ppermute x28, waiting for transfers between devices, exchange(): return lax.ppermute(piece, 'index', [(i, i ^ flip) for i in range(size)])  24.5 us
  transfers between devices with their start and end apart: 67, of which 17 were waited for; matrix products, arithmetic and copies ran while one was open for 17% of the time, Pallas kernels for 29%

profile of v4, /device:TPU:0, one launch (start us, length us, event | category | flops | bytes accessed | tf_op | source)
XLA Modules:
  0.0 539.4 jit_solution(15680084132742234615)
XLA Ops:
  11.4 3.1 collective-permute-start
  19.7 4.1 all-to-all-start
  25.7 10.2 %all-to-all-done.__3_.__0_ = bf16[8,176,128]{2,1,0:T(8,128)(2,1)} async-done(((bf16[8,176,128]{2,1,0:T(8,128)(2,1)}), bf16[8,176,128]{2,1,0:T(8,128)(2,1)}, u32[]{:S(2)}, u32[]{:S(2)}) %all-to-all-start) | async-done | bytes 360480 | tf_op jit(solution)/shard_map/all_to_all | solution.py:1411
  50.9 10.7 %collective-permute-done.4.__1_ = bf16[8,176,128]{2,1,0:T(8,128)(2,1)} collective-permute-done((bf16[8,176,128]{2,1,0:T(8,128)(2,1)}, bf16[8,176,128]{2,1,0:T(8,128)(2,1)}, u32[]{:S(2)}, u32[]{:S(2)}) %collective-permute-start.4) | collective-permute-done | bytes 360480 | tf_op jit(solution)/shard_map/ppermute | solution.py:1176
  61.6 15.8 %collective-permute-done.8.__5_ = bf16[4,32,2048]{2,1,0:T(8,128)(2,1)S(1)} collective-permute-done((bf16[4,32,2048]{2,1,0:T(8,128)(2,1)S(1)}, bf16[4,32,2048]{2,1,0:T(8,128)(2,1)S(1)}, u32[]{:S(2)}, u32[]{:S(2)}) %collective-permute-start.8) | collective-permute-done | bytes 524320 | tf_op jit(solution)/shard_map/ppermute | solution.py:1245
  84.1 4.2 gather_fusion
  89.9 3.3 all-to-all-start.1
  96.7 8.5 %all-to-all-done.1 = f32[8,8,128]{2,1,0:T(8,128)S(1)} async-done(((f32[8,8,128]{2,1,0:T(8,128)}), f32[8,8,128]{2,1,0:T(8,128)S(1)}, u32[]{:S(2)}, u32[]{:S(2)}) %all-to-all-start.1) | async-done | bytes 32800 | tf_op jit(solution)/shard_map/all_to_all | solution.py:1411
  108.7 8.2 %all-gather.6.cloned.1.call-done = bf16[16,384,1024]{2,1,0:T(8,128)(2,1)} async-done(((bf16[2,384,1024]{2,1,0:T(8,128)(2,1)}), bf16[16,384,1024]{2,1,0:T(8,128)(2,1)}) %all-gather.6.cloned.1.call-update) | async-done | bytes 12582928 | tf_op jit(solution)/shard_map/all_gather | solution.py:1466
  116.8 8.2 %self_qkv.1.__0_ = bf16[8,3,2,128,128]{4,3,2,1,0:T(8,128)(2,1)} custom-call(bf16[8,2,384,1024]{3,2,1,0:T(8,128)(2,1)} %bitcast.231, bf16[4,8,176,128]{3,2,1,0:T(8,128)(2,1)} %get-tuple-element.150.slice_ref.__0_, f32[1,384]{1,0:T(1,128)} %fusion.18.bias_ref), custom_call_target="tpu_custom_call" | custom-call | flops 100663296 | bytes 262144 | tf_op jit(solution)/shard_map/self_qkv/pallas_call | solution.py:709
  135.6 10.1 %attend_self.1 = (bf16[8,2,128,128]{3,2,1,0:T(8,128)(2,1)}, f32[2,2,1024]{2,1,0:T(2,128)}) custom-call(bf16[8,3,2,128,128]{4,3,2,1,0:T(8,128)(2,1)} %get-tuple-element.151.q_ref.k_ref.v_ref, bf16[8,3,2,128,128]{4,3,2,1,0:T(8,128)(2,1)} %get-tuple-element.151.q_ref.k_ref.v_ref, bf16[8,3,2,128,128]{4,3,2,1,0:T(8,128)(2,1)} %get-tuple-element.151.q_ref.k_ref.v_ref, ...), custom_call_target="tpu_custom_call" | custom-call | flops 268435456 | bytes 131072 | tf_op jit(solution)/shard_map/attend_self/pallas_call | solution.py:606
  145.8 7.4 %collective-permute-done.16.__2_ = bf16[2,128,1024]{2,1,0:T(8,128)(2,1)S(1)} collective-permute-done((bf16[2,128,1024]{2,1,0:T(8,128)(2,1)S(1)}, bf16[2,128,1024]{2,1,0:T(8,128)(2,1)S(1)}, u32[]{:S(2)}, u32[]{:S(2)}) %collective-permute-start.16) | collective-permute-done | bytes 524320 | tf_op jit(solution)/shard_map/ppermute | solution.py:1250
  153.2 6.5 %collective-permute-done.15.__1_ = bf16[2,128,1024]{2,1,0:T(8,128)(2,1)S(1)} collective-permute-done((bf16[2,128,1024]{2,1,0:T(8,128)(2,1)S(1)}, bf16[2,128,1024]{2,1,0:T(8,128)(2,1)S(1)}, u32[]{:S(2)}, u32[]{:S(2)}) %collective-permute-start.15) | collective-permute-done | bytes 524320 | tf_op jit(solution)/shard_map/ppermute | solution.py:1250
  160.5 3.2 pad_maximum_fusion
  164.5 3.9 all-to-all-start.2
  170.0 2.9 collective-permute-start.18
  187.3 5.1 first_forward.1
  192.5 4.0 all-to-all-start.3
  197.6 9.0 %memory_kv.1.k_ref.v_ref = bf16[8,2,2,240,128]{4,3,2,1,0:T(8,128)(2,1)} custom-call(bf16[8,2,384,1024]{3,2,1,0:T(8,128)(2,1)} %bitcast.232, bf16[4,8,176,128]{3,2,1,0:T(8,128)(2,1)} %hold.39.slice_ref.refs_1_.refs_2_, f32[1,256]{1,0:T(1,128)} %concatenate.81.bias_ref), custom_call_target="tpu_custom_call" | custom-call | flops 125829120 | bytes 491520 | tf_op jit(solution)/shard_map/memory_kv/pallas_call | solution.py:709
  207.4 19.6 %attend_memory.1 = (bf16[8,2,128,128]{3,2,1,0:T(8,128)(2,1)}, f32[2,2,1024]{2,1,0:T(2,128)}) custom-call(bf16[8,1,2,128,128]{4,3,2,1,0:T(8,128)(2,1)} %bitcast.295, bf16[8,2,2,240,128]{4,3,2,1,0:T(8,128)(2,1)} %memory_kv.1.k_ref.v_ref, bf16[8,2,2,240,128]{4,3,2,1,0:T(8,128)(2,1)} %memory_kv.1.k_ref.v_ref, f32[2,1,1920]{2,1,0:T(1,128)} %broadcast_in_dim_reshape.6.bias_ref), custom_call_target="tpu_custom_call" | custom-call | flops 503316480 | bytes 188416 | tf_op jit(solution)/shard_map/attend_memory/pallas_call | solution.py:606
  227.6 4.1 all-to-all-start.4
  231.7 13.1 %reduce-scatter.2.cloned.1.call-start = ((), (), s32[]{:S(2)}) async-start(), calls=%async_computation.12 | async-start | bytes 9437184 | tf_op jit(solution)/shard_map/reduce_scatter | solution.py:1599
  247.6 26.2 %ffn.1 = (bf16[256,1024]{1,0:T(8,128)(2,1)}, bf16[256,1024]{1,0:T(8,128)(2,1)}, bf16[8,4,128,1024]{3,2,1,0:T(8,128)(2,1)}, bf16[2,2,128,1024]{3,2,1,0:T(8,128)(2...) custom-call(s32[8]{0:T(128)} %pad_add_fusion.order._, ...), custom_call_target="tpu_custom_call" | custom-call | flops 805306368 | bytes 4194304 | tf_op jit(solution)/shard_map/ffn/pallas_call | solution.py:1013
  274.4 3.8 all-to-all-start.5
  282.7 2.9 add.551
  291.3 29.3 %attend_memory_back.1 = (bf16[8,2,128,128]{3,2,1,0:T(8,128)(2,1)}, bf16[8,2,2,240,128]{4,3,2,1,0:T(8,128)(2,1)}, f32[2,1,1920]{2,1,0:T(1,128)}) custom-call(bf16[8,1,2,128,128]{4,3,2,1,0:T(8,128)(2,1)} %bitcast.296, bf16[8,2,2,240,128]{4,3,2,1,0:T(8,128)(2,1)} %memory_kv.1.k_ref.v_ref, bf16[8,2,2,240,128]{4,3,2,1,0:T(8,128)(2,1)} %memory_kv.1.k_ref.v_ref, ...), custom_call_target="tpu_custom_call" | custom-call | flops 1258291200 | bytes 376832 | tf_op jit(solution)/shard_map/attend_memory_back/pallas_call | solution.py:642
  320.6 13.8 %memory_kv_back.1 = (bf16[4,1,480,1024]{3,2,1,0:T(8,128)(2,1)}, bf16[4,1,480,1024]{3,2,1,0:T(8,128)(2,1)}, bf16[4,8,64,128]{3,2,1,0:T(8,128)(2,1)}, f32[1,256]{1,0:T(1,128)}) custom-call(s32[8]{0:T(128)} %pad_add_fusion.order._, bf16[8,2,384,1024]{3,2,1,0:T(8,128)(2,1)} %bitcast.233, bf16[8,2,2,240,128]{4,3,2,1,0:T(8,128)(2,1)} %get-tuple-element.187.refs_0_, ...), custom_call_target="tpu_custom_call" | custom-call | flops 251658240 | bytes 983040 | tf_op jit(solution)/shard_map/memory_kv_back/pallas_call | solution.py:791
  336.7 3.7 all-to-all-start.6
  346.2 3.9 all-to-all-done.6.__0_
  350.9 5.7 %first_back.1 = (bf16[256,1024]{1,0:T(8,128)(2,1)}, f32[256,1024]{1,0:T(8,128)}, bf16[256,1024]{1,0:T(8,128)(2,1)}, bf16[8,2,128,128]{3,2,1,0:T(8,128)(2,1)}, f32[8,1024]{1,0:T(8,128)}) custom-call(bf16[8,2,128,128]{3,2,1,0:T(8,128)(2,1)} %get-tuple-element.196.dq_ref, f32[256,1024]{1,0:T(8,128)} %get-tuple-element.197.second_grad, ...), custom_call_target="tpu_custom_call" | custom-call | flops 67108864 | bytes 262144 | tf_op jit(solution)/shard_map/first_back/pallas_call | solution.py:1100
  356.6 7.0 %weight_grads.1 = (bf16[4,4,96,1024]{3,2,1,0:T(8,128)(2,1)}, bf16[4,4,96,1024]{3,2,1,0:T(8,128)(2,1)}) custom-call(s32[8]{0:T(128)} %pad_add_fusion.order._, bf16[256,1024]{1,0:T(8,128)(2,1)} %get-tuple-element.204.mixed, bf16[256,1024]{1,0:T(8,128)(2,1)} %get-tuple-element.205.self_low, bf16[256,1024]{1,0:T(8,128)(2,1)} %get-tuple-element.167.__1_.first_low, ...), custom_call_target="tpu_custom_call" | custom-call | flops 100663296 | bytes 393216 | tf_op jit(solution)/shard_map/weight_grads/pallas_call | solution.py:1157
  364.7 4.2 all-to-all-start.7
  377.6 3.6 combine.5
  384.8 3.2 combine.6
  390.8 11.9 %attend_self_back.1 = (bf16[8,2,128,128]{3,2,1,0:T(8,128)(2,1)}, bf16[8,2,2,128,128]{4,3,2,1,0:T(8,128)(2,1)}, f32[2,1,1024]{2,1,0:T(1,128)}) custom-call(bf16[8,3,2,128,128]{4,3,2,1,0:T(8,128)(2,1)} %get-tuple-element.151.q_ref.k_ref.v_ref, bf16[8,3,2,128,128]{4,3,2,1,0:T(8,128)(2,1)} %get-tuple-element.151.q_ref.k_ref.v_ref, ...), custom_call_target="tpu_custom_call" | custom-call | flops 671088640 | bytes 262144 | tf_op jit(solution)/shard_map/attend_self_back/pallas_call | solution.py:642
  407.4 12.1 %self_qkv_back.1 = (bf16[4,1,256,1024]{3,2,1,0:T(8,128)(2,1)}, bf16[4,1,256,1024]{3,2,1,0:T(8,128)(2,1)}, bf16[4,8,96,128]{3,2,1,0:T(8,128)(2,1)}, f32[1,384]{1,0:T(1,128)}) custom-call(s32[8]{0:T(128)} %pad_add_fusion.order._, bf16[8,2,384,1024]{3,2,1,0:T(8,128)(2,1)} %bitcast.234, bf16[8,2,128,128]{3,2,1,0:T(8,128)(2,1)} %get-tuple-element.220.refs_0_, ...), custom_call_target="tpu_custom_call" | custom-call | flops 201326592 | bytes 524288 | tf_op jit(solution)/shard_map/self_qkv_back/pallas_call | solution.py:791
  424.3 4.1 combine.7
  438.2 3.3 all-to-all-start.8
  442.6 8.2 %collective-permute-done.41.__1_ = bf16[432,1024]{1,0:T(8,128)(2,1)S(1)} collective-permute-done((bf16[432,1024]{1,0:T(8,128)(2,1)}, bf16[432,1024]{1,0:T(8,128)(2,1)S(1)}, u32[]{:S(2)}, u32[]{:S(2)}) %collective-permute-start.41) | collective-permute-done | bytes 884768 | tf_op jit(solution)/shard_map/ppermute | solution.py:1245
  450.7 3.0 collective-permute-start.45
  455.1 3.6 combine.8
  473.9 3.4 all-to-all-start.9
  480.0 5.3 all-to-all-done.9.__0_
  485.3 3.9 collective-permute-done.46.__1_
  492.4 3.0 combine.9
  500.8 2.8 collective-permute-start.52
  505.0 2.8 bitcast_add_fusion.1
  510.9 9.6 %collective-permute-done.52 = bf16[96,1024]{1,0:T(8,128)(2,1)} collective-permute-done((bf16[96,1024]{1,0:T(8,128)(2,1)}, bf16[96,1024]{1,0:T(8,128)(2,1)}, u32[]{:S(2)}, u32[]{:S(2)}) %collective-permute-start.52) | collective-permute-done | bytes 196640 | tf_op jit(solution)/shard_map/ppermute | solution.py:1250
  (508 shorter events, 174.3 us)
Async XLA Ops:
  7.2 109.7 %all-gather.6.cloned.1.call-start = ((), (), s32[]{:S(2)}) async-start(), calls=%async_computation.13 | async-start | bytes 14155776 | tf_op jit(solution)/shard_map/all_gather | solution.py:1466
  39.2 22.4 %collective-permute-start.6 = (bf16[4,32,2048]{2,1,0:T(8,128)(2,1)S(1)}, bf16[4,32,2048]{2,1,0:T(8,128)(2,1)S(1)}, u32[]{:S(2)}, u32[]{:S(2)}) collective-permute-start(bf16[4,32,2048]{2,1,0:T(8,128)(2,1)S(1)} %bitcast_dynamic-update-slice_fusion.9.__0_), channel_id=1, source_target_pairs={{0,2},{1,3},{2,0},{3,1},{4,6},{5,7},{6,4},{7,5},{8,10},{9,11},{10,... | collective-permute-start | bytes 1572872 | tf_op jit(solution)/shard_map/ppermute | solution.py:1245
  39.3 22.3 %collective-permute-start.7 = (bf16[4,32,2048]{2,1,0:T(8,128)(2,1)S(1)}, bf16[4,32,2048]{2,1,0:T(8,128)(2,1)S(1)}, u32[]{:S(2)}, u32[]{:S(2)}) collective-permute-start(bf16[4,32,2048]{2,1,0:T(8,128)(2,1)S(1)} %bitcast_dynamic-update-slice_fusion.9.__0_), channel_id=1, source_target_pairs={{0,4},{1,5},{2,6},{3,7},{4,0},{5,1},{6,2},{7,3},{8,12},{9,13},{10,... | collective-permute-start | bytes 1572872 | tf_op jit(solution)/shard_map/ppermute | solution.py:1245
  40.4 37.0 %collective-permute-start.8 = (bf16[4,32,2048]{2,1,0:T(8,128)(2,1)S(1)}, bf16[4,32,2048]{2,1,0:T(8,128)(2,1)S(1)}, u32[]{:S(2)}, u32[]{:S(2)}) collective-permute-start(bf16[4,32,2048]{2,1,0:T(8,128)(2,1)S(1)} %bitcast_dynamic-update-slice_fusion.9.__0_), channel_id=1, source_target_pairs={{0,6},{1,7},{2,4},{3,5},{4,2},{5,3},{6,0},{7,1},{8,14},{9,15},{10,... | collective-permute-start | bytes 1572872 | tf_op jit(solution)/shard_map/ppermute | solution.py:1245
  78.3 27.2 %collective-permute-start.10 = (bf16[128,1024]{1,0:T(8,128)(2,1)}, bf16[128,1024]{1,0:T(8,128)(2,1)}, u32[]{:S(2)}, u32[]{:S(2)}) collective-permute-start(bf16[128,1024]{1,0:T(8,128)(2,1)} %hold.31), channel_id=1, source_target_pairs={{0,4},{1,5},{2,6},{3,7},{4,0},{5,1},{6,2},{7,3},{8,12},{9,13},{10,... | collective-permute-start | bytes 786440 | tf_op jit(solution)/shard_map/ppermute | solution.py:1245
  79.1 29.5 %collective-permute-start.11 = (bf16[128,1024]{1,0:T(8,128)(2,1)}, bf16[128,1024]{1,0:T(8,128)(2,1)}, u32[]{:S(2)}, u32[]{:S(2)}) collective-permute-start(bf16[128,1024]{1,0:T(8,128)(2,1)} %hold.31), channel_id=1, source_target_pairs={{0,6},{1,7},{2,4},{3,5},{4,2},{5,3},{6,0},{7,1},{8,14},{9,15},{10,... | collective-permute-start | bytes 786440 | tf_op jit(solution)/shard_map/ppermute | solution.py:1245
  80.1 28.6 %collective-permute-start.9 = (bf16[128,1024]{1,0:T(8,128)(2,1)}, bf16[128,1024]{1,0:T(8,128)(2,1)}, u32[]{:S(2)}, u32[]{:S(2)}) collective-permute-start(bf16[128,1024]{1,0:T(8,128)(2,1)} %hold.31), channel_id=1, source_target_pairs={{0,2},{1,3},{2,0},{3,1},{4,6},{5,7},{6,4},{7,5},{8,10},{9,11},{10,... | collective-permute-start | bytes 786440 | tf_op jit(solution)/shard_map/ppermute | solution.py:1245
  81.8 43.3 %collective-permute-start.12 = (bf16[160,1024]{1,0:T(8,128)(2,1)}, bf16[160,1024]{1,0:T(8,128)(2,1)}, u32[]{:S(2)}, u32[]{:S(2)}) collective-permute-start(bf16[160,1024]{1,0:T(8,128)(2,1)} %hold.34), channel_id=1, source_target_pairs={{0,8},{8,16},{16,24},{24,0},{1,9},{9,17},{17,25},{25,1},{2,10},{10... | collective-permute-start | bytes 983048 | tf_op jit(solution)/shard_map/ppermute | solution.py:1176
  83.1 41.9 %collective-permute-start.13 = (bf16[160,1024]{1,0:T(8,128)(2,1)}, bf16[160,1024]{1,0:T(8,128)(2,1)}, u32[]{:S(2)}, u32[]{:S(2)}) collective-permute-start(bf16[160,1024]{1,0:T(8,128)(2,1)} %hold.34), channel_id=1, source_target_pairs={{0,16},{8,24},{16,0},{24,8},{1,17},{9,25},{17,1},{25,9},{2,18},{10... | collective-permute-start | bytes 983048 | tf_op jit(solution)/shard_map/ppermute | solution.py:1176
  93.2 153.6 %all-gather.4.cloned.1.call-start = ((), (), s32[]{:S(2)}) async-start(), calls=%async_computation.11 | async-start | bytes 11796480 | tf_op jit(solution)/shard_map/all_gather | solution.py:1553
  105.5 19.6 %collective-permute-start.14 = (bf16[160,1024]{1,0:T(8,128)(2,1)S(1)}, bf16[160,1024]{1,0:T(8,128)(2,1)}, u32[]{:S(2)}, u32[]{:S(2)}) collective-permute-start(bf16[160,1024]{1,0:T(8,128)(2,1)S(1)} %copy-done.42), channel_id=1, source_target_pairs={{0,24},{8,0},{16,8},{24,16},{1,25},{9,1},{17,9},{25,17},{2,26},{10... | collective-permute-start | bytes 983048 | tf_op jit(solution)/shard_map/ppermute | solution.py:1176
  130.3 22.9 %collective-permute-start.16 = (bf16[2,128,1024]{2,1,0:T(8,128)(2,1)S(1)}, bf16[2,128,1024]{2,1,0:T(8,128)(2,1)S(1)}, u32[]{:S(2)}, u32[]{:S(2)}) collective-permute-start(bf16[2,128,1024]{2,1,0:T(8,128)(2,1)S(1)} %get-tuple-element.306), channel_id=1, source_target_pairs={{0,8},{8,0},{16,24},{24,16},{1,9},{9,1},{17,25},{25,17},{2,10},{10... | collective-permute-start | bytes 1572872 | tf_op jit(solution)/shard_map/ppermute | solution.py:1250
  133.7 26.0 %collective-permute-start.15 = (bf16[2,128,1024]{2,1,0:T(8,128)(2,1)S(1)}, bf16[2,128,1024]{2,1,0:T(8,128)(2,1)S(1)}, u32[]{:S(2)}, u32[]{:S(2)}) collective-permute-start(bf16[2,128,1024]{2,1,0:T(8,128)(2,1)S(1)} %get-tuple-element.308), channel_id=1, source_target_pairs={{0,16},{8,24},{16,0},{24,8},{1,17},{9,25},{17,1},{25,9},{2,18},{10... | collective-permute-start | bytes 1572872 | tf_op jit(solution)/shard_map/ppermute | solution.py:1250
  164.5 22.1 %all-to-all-start.2 = ((bf16[8,2,128,128]{3,2,1,0:T(8,128)(2,1)}), bf16[8,2,128,128]{3,2,1,0:T(8,128)(2,1)S(1)}, u32[]{:S(2)}, u32[]{:S(2)}) async-start(bf16[8,2,128,128]{3,2,1,0:T(8,128)(2,1)} %get-tuple-element.156.__4_), calls=%async_computation.2 | async-start | bytes 1048576 | tf_op jit(solution)/shard_map/all_to_all | solution.py:1411
  168.5 58.5 %collective-permute-start.19 = (bf16[2,2,128,1024]{3,2,1,0:T(8,128)(2,1)S(1)}, bf16[2,2,128,1024]{3,2,1,0:T(8,128)(2,1)}, u32[]{:S(2)}, u32[]{:S(2)}) collective-permute-start(bf16[2,2,128,1024]{3,2,1,0:T(8,128)(2,1)S(1)} %pad_maximum_fusion.4.refs_2_), channel_id=1, source_target_pairs={{0,16},{8,24},{16,0},{24,8},{1,17},{9,25},{17,1},{25,9},{2,18},{10... | collective-permute-start | bytes 3145736 | tf_op jit(solution)/shard_map/ppermute | solution.py:1250
  170.0 56.9 %collective-permute-start.18 = (bf16[2,2,128,1024]{3,2,1,0:T(8,128)(2,1)S(1)}, bf16[2,2,128,1024]{3,2,1,0:T(8,128)(2,1)}, u32[]{:S(2)}, u32[]{:S(2)}) collective-permute-start(bf16[2,2,128,1024]{3,2,1,0:T(8,128)(2,1)S(1)} %pad_maximum_fusion.3.refs_0_), channel_id=1, source_target_pairs={{0,8},{8,0},{16,24},{24,16},{1,9},{9,1},{17,25},{25,17},{2,10},{10... | collective-permute-start | bytes 3145736 | tf_op jit(solution)/shard_map/ppermute | solution.py:1250
  197.0 49.7 %collective-permute-start.22 = (bf16[2,2,128,1024]{3,2,1,0:T(8,128)(2,1)S(1)}, bf16[2,2,128,1024]{3,2,1,0:T(8,128)(2,1)}, u32[]{:S(2)}, u32[]{:S(2)}) collective-permute-start(bf16[2,2,128,1024]{3,2,1,0:T(8,128)(2,1)S(1)} %pad_maximum_fusion.4.refs_2_), channel_id=1, source_target_pairs={{0,1},{1,0},{2,3},{3,2},{4,5},{5,4},{6,7},{7,6},{8,9},{9,8},{10,11... | collective-permute-start | bytes 3145736 | tf_op jit(solution)/shard_map/ppermute | solution.py:1245
  197.5 49.2 %collective-permute-start.20 = (bf16[2,2,128,1024]{3,2,1,0:T(8,128)(2,1)S(1)}, bf16[2,2,128,1024]{3,2,1,0:T(8,128)(2,1)}, u32[]{:S(2)}, u32[]{:S(2)}) collective-permute-start(bf16[2,2,128,1024]{3,2,1,0:T(8,128)(2,1)S(1)} %pad_maximum_fusion.3.refs_0_), channel_id=1, source_target_pairs={{0,1},{1,0},{2,3},{3,2},{4,5},{5,4},{6,7},{7,6},{8,9},{9,8},{10,11... | collective-permute-start | bytes 3145736 | tf_op jit(solution)/shard_map/ppermute | solution.py:1245
  227.0 19.8 %collective-permute-start.21 = (bf16[2,2,128,1024]{3,2,1,0:T(8,128)(2,1)}, bf16[2,2,128,1024]{3,2,1,0:T(8,128)(2,1)}, u32[]{:S(2)}, u32[]{:S(2)}) collective-permute-start(bf16[2,2,128,1024]{3,2,1,0:T(8,128)(2,1)} %get-tuple-element.174.refs_1_), channel_id=1, source_target_pairs={{0,1},{1,0},{2,3},{3,2},{4,5},{5,4},{6,7},{7,6},{8,9},{9,8},{10,11... | collective-permute-start | bytes 3145736 | tf_op jit(solution)/shard_map/ppermute | solution.py:1245
  227.5 19.3 %collective-permute-start.23 = (bf16[2,2,128,1024]{3,2,1,0:T(8,128)(2,1)}, bf16[2,2,128,1024]{3,2,1,0:T(8,128)(2,1)}, u32[]{:S(2)}, u32[]{:S(2)}) collective-permute-start(bf16[2,2,128,1024]{3,2,1,0:T(8,128)(2,1)} %get-tuple-element.175.refs_3_), channel_id=1, source_target_pairs={{0,1},{1,0},{2,3},{3,2},{4,5},{5,4},{6,7},{7,6},{8,9},{9,8},{10,11... | collective-permute-start | bytes 3145736 | tf_op jit(solution)/shard_map/ppermute | solution.py:1245
  227.6 19.2 %all-to-all-start.4 = ((bf16[8,2,128,128]{3,2,1,0:T(8,128)(2,1)}), bf16[8,2,128,128]{3,2,1,0:T(8,128)(2,1)S(1)}, u32[]{:S(2)}, u32[]{:S(2)}) async-start(bf16[8,2,128,128]{3,2,1,0:T(8,128)(2,1)} %get-tuple-element.168.__2_), calls=%async_computation.4 | async-start | bytes 1048576 | tf_op jit(solution)/shard_map/all_to_all | solution.py:1411
  231.7 171.0 %reduce-scatter.2.cloned.1.call-start = ((), (), s32[]{:S(2)}) async-start(), calls=%async_computation.12 | async-start | bytes 9437184 | tf_op jit(solution)/shard_map/reduce_scatter | solution.py:1599
  288.8 45.7 %collective-permute-start.26 = (bf16[2,2,128,1024]{3,2,1,0:T(8,128)(2,1)}, bf16[2,2,128,1024]{3,2,1,0:T(8,128)(2,1)S(1)}, u32[]{:S(2)}, u32[]{:S(2)}) collective-permute-start(bf16[2,2,128,1024]{3,2,1,0:T(8,128)(2,1)} %get-tuple-element.184._), channel_id=1, source_target_pairs={{0,8},{8,0},{16,24},{24,16},{1,9},{9,1},{17,25},{25,17},{2,10},{10... | collective-permute-start | bytes 3145736 | tf_op jit(solution)/shard_map/ppermute | solution.py:1250
  288.9 46.8 %collective-permute-start.27 = (bf16[2,2,128,1024]{3,2,1,0:T(8,128)(2,1)}, bf16[2,2,128,1024]{3,2,1,0:T(8,128)(2,1)S(1)}, u32[]{:S(2)}, u32[]{:S(2)}) collective-permute-start(bf16[2,2,128,1024]{3,2,1,0:T(8,128)(2,1)} %get-tuple-element.186), channel_id=1, source_target_pairs={{0,16},{8,24},{16,0},{24,8},{1,17},{9,25},{17,1},{25,9},{2,18},{10... | collective-permute-start | bytes 3145736 | tf_op jit(solution)/shard_map/ppermute | solution.py:1250
  290.8 49.6 %collective-permute-start.29 = (bf16[2,2,128,1024]{3,2,1,0:T(8,128)(2,1)}, bf16[2,2,128,1024]{3,2,1,0:T(8,128)(2,1)S(1)}, u32[]{:S(2)}, u32[]{:S(2)}) collective-permute-start(bf16[2,2,128,1024]{3,2,1,0:T(8,128)(2,1)} %get-tuple-element.194), channel_id=1, source_target_pairs={{0,1},{1,0},{2,3},{3,2},{4,5},{5,4},{6,7},{7,6},{8,9},{9,8},{10,11... | collective-permute-start | bytes 3145736 | tf_op jit(solution)/shard_map/ppermute | solution.py:1245
  290.8 53.0 %collective-permute-start.28 = (bf16[2,2,128,1024]{3,2,1,0:T(8,128)(2,1)}, bf16[2,2,128,1024]{3,2,1,0:T(8,128)(2,1)}, u32[]{:S(2)}, u32[]{:S(2)}) collective-permute-start(bf16[2,2,128,1024]{3,2,1,0:T(8,128)(2,1)} %get-tuple-element.191), channel_id=1, source_target_pairs={{0,1},{1,0},{2,3},{3,2},{4,5},{5,4},{6,7},{7,6},{8,9},{9,8},{10,11... | collective-permute-start | bytes 3145736 | tf_op jit(solution)/shard_map/ppermute | solution.py:1245
  334.4 43.2 %collective-permute-start.31 = (bf16[4,1,480,1024]{3,2,0,1:T(8,128)(2,1)}, bf16[4,1,480,1024]{3,2,0,1:T(8,128)(2,1)}, u32[]{:S(2)}, u32[]{:S(2)}) collective-permute-start(bf16[4,1,480,1024]{3,2,0,1:T(8,128)(2,1)} %bitcast.340), channel_id=1, source_target_pairs={{0,1},{1,0},{2,3},{3,2},{4,5},{5,4},{6,7},{7,6},{8,9},{9,8},{10,11... | collective-permute-start | bytes 11796488 | tf_op jit(solution)/shard_map/ppermute | solution.py:1245
  363.7 19.4 %collective-permute-start.32 = (bf16[4,4,96,1024]{3,2,1,0:T(8,128)(2,1)}, bf16[4,4,96,1024]{3,2,1,0:T(8,128)(2,1)S(1)}, u32[]{:S(2)}, u32[]{:S(2)}) collective-permute-start(bf16[4,4,96,1024]{3,2,1,0:T(8,128)(2,1)} %get-tuple-element.210), channel_id=1, source_target_pairs={{0,1},{1,0},{2,3},{3,2},{4,5},{5,4},{6,7},{7,6},{8,9},{9,8},{10,11... | collective-permute-start | bytes 9437192 | tf_op jit(solution)/shard_map/ppermute | solution.py:1245
  364.7 23.2 %all-to-all-start.7 = ((bf16[8,2,128,128]{3,2,1,0:T(8,128)(2,1)}), bf16[8,2,128,128]{3,2,1,0:T(8,128)(2,1)}, u32[]{:S(2)}, u32[]{:S(2)}) async-start(bf16[8,2,128,128]{3,2,1,0:T(8,128)(2,1)} %get-tuple-element.199), calls=%async_computation.7 | async-start | bytes 1048576 | tf_op jit(solution)/shard_map/all_to_all | solution.py:1411
  371.7 33.0 %collective-permute-start.34 = (bf16[2,128,1024]{2,1,0:T(8,128)(2,1)}, bf16[2,128,1024]{2,1,0:T(8,128)(2,1)}, u32[]{:S(2)}, u32[]{:S(2)}) collective-permute-start(bf16[2,128,1024]{2,1,0:T(8,128)(2,1)} %get-tuple-element.218), channel_id=1, source_target_pairs={{0,16},{8,24},{16,0},{24,8},{1,17},{9,25},{17,1},{25,9},{2,18},{10... | collective-permute-start | bytes 1572872 | tf_op jit(solution)/shard_map/ppermute | solution.py:1250
  374.1 31.0 %collective-permute-start.35 = (bf16[2,128,1024]{2,1,0:T(8,128)(2,1)}, bf16[2,128,1024]{2,1,0:T(8,128)(2,1)}, u32[]{:S(2)}, u32[]{:S(2)}) collective-permute-start(bf16[2,128,1024]{2,1,0:T(8,128)(2,1)} %get-tuple-element.219), channel_id=1, source_target_pairs={{0,8},{8,0},{16,24},{24,16},{1,9},{9,1},{17,25},{25,17},{2,10},{10... | collective-permute-start | bytes 1572872 | tf_op jit(solution)/shard_map/ppermute | solution.py:1250
  381.2 41.4 %collective-permute-start.36 = (bf16[2,240,1024]{2,1,0:T(8,128)(2,1)}, bf16[2,240,1024]{2,1,0:T(8,128)(2,1)}, u32[]{:S(2)}, u32[]{:S(2)}) collective-permute-start(bf16[2,240,1024]{2,1,0:T(8,128)(2,1)} %get-tuple-element.202.__2_), channel_id=1, source_target_pairs={{0,2},{1,3},{2,0},{3,1},{4,6},{5,7},{6,4},{7,5},{8,10},{9,11},{10,... | collective-permute-start | bytes 2949128 | tf_op jit(solution)/shard_map/ppermute | solution.py:1245
  383.1 39.5 %collective-permute-start.37 = (bf16[2,240,1024]{2,1,0:T(8,128)(2,1)}, bf16[2,240,1024]{2,1,0:T(8,128)(2,1)}, u32[]{:S(2)}, u32[]{:S(2)}) collective-permute-start(bf16[2,240,1024]{2,1,0:T(8,128)(2,1)} %get-tuple-element.203.__3_), channel_id=1, source_target_pairs={{0,4},{1,5},{2,6},{3,7},{4,0},{5,1},{6,2},{7,3},{8,12},{9,13},{10,... | collective-permute-start | bytes 2949128 | tf_op jit(solution)/shard_map/ppermute | solution.py:1245
  424.3 29.5 %collective-permute-start.40 = (bf16[4,1,256,1024]{3,2,1,0:T(8,128)(2,1)}, bf16[4,1,256,1024]{3,2,1,0:T(8,128)(2,1)S(1)}, u32[]{:S(2)}, u32[]{:S(2)}) collective-permute-start(bf16[4,1,256,1024]{3,2,1,0:T(8,128)(2,1)} %get-tuple-element.236), channel_id=1, source_target_pairs={{0,1},{1,0},{2,3},{3,2},{4,5},{5,4},{6,7},{7,6},{8,9},{9,8},{10,11... | collective-permute-start | bytes 6291464 | tf_op jit(solution)/shard_map/ppermute | solution.py:1245
  428.4 22.4 %collective-permute-start.41 = (bf16[432,1024]{1,0:T(8,128)(2,1)}, bf16[432,1024]{1,0:T(8,128)(2,1)S(1)}, u32[]{:S(2)}, u32[]{:S(2)}) collective-permute-start(bf16[432,1024]{1,0:T(8,128)(2,1)} %bitcast.324), channel_id=1, source_target_pairs={{0,4},{1,5},{2,6},{3,7},{4,0},{5,1},{6,2},{7,3},{8,12},{9,13},{10,... | collective-permute-start | bytes 2654216 | tf_op jit(solution)/shard_map/ppermute | solution.py:1245
  429.8 23.9 %collective-permute-start.42 = (bf16[432,1024]{1,0:T(8,128)(2,1)}, bf16[432,1024]{1,0:T(8,128)(2,1)}, u32[]{:S(2)}, u32[]{:S(2)}) collective-permute-start(bf16[432,1024]{1,0:T(8,128)(2,1)} %bitcast.322), channel_id=1, source_target_pairs={{0,2},{1,3},{2,0},{3,1},{4,6},{5,7},{6,4},{7,5},{8,10},{9,11},{10,... | collective-permute-start | bytes 2654216 | tf_op jit(solution)/shard_map/ppermute | solution.py:1245
  433.2 34.5 %collective-permute-start.43 = (bf16[8,112,128]{2,1,0:T(8,128)(2,1)}, bf16[8,112,128]{2,1,0:T(8,128)(2,1)}, u32[]{:S(2)}, u32[]{:S(2)}) collective-permute-start(bf16[8,112,128]{2,1,0:T(8,128)(2,1)} %get-tuple-element.302), channel_id=1, source_target_pairs={{0,8},{8,16},{16,24},{24,0},{1,9},{9,17},{17,25},{25,1},{2,10},{10... | collective-permute-start | bytes 688136 | tf_op jit(solution)/shard_map/ppermute | solution.py:1201
  434.2 33.6 %collective-permute-start.44 = (bf16[8,112,128]{2,1,0:T(8,128)(2,1)}, bf16[8,112,128]{2,1,0:T(8,128)(2,1)}, u32[]{:S(2)}, u32[]{:S(2)}) collective-permute-start(bf16[8,112,128]{2,1,0:T(8,128)(2,1)} %get-tuple-element.301), channel_id=1, source_target_pairs={{0,16},{8,24},{16,0},{24,8},{1,17},{9,25},{17,1},{25,9},{2,18},{10... | collective-permute-start | bytes 688136 | tf_op jit(solution)/shard_map/ppermute | solution.py:1201
  438.2 26.8 %all-to-all-start.8 = ((f32[8,8,128]{2,1,0:T(8,128)}), f32[8,8,128]{2,1,0:T(8,128)S(1)}, u32[]{:S(2)}, u32[]{:S(2)}) async-start(f32[8,8,128]{2,1,0:T(8,128)} %broadcast_in_dim.131), calls=%async_computation.9 | async-start | bytes 65536 | tf_op jit(solution)/shard_map/all_to_all | solution.py:1411
  450.7 19.0 %collective-permute-start.45 = (bf16[8,112,128]{2,1,0:T(8,128)(2,1)}, bf16[8,112,128]{2,1,0:T(8,128)(2,1)}, u32[]{:S(2)}, u32[]{:S(2)}) collective-permute-start(bf16[8,112,128]{2,1,0:T(8,128)(2,1)} %get-tuple-element.300), channel_id=1, source_target_pairs={{0,24},{8,0},{16,8},{24,16},{1,25},{9,1},{17,9},{25,17},{2,26},{10... | collective-permute-start | bytes 688136 | tf_op jit(solution)/shard_map/ppermute | solution.py:1201
  458.7 30.5 %collective-permute-start.48 = (bf16[2,192,1024]{2,1,0:T(8,128)(2,1)}, bf16[2,192,1024]{2,1,0:T(8,128)(2,1)S(1)}, u32[]{:S(2)}, u32[]{:S(2)}) collective-permute-start(bf16[2,192,1024]{2,1,0:T(8,128)(2,1)} %get-tuple-element.249.__3_.__1_.__2_), channel_id=1, source_target_pairs={{0,2},{1,3},{2,0},{3,1},{4,6},{5,7},{6,4},{7,5},{8,10},{9,11},{10,... | collective-permute-start | bytes 2359304 | tf_op jit(solution)/shard_map/ppermute | solution.py:1245
  460.1 29.1 %collective-permute-start.49 = (bf16[2,192,1024]{2,1,0:T(8,128)(2,1)}, bf16[2,192,1024]{2,1,0:T(8,128)(2,1)S(1)}, u32[]{:S(2)}, u32[]{:S(2)}) collective-permute-start(bf16[2,192,1024]{2,1,0:T(8,128)(2,1)} %get-tuple-element.250.__4_.__2_.__3_), channel_id=1, source_target_pairs={{0,4},{1,5},{2,6},{3,7},{4,0},{5,1},{6,2},{7,3},{8,12},{9,13},{10,... | collective-permute-start | bytes 2359304 | tf_op jit(solution)/shard_map/ppermute | solution.py:1245
  467.6 21.5 %collective-permute-start.47 = (bf16[2,128,1024]{2,1,0:T(8,128)(2,1)}, bf16[2,128,1024]{2,1,0:T(8,128)(2,1)S(1)}, u32[]{:S(2)}, u32[]{:S(2)}) collective-permute-start(bf16[2,128,1024]{2,1,0:T(8,128)(2,1)} %hold.53), channel_id=1, source_target_pairs={{0,8},{8,0},{16,24},{24,16},{1,9},{9,1},{17,25},{25,17},{2,10},{10... | collective-permute-start | bytes 1572872 | tf_op jit(solution)/shard_map/ppermute | solution.py:1250
  467.7 21.5 %collective-permute-start.46 = (bf16[2,96,1024]{2,1,0:T(8,128)(2,1)}, bf16[2,96,1024]{2,1,0:T(8,128)(2,1)}, u32[]{:S(2)}, u32[]{:S(2)}) collective-permute-start(bf16[2,96,1024]{2,1,0:T(8,128)(2,1)} %pad_maximum_fusion.10), channel_id=1, source_target_pairs={{0,8},{8,0},{16,24},{24,16},{1,9},{9,1},{17,25},{25,17},{2,10},{10... | collective-permute-start | bytes 1179656 | tf_op jit(solution)/shard_map/ppermute | solution.py:1250
  495.5 31.3 %collective-permute-start.50 = (bf16[192,1024]{1,0:T(8,128)(2,1)}, bf16[192,1024]{1,0:T(8,128)(2,1)S(1)}, u32[]{:S(2)}, u32[]{:S(2)}) collective-permute-start(bf16[192,1024]{1,0:T(8,128)(2,1)} %bitcast.343), channel_id=1, source_target_pairs={{0,4},{1,5},{2,6},{3,7},{4,0},{5,1},{6,2},{7,3},{8,12},{9,13},{10,... | collective-permute-start | bytes 1179656 | tf_op jit(solution)/shard_map/ppermute | solution.py:1245
  496.0 30.8 %collective-permute-start.51 = (bf16[192,1024]{1,0:T(8,128)(2,1)}, bf16[192,1024]{1,0:T(8,128)(2,1)S(1)}, u32[]{:S(2)}, u32[]{:S(2)}) collective-permute-start(bf16[192,1024]{1,0:T(8,128)(2,1)} %bitcast.342), channel_id=1, source_target_pairs={{0,2},{1,3},{2,0},{3,1},{4,6},{5,7},{6,4},{7,5},{8,10},{9,11},{10,... | collective-permute-start | bytes 1179656 | tf_op jit(solution)/shard_map/ppermute | solution.py:1245
  499.0 24.8 %collective-permute-start.53 = (bf16[128,1024]{1,0:T(8,128)(2,1)}, bf16[128,1024]{1,0:T(8,128)(2,1)}, u32[]{:S(2)}, u32[]{:S(2)}) collective-permute-start(bf16[128,1024]{1,0:T(8,128)(2,1)} %fusion.5), channel_id=1, source_target_pairs={{0,16},{8,24},{16,0},{24,8},{1,17},{9,25},{17,1},{25,9},{2,18},{10... | collective-permute-start | bytes 786440 | tf_op jit(solution)/shard_map/ppermute | solution.py:1250
  500.8 19.7 %collective-permute-start.52 = (bf16[96,1024]{1,0:T(8,128)(2,1)}, bf16[96,1024]{1,0:T(8,128)(2,1)}, u32[]{:S(2)}, u32[]{:S(2)}) collective-permute-start(bf16[96,1024]{1,0:T(8,128)(2,1)} %fusion.10), channel_id=1, source_target_pairs={{0,16},{8,24},{16,0},{24,8},{1,17},{9,25},{17,1},{25,9},{2,18},{10... | collective-permute-start | bytes 589832 | tf_op jit(solution)/shard_map/ppermute | solution.py:1250
  (109 other events, 776.8 us)
Sparse Core Ops, SparseCore 0:
  11.3 105.4 all-gather.5
  129.3 66.8 all-gather.3
  273.9 70.6 reduce-scatter.1
